TPU v7x, 32 devices: a whole 2x2x4 slice. The times are simulated.
32 devices in a mesh: section: 4 (over y, x), dp: 8 (over z, core).
Axes of the slice: x: 2, y: 2, z: 4, core: 2. Of those that a mesh axis runs over, the one named last changes fastest.
Arguments:
- tokens: bfloat16 [2, 4096, 768], P(None, 'dp'), may hold values from -6 to 6
- cotangent: bfloat16 [2, 4096, 768], P(None, 'dp'), may hold values from -6 to 6
- norm_gain: bfloat16 [4, 768], P('section'), may hold values from 0.25 to 1.75
- norm_shift: bfloat16 [4, 768], P('section'), may hold values from -1.796875 to 1.796875
- in_weight: bfloat16 [4, 768, 3072], P('section'), may hold values from -1 to 1
- out_bias: bfloat16 [4, 768], P('section'), may hold values from -1.796875 to 1.796875
- down_weight: bfloat16 [6144, 768], P('section'), may hold values from -0.109375 to 0.109375
- hidden_bias: bfloat16 [6144], P('section'), may hold values from -3 to 3
- frame_device: int32 [2, 8], replicated, may hold values from 0 to 7, each once within a row
- tube_device: int32 [2, 8], replicated, may hold values from 0 to 7, each once within a row
- clip_kind: int32 [2], replicated, may hold values from 0 to 1
Outputs:
- output: bfloat16 [2, 4096, 768], P(None, 'dp', 'section')
- input_grad: float32 [2, 4096, 768], P(None, 'dp', 'section')
- grad_norm_gain: float32 [4, 768], P('section')
- grad_norm_shift: float32 [4, 768], P('section')
- grad_in_weight: float32 [4, 768, 3072], P('section')
- grad_out_bias: float32 [4, 768], P('section')
- grad_down_weight: float32 [6144, 768], P('section')
- grad_hidden_bias: float32 [6144], P('section')
Inputs may be any that keep to these rules, and one draw needn't show every extreme that they name: `frame_device`: each row is a permutation. `tube_device`: each row is a permutation. `clip_kind`: 0 stands for 16x16 clips, 1 for 8x8 clips.
All inputs are finite; a program needn't handle non-finite values.
Results may differ from a plain program's by a relative error of at most 0.018.
Values may be sent and summed in bfloat16 or wider, within the bound.
A program may use at most 384 MiB of HBM per device.

v0:
```python
import jax
import jax.numpy as jnp
from jax import lax
from jax.sharding import PartitionSpec as P

HEADS = 12
HEAD_DIM = 64
WINDOW = 256


EPS = 1e-06
NEGATIVE = -1e30
ROOT_HALF = 0.7071067811865476
INV_ROOT_TWO_PI = 0.3989422804014327


def shortened(shard):

    def short(part):
        return part.astype(jnp.bfloat16) if part.dtype == jnp.float32 else part

    return jax.tree.map(short, shard)


def shifted(value, axis, steps):
    count = lax.axis_size(axis)
    leading, last = (max(0, -steps), min(count, count - steps))
    return lax.ppermute(value, axis, [(source, source + steps) for source in range(leading, last)])


def inner_rows(left_side, right_side):
    return lax.dot_general(
        left_side, right_side, (((0,), (0,)), ((), ())), preferred_element_type=jnp.float32
    )


def times_transposed(left_side, right_side):
    return lax.dot_general(
        left_side, right_side, (((1,), (1,)), ((), ())), preferred_element_type=jnp.float32
    )


def norm_forward(hidden, gain_row, shift_row):
    average = jnp.mean(hidden, axis=-1, keepdims=True)
    centred = hidden - average
    inverse = lax.rsqrt(jnp.mean(centred * centred, axis=-1, keepdims=True) + EPS)
    normal = centred * inverse
    return (normal * gain_row + shift_row, normal, inverse)


def norm_backward(grad_normed, normal, inverse, gain_row):
    weighted = grad_normed * gain_row
    first_mean = jnp.mean(weighted, axis=-1, keepdims=True)
    second_mean = jnp.mean(weighted * normal, axis=-1, keepdims=True)
    grad_hidden = inverse * (weighted - first_mean - normal * second_mean)
    return (grad_hidden, jnp.sum(grad_normed * normal, axis=0), jnp.sum(grad_normed, axis=0))


def window_allowed(clip_type):
    window_id = jnp.arange(WINDOW) % 16 // 4
    return jnp.logical_or(window_id[:, None] == window_id[None, :], clip_type == 0)


def split_heads(matrix):
    return matrix.reshape(matrix.shape[0] // WINDOW, WINDOW, HEADS, HEAD_DIM)


def attention_parts(normed_low, weight, allowed):
    model_width = normed_low.shape[1]
    projected = jnp.dot(
        normed_low, weight[:, : 3 * model_width], preferred_element_type=jnp.float32
    )
    queries = split_heads(projected[:, :model_width].astype(jnp.bfloat16))
    key_heads = split_heads(projected[:, model_width : 2 * model_width].astype(jnp.bfloat16))
    values = split_heads(projected[:, 2 * model_width :].astype(jnp.bfloat16))
    scores = jnp.einsum("sqhd,skhd->shqk", queries, key_heads, preferred_element_type=jnp.float32)
    scaled = jnp.where(allowed, scores * HEAD_DIM ** (-0.5), NEGATIVE)
    row_max = jnp.max(scaled, axis=-1, keepdims=True)
    exponent = jnp.exp(scaled - row_max)
    attend_probs = exponent / jnp.sum(exponent, axis=-1, keepdims=True)
    probs_low = attend_probs.astype(jnp.bfloat16)
    attended = jnp.einsum("shqk,skhd->sqhd", probs_low, values, preferred_element_type=jnp.float32)
    attended = attended.astype(jnp.bfloat16).reshape(normed_low.shape)
    return (queries, key_heads, values, attend_probs, probs_low, attended)


def attention_forward(entering, gain_row, shift_row, weight, bias_row, allowed):
    hidden = entering.astype(jnp.float32)
    model_width = hidden.shape[1]
    normed = norm_forward(hidden, gain_row, shift_row)[0]
    attended = attention_parts(normed.astype(jnp.bfloat16), weight, allowed)[5]
    branch_out = jnp.dot(attended, weight[:, 3 * model_width :], preferred_element_type=jnp.float32)
    return (hidden + branch_out + bias_row).astype(jnp.bfloat16)


def feed_forward(entering, gain_row, shift_row, weight, down_full, bias_full, bias_row):
    hidden = entering.astype(jnp.float32)
    normed = norm_forward(hidden, gain_row, shift_row)[0].astype(jnp.bfloat16)
    pre_gelu = jnp.dot(normed, weight, preferred_element_type=jnp.float32) + bias_full
    active_low = jax.nn.gelu(pre_gelu, approximate=False).astype(jnp.bfloat16)
    branch_out = jnp.dot(active_low, down_full, preferred_element_type=jnp.float32)
    return (hidden + branch_out + bias_row).astype(jnp.bfloat16)


def attention_backward(entering, grad_low, gain_row, shift_row, weight, allowed, hidden_width):
    hidden = entering.astype(jnp.float32)
    row_count, model_width = hidden.shape
    normed, normal, inverse = norm_forward(hidden, gain_row, shift_row)
    normed_low = normed.astype(jnp.bfloat16)
    queries, key_heads, values, attend_probs, probs_low, attended = attention_parts(
        normed_low, weight, allowed
    )
    grad_out_weight = inner_rows(attended, grad_low)
    grad_bias = jnp.sum(grad_low.astype(jnp.float32), axis=0)
    grad_attended = split_heads(
        times_transposed(grad_low, weight[:, 3 * model_width :]).astype(jnp.bfloat16)
    )
    grad_probs = jnp.einsum(
        "sqhd,skhd->shqk", grad_attended, values, preferred_element_type=jnp.float32
    )
    grad_values = jnp.einsum(
        "shqk,sqhd->skhd", probs_low, grad_attended, preferred_element_type=jnp.float32
    )
    row_dot = jnp.sum(attend_probs * grad_probs, axis=-1, keepdims=True)
    grad_scores = (attend_probs * (grad_probs - row_dot) * HEAD_DIM ** (-0.5)).astype(jnp.bfloat16)
    grad_queries = jnp.einsum(
        "shqk,skhd->sqhd", grad_scores, key_heads, preferred_element_type=jnp.float32
    )
    grad_keys = jnp.einsum(
        "shqk,sqhd->skhd", grad_scores, queries, preferred_element_type=jnp.float32
    )
    grad_projected = jnp.concatenate(
        [
            component.reshape(row_count, model_width).astype(jnp.bfloat16)
            for component in (grad_queries, grad_keys, grad_values)
        ],
        axis=1,
    )
    grad_in_projection = inner_rows(normed_low, grad_projected)
    grad_normed = times_transposed(grad_projected, weight[:, : 3 * model_width])
    grad_hidden, grad_gain, grad_shift = norm_backward(grad_normed, normal, inverse, gain_row)
    grad_weight = jnp.concatenate([grad_in_projection, grad_out_weight], axis=1)
    zero_down = jnp.zeros((hidden_width, model_width), jnp.float32)
    zero_bias = jnp.zeros((hidden_width,), jnp.float32)
    return (
        grad_low.astype(jnp.float32) + grad_hidden,
        (grad_weight, zero_down, zero_bias, grad_gain, grad_shift, grad_bias),
    )


def feed_backward(entering, grad_low, gain_row, shift_row, weight, down_full, bias_full):
    hidden = entering.astype(jnp.float32)
    normed, normal, inverse = norm_forward(hidden, gain_row, shift_row)
    normed_low = normed.astype(jnp.bfloat16)
    pre_gelu = jnp.dot(normed_low, weight, preferred_element_type=jnp.float32) + bias_full
    active_low = jax.nn.gelu(pre_gelu, approximate=False).astype(jnp.bfloat16)
    grad_down = inner_rows(active_low, grad_low)
    grad_bias = jnp.sum(grad_low.astype(jnp.float32), axis=0)
    grad_active = times_transposed(grad_low, down_full).astype(jnp.bfloat16)
    gelu_slope = (
        0.5 * (1.0 + lax.erf(pre_gelu * ROOT_HALF))
        + pre_gelu * jnp.exp(-0.5 * pre_gelu * pre_gelu) * INV_ROOT_TWO_PI
    )
    grad_pre = (grad_active.astype(jnp.float32) * gelu_slope).astype(jnp.bfloat16)
    grad_hidden_bias = jnp.sum(grad_pre.astype(jnp.float32), axis=0)
    grad_weight = inner_rows(normed_low, grad_pre)
    grad_normed = times_transposed(grad_pre, weight)
    grad_hidden, grad_gain, grad_shift = norm_backward(grad_normed, normal, inverse, gain_row)
    return (
        grad_low.astype(jnp.float32) + grad_hidden,
        (grad_weight, grad_down, grad_hidden_bias, grad_gain, grad_shift, grad_bias),
    )


def layout_sizes(slot_count):
    devices = lax.axis_size("dp")
    across = min(devices, 16)
    repeat = 16 // across
    per_group = slot_count // repeat
    return (devices, across, repeat, per_group)


def own_family(table, devices, across):
    here = lax.axis_index("dp")
    role = jnp.sum(jnp.where(table == here, jnp.arange(devices, dtype=jnp.int32), 0))
    return role // across


def to_tubes(local_rows, frame_row, tube_row):
    row_count, model_width = local_rows.shape
    devices, across, repeat, per_group = layout_sizes(row_count // WINDOW)
    pieces = local_rows.reshape(per_group, repeat, repeat, across, 16, model_width)
    by_target = pieces.transpose(3, 0, 1, 2, 4, 5).reshape(across, -1, model_width)
    sender_family = own_family(frame_row, devices, across)
    targets = lax.dynamic_slice_in_dim(tube_row, sender_family * across, across)
    outgoing = (
        jnp.zeros((devices, by_target.shape[1], model_width), local_rows.dtype)
        .at[targets]
        .set(by_target)
    )
    arrived = lax.all_to_all(
        shortened(outgoing), "dp", split_axis=0, concat_axis=0, tiled=True
    ).astype(outgoing.dtype)
    receiver_family = own_family(tube_row, devices, across)
    sources = lax.dynamic_slice_in_dim(frame_row, receiver_family * across, across)
    from_roles = arrived[sources].reshape(across, per_group, repeat, repeat, 16, model_width)
    return from_roles.transpose(1, 3, 0, 2, 4, 5).reshape(row_count, model_width)


def to_frames(local_rows, frame_row, tube_row):
    row_count, model_width = local_rows.shape
    devices, across, repeat, per_group = layout_sizes(row_count // WINDOW)
    pieces = local_rows.reshape(per_group, repeat, across, repeat, 16, model_width)
    by_target = pieces.transpose(2, 0, 3, 1, 4, 5).reshape(across, -1, model_width)
    sender_family = own_family(tube_row, devices, across)
    targets = lax.dynamic_slice_in_dim(frame_row, sender_family * across, across)
    outgoing = (
        jnp.zeros((devices, by_target.shape[1], model_width), local_rows.dtype)
        .at[targets]
        .set(by_target)
    )
    arrived = lax.all_to_all(outgoing, "dp", split_axis=0, concat_axis=0, tiled=True)
    receiver_family = own_family(frame_row, devices, across)
    sources = lax.dynamic_slice_in_dim(tube_row, receiver_family * across, across)
    from_roles = arrived[sources].reshape(across, per_group, repeat, repeat, 16, model_width)
    return from_roles.transpose(1, 2, 3, 0, 4, 5).reshape(row_count, model_width)


def on_device(
    tokens,
    cotangent,
    norm_gain,
    norm_shift,
    in_weight,
    out_bias,
    down_weight,
    hidden_bias,
    frame_device,
    tube_device,
    clip_kind,
):
    section_index = lax.axis_index("section")
    micro_count, row_count, model_width = tokens.shape
    gain_row = norm_gain[0].astype(jnp.float32)
    shift_row = norm_shift[0].astype(jnp.float32)
    weight = in_weight[0]
    bias_row = out_bias[0].astype(jnp.float32)
    earlier_down, earlier_bias = shifted((down_weight, hidden_bias), "section", 1)
    down_full = jnp.concatenate([earlier_down, down_weight], axis=0)
    bias_full = jnp.concatenate([earlier_bias, hidden_bias]).astype(jnp.float32)
    hidden_width = down_full.shape[0]
    odd_section = section_index % 2 == 1

    def attention_branch(entering, allowed):
        return attention_forward(entering, gain_row, shift_row, weight, bias_row, allowed)

    def feed_branch(entering, allowed):
        return feed_forward(entering, gain_row, shift_row, weight, down_full, bias_full, bias_row)

    def spare_branch(entering, allowed):
        return jnp.zeros_like(entering)

    saved = jnp.zeros_like(tokens)
    finished = jnp.zeros_like(tokens)
    incoming = jnp.zeros_like(tokens[0])
    for moment in range(micro_count + 3):
        micro_index = moment - section_index
        active = (micro_index >= 0) & (micro_index < micro_count)
        clamped = jnp.clip(micro_index, 0, micro_count - 1)
        entering = incoming
        if moment < micro_count:
            entering = jnp.where(section_index == 0, tokens[moment], incoming)
        saved = jnp.where(
            active, lax.dynamic_update_index_in_dim(saved, entering, clamped, 0), saved
        )
        allowed = window_allowed(clip_kind[clamped])
        selector = jnp.where(active, section_index % 2, 2)
        leaving = lax.switch(
            selector, [attention_branch, feed_branch, spare_branch], entering, allowed
        )
        finished = jnp.where(
            active & (section_index == 3),
            lax.dynamic_update_index_in_dim(finished, leaving, clamped, 0),
            finished,
        )
        if 1 <= moment <= micro_count:
            regrouped = to_tubes(leaving, frame_device[moment - 1], tube_device[moment - 1])
            leaving = jnp.where(section_index == 1, regrouped, leaving)
        if moment <= micro_count + 1:
            incoming = jax.tree.map(
                lambda part, own: part.astype(own.dtype),
                shifted(shortened(leaving), "section", 1),
                leaving,
            )
    zero_grads = (
        jnp.zeros((model_width, hidden_width), jnp.float32),
        jnp.zeros((hidden_width, model_width), jnp.float32),
        jnp.zeros((hidden_width,), jnp.float32),
        jnp.zeros((model_width,), jnp.float32),
        jnp.zeros((model_width,), jnp.float32),
        jnp.zeros((model_width,), jnp.float32),
    )

    def attention_back(kept_input, arriving, allowed):
        return attention_backward(
            kept_input, arriving, gain_row, shift_row, weight, allowed, hidden_width
        )

    def feed_back(kept_input, arriving, allowed):
        return feed_backward(
            kept_input, arriving, gain_row, shift_row, weight, down_full, bias_full
        )

    def spare_back(kept_input, arriving, allowed):
        return (jnp.zeros(kept_input.shape, jnp.float32), zero_grads)

    totals = zero_grads
    returned = jnp.zeros(tokens.shape, jnp.float32)
    upstream = jnp.zeros_like(tokens[0])
    for moment in range(micro_count + 3):
        micro_index = micro_count - 1 - moment + (3 - section_index)
        active = (micro_index >= 0) & (micro_index < micro_count)
        clamped = jnp.clip(micro_index, 0, micro_count - 1)
        arriving = upstream
        if moment < micro_count:
            arriving = jnp.where(section_index == 3, cotangent[micro_count - 1 - moment], upstream)
        kept_input = lax.dynamic_index_in_dim(saved, clamped, 0, keepdims=False)
        allowed = window_allowed(clip_kind[clamped])
        selector = jnp.where(active, section_index % 2, 2)
        grad_input, gradients = lax.switch(
            selector, [attention_back, feed_back, spare_back], kept_input, arriving, allowed
        )
        totals = jax.tree.map(jnp.add, totals, gradients)
        returned = jnp.where(
            active & (section_index == 0),
            lax.dynamic_update_index_in_dim(returned, grad_input, clamped, 0),
            returned,
        )
        sending = grad_input.astype(jnp.bfloat16)
        if 1 <= moment <= micro_count:
            regrouped = to_frames(
                sending, frame_device[micro_count - moment], tube_device[micro_count - moment]
            )
            sending = jnp.where(section_index == 2, regrouped, sending)
        if moment <= micro_count + 1:
            upstream = shifted(sending, "section", -1)
    output = lax.psum_scatter(
        finished.astype(jnp.float32).astype(jnp.bfloat16),
        "section",
        scatter_dimension=2,
        tiled=True,
    )
    input_grad = lax.psum_scatter(
        returned.astype(jnp.bfloat16), "section", scatter_dimension=2, tiled=True
    ).astype(jnp.float32)
    grad_weight, grad_down, grad_hidden, grad_gain, grad_shift, grad_bias = totals
    half_rows = hidden_width // 2
    summed = lax.psum((grad_weight, grad_down, grad_hidden, grad_gain, grad_shift, grad_bias), "dp")
    passed_down, passed_bias = (
        shifted(summed[1][:half_rows].astype(jnp.bfloat16), "section", -1).astype(jnp.float32),
        shifted(summed[2][:half_rows].astype(jnp.bfloat16), "section", -1).astype(jnp.float32),
    )
    own_down = jnp.where(odd_section, summed[1][half_rows:], passed_down)
    own_bias = jnp.where(odd_section, summed[2][half_rows:], passed_bias)
    return (
        output,
        input_grad,
        summed[3][None],
        summed[4][None],
        summed[0][None],
        summed[5][None],
        own_down,
        own_bias,
    )


def solution(mesh):
    return jax.shard_map(
        on_device,
        mesh=mesh,
        in_specs=(
            P(None, "dp", None),
            P(None, "dp", None),
            P("section", None),
            P("section", None),
            P("section", None, None),
            P("section", None),
            P("section", None),
            P("section"),
            P(),
            P(),
            P(),
        ),
        out_specs=(
            P(None, "dp", "section"),
            P(None, "dp", "section"),
            P("section", None),
            P("section", None),
            P("section", None, None),
            P("section", None),
            P("section", None),
            P("section"),
        ),
        check_vma=False,
    )
```

profile of v0, /device:TPU:0, one launch (start us, length us, event | category | flops | bytes accessed | tf_op | source)
XLA Modules:
  0.0 1422.6 jit_solution(16613874709038739594)
XLA Ops:
  7.2 6.3 collective-permute-start.1
  24.1 38.8 %collective-permute-done = bf16[1536]{0:T(1024)(128)(2,1)S(1)} collective-permute-done((bf16[1536]{0:T(1024)(128)(2,1)}, bf16[1536]{0:T(1024)(128)(2,1)S(1)}, u32[]{:S(2)}, u32[]{:S(2)}) %collective-permute-start) | collective-permute-done | bytes 3104 | tf_op jit(solution)/shard_map/ppermute | solution.py:28
  63.6 3.2 constant_dynamic-update-slice_fusion.16
  68.4 36.2 %conditional.10 = (bf16[512,768]{1,0:T(8,128)(2,1)}, bf16[1,512,768]{2,1,0:T(8,128)(2,1)S(1)}) conditional(s32[]{:T(128)} %clamp.20, (bf16[512,768]{1,0:T(8,128)(2,1)S(1)}, f32[768]{0:T(1024)S(1)}, f32[768]{0:T(1024)S(1)}, bf16[768,3072]{1,0:T(8,128)(2,1)}, pred[256,256]{0,1:T(8,128)(4,1)S(1)}, ...), branch_computations={%region_0.5_spmd, %region_5.8_spmd, %region_8.9_spmd} | conditional | flops 4941939200 | bytes 62270508 | solution.py:278
  68.9 4.2 convolution_convert_fusion
  106.6 15.8 %collective-permute-done.2 = bf16[512,768]{1,0:T(8,128)(2,1)S(1)} collective-permute-done((bf16[512,768]{1,0:T(8,128)(2,1)}, bf16[512,768]{1,0:T(8,128)(2,1)S(1)}, u32[]{:S(2)}, u32[]{:S(2)}) %collective-permute-start.2) | collective-permute-done | bytes 786464 | tf_op jit(solution)/shard_map/ppermute | solution.py:28
  125.9 24.6 %conditional.11 = (bf16[512,768]{1,0:T(8,128)(2,1)S(1)}) conditional(s32[]{:T(128)} %clamp.21, (bf16[512,768]{1,0:T(8,128)(2,1)S(1)}, f32[768]{0:T(1024)S(1)}, f32[768]{0:T(1024)S(1)}, bf16[768,3072]{1,0:T(8,128)(2,1)}, pred[256,256]{0,1:T(8,128)(4,1)S(1)}, /*index=5*/f32[768]{0:T(1024)S(1)}) %tuple.342, ...), branch_computations={%region_9.14_spmd, %region_14.17_spmd, %region_17.18_spmd} | conditional | flops 4941939200 | bytes 60697636 | solution.py:278
  126.4 4.2 convolution_convert_fusion.1
  154.3 4.9 all-to-all-start
  159.2 21.0 %all-to-all-done = bf16[8,64,768]{2,1,0:T(8,128)(2,1)S(1)} async-done(((bf16[8,64,768]{2,1,0:T(8,128)(2,1)}), bf16[8,64,768]{2,1,0:T(8,128)(2,1)S(1)}, u32[]{:S(2)}, u32[]{:S(2)}) %all-to-all-start) | async-done | bytes 786464 | tf_op jit(solution)/shard_map/all_to_all | solution.py:201
  181.0 9.6 collective-permute-start.3
  190.6 16.5 %collective-permute-done.3 = bf16[512,768]{1,0:T(8,128)(2,1)S(1)} collective-permute-done((bf16[512,768]{1,0:T(8,128)(2,1)S(1)}, bf16[512,768]{1,0:T(8,128)(2,1)S(1)}, u32[]{:S(2)}, u32[]{:S(2)}) %collective-permute-start.3) | collective-permute-done | bytes 786464 | tf_op jit(solution)/shard_map/ppermute | solution.py:28
  207.1 9.9 conditional.12
  220.9 3.5 all-to-all-start.1
  224.5 20.9 %all-to-all-done.1 = bf16[8,64,768]{2,1,0:T(8,128)(2,1)S(1)} async-done(((bf16[8,64,768]{2,1,0:T(8,128)(2,1)}), bf16[8,64,768]{2,1,0:T(8,128)(2,1)S(1)}, u32[]{:S(2)}, u32[]{:S(2)}) %all-to-all-start.1) | async-done | bytes 786464 | tf_op jit(solution)/shard_map/all_to_all | solution.py:201
  246.2 25.4 %collective-permute-start.4 = (bf16[512,768]{1,0:T(8,128)(2,1)S(1)}, bf16[512,768]{1,0:T(8,128)(2,1)S(1)}, u32[]{:S(2)}, u32[]{:S(2)}) collective-permute-start(bf16[512,768]{1,0:T(8,128)(2,1)S(1)} %bitcast_select_fusion.10), channel_id=1, source_target_pairs={{0,8},{8,16},{16,24},{1,9},{9,17},{17,25},{2,10},{10,18},{18,26},{... | collective-permute-start | bytes 2359304 | tf_op jit(solution)/shard_map/ppermute | solution.py:28
  271.6 16.5 %collective-permute-done.4 = bf16[512,768]{1,0:T(8,128)(2,1)S(1)} collective-permute-done((bf16[512,768]{1,0:T(8,128)(2,1)S(1)}, bf16[512,768]{1,0:T(8,128)(2,1)S(1)}, u32[]{:S(2)}, u32[]{:S(2)}) %collective-permute-start.4) | collective-permute-done | bytes 786464 | tf_op jit(solution)/shard_map/ppermute | solution.py:28
  288.1 9.4 conditional.13
  297.6 4.2 collective-permute-start.5
  303.5 14.2 collective-permute-done.5
  320.4 21.2 %conditional.15 = (bf16[512,768]{1,0:T(8,128)(2,1)S(1)}, f32[768,3072]{1,0:T(8,128)}, f32[3072,768]{1,0:T(8,128)S(1)}, f32[3072]{0:T(1024)S(1)}, f32[768]{0:T(10...) conditional(s32[]{:T(128)} %clamp.24, (bf16[512,768]{1,0:T(8,128)(2,1)S(1)}, ...), branch_computations={%region_48.59_spmd, %region_59.68_spmd, %region_68.69_spmd} | conditional | flops 12223115264 | bytes 238172544 | solution.py:330
  335.0 4.9 broadcast_in_dim.236
  343.0 49.1 %collective-permute-done.6 = bf16[512,768]{1,0:T(8,128)(2,1)S(1)} collective-permute-done((bf16[512,768]{1,0:T(8,128)(2,1)S(1)}, bf16[512,768]{1,0:T(8,128)(2,1)S(1)}, u32[]{:S(2)}, u32[]{:S(2)}) %collective-permute-start.6) | collective-permute-done | bytes 786464 | tf_op jit(solution)/shard_map/ppermute | solution.py:28
  393.5 19.4 %conditional.16 = (bf16[512,768]{1,0:T(8,128)(2,1)S(1)}, f32[768,3072]{1,0:T(8,128)}, f32[3072,768]{1,0:T(8,128)}, f32[3072]{0:T(1024)S(1)}, f32[768]{0:T(1024)}, /*index=5*/f32[768]{0:T(1024)}, f32[768]{0:T(1024)S(1)}) conditional(s32[]{:T(128)} %clamp.23, (bf16[512,768]{1,0:T(8,128)(2,1)S(1)}, ...), branch_computations={%region_69.80_spmd, %region_80.89_spmd, %region_89.90_spmd} | conditional | flops 12223115264 | bytes 231881056 | solution.py:330
  403.4 4.2 broadcast.1823
  407.6 4.8 broadcast_in_dim.239
  416.7 4.0 all-to-all-start.2
  420.7 20.9 %all-to-all-done.2 = bf16[8,64,768]{2,1,0:T(8,128)(2,1)S(1)} async-done(((bf16[8,64,768]{2,1,0:T(8,128)(2,1)}), bf16[8,64,768]{2,1,0:T(8,128)(2,1)S(1)}, u32[]{:S(2)}, u32[]{:S(2)}) %all-to-all-start.2) | async-done | bytes 786464 | tf_op jit(solution)/shard_map/all_to_all | solution.py:222
  443.8 20.7 %collective-permute-done.7 = bf16[512,768]{1,0:T(8,128)(2,1)S(1)} collective-permute-done((bf16[512,768]{1,0:T(8,128)(2,1)S(1)}, bf16[512,768]{1,0:T(8,128)(2,1)S(1)}, u32[]{:S(2)}, u32[]{:S(2)}) %collective-permute-start.7) | collective-permute-done | bytes 786464 | tf_op jit(solution)/shard_map/ppermute | solution.py:28
  464.4 18.4 %conditional.17 = (bf16[512,768]{1,0:T(8,128)(2,1)S(1)}, f32[768,3072]{1,0:T(8,128)}, f32[3072,768]{1,0:T(8,128)}, f32[3072]{0:T(1024)S(1)}, f32[768]{0:T(1024)S(1)}, /*index=5*/f32[768]{0:T(1024)S(1)}, f32[768]{0:T(1024)}) conditional(s32[]{:T(128)} %clamp.22, (bf16[512,768]{1,0:T(8,128)(2,1)S(1)}, ...), branch_computations={%region_91.102_spmd, %region_102.111_spmd, %region_111.112_spmd} | conditional | flops 12223115264 | bytes 231881056 | solution.py:330
  473.7 4.1 broadcast.1866
  477.8 4.8 broadcast_in_dim.242
  486.7 3.5 all-to-all-start.3
  490.3 20.8 %all-to-all-done.3 = bf16[8,64,768]{2,1,0:T(8,128)(2,1)S(1)} async-done(((bf16[8,64,768]{2,1,0:T(8,128)(2,1)}), bf16[8,64,768]{2,1,0:T(8,128)(2,1)S(1)}, u32[]{:S(2)}, u32[]{:S(2)}) %all-to-all-start.3) | async-done | bytes 786464 | tf_op jit(solution)/shard_map/all_to_all | solution.py:222
  515.3 151.8 %collective-permute-done.8 = bf16[512,768]{1,0:T(8,128)(2,1)S(1)} collective-permute-done((bf16[512,768]{1,0:T(8,128)(2,1)S(1)}, bf16[512,768]{1,0:T(8,128)(2,1)S(1)}, u32[]{:S(2)}, u32[]{:S(2)}) %collective-permute-start.8) | collective-permute-done | bytes 786464 | tf_op jit(solution)/shard_map/ppermute | solution.py:28
  667.2 91.6 %conditional.18 = (bf16[512,768]{1,0:T(8,128)(2,1)S(1)}, f32[768,3072]{1,0:T(8,128)}, f32[3072,768]{1,0:T(8,128)}, f32[3072]{0:T(1024)S(1)}, f32[768]{0:T(1024)S(1)}, /*index=5*/f32[768]{0:T(1024)S(1)}, f32[768]{0:T(1024)S(1)}) conditional(s32[]{:T(128)} %clamp.21, (bf16[512,768]{1,0:T(8,128)(2,1)S(1)}, ...), branch_computations={%region_113.124_spmd, %region_124.133_spmd, %region_133.134_spmd} | conditional | flops 12223115264 | bytes 228735296 | solution.py:330
  673.3 4.1 convolution_convert_fusion.14
  693.5 5.0 fusion.946
  705.3 11.4 fusion.935
  716.8 11.3 fusion.938
  728.1 3.7 fusion.929
  740.5 5.2 fusion.958
  745.7 8.7 pad_maximum_fusion.3
  754.4 4.3 broadcast.1872
  760.2 20.7 %collective-permute-done.9 = bf16[512,768]{1,0:T(8,128)(2,1)S(1)} collective-permute-done((bf16[512,768]{1,0:T(8,128)(2,1)S(1)}, bf16[512,768]{1,0:T(8,128)(2,1)S(1)}, u32[]{:S(2)}, u32[]{:S(2)}) %collective-permute-start.9) | collective-permute-done | bytes 786464 | tf_op jit(solution)/shard_map/ppermute | solution.py:28
  780.9 95.5 %conditional.19 = (f32[768,3072]{1,0:T(8,128)}, f32[3072,768]{1,0:T(8,128)}, f32[3072]{0:T(1024)S(1)}, f32[768]{0:T(1024)S(1)}, f32[768]{0:T(1024)S(1)}, /*index=5*/f32[768]{0:T(1024)S(1)}, bf16[1,512,768]{1,2,0:T(8,128)(2,1)}) conditional(s32[]{:T(128)} %clamp.20, (bf16[512,768]{1,0:T(8,128)(2,1)S(1)}, ...), branch_computations={%region_134.145_spmd, %region_145.154_spmd, %region_154.155_spmd} | conditional | flops 12223113216 | bytes 252328320 | solution.py:330
  787.5 4.1 convolution_convert_fusion.17
  803.3 5.1 fusion.1093
  815.0 11.4 fusion.1082
  826.4 11.3 fusion.1085
  837.7 3.5 fusion.1076
  853.3 6.9 fusion.1105
  860.1 8.1 pad_maximum_fusion.4
  868.2 4.3 broadcast.1915
  876.5 19.8 %add_add_fusion = f32[3072,768]{1,0:T(8,128)} fusion(f32[3072,768]{1,0:T(8,128)} %get-tuple-element.488, f32[3072,768]{1,0:T(8,128)} %get-tuple-element.487, f32[3072,768]{1,0:T(8,128)} %get-tuple-element.486, f32[3072,768]{1,0:T(8,128)} %copy-done.5, f32[3072,768]{1,0:T(8,128)} %get-tuple-element.485), kind=kLoop, calls=%fused_computation.1332 | loop fusion | flops 9437184 | bytes 56623104 | tf_op jit(solution)/shard_map/add | solution.py:333
  899.7 14.8 %add_bitcast_fusion = f32[1,768,3072]{2,1,0:T(8,128)} fusion(f32[768,3072]{1,0:T(8,128)} %get-tuple-element.478, f32[768,3072]{1,0:T(8,128)S(1)} %bitcast.457, f32[768,3072]{1,0:T(8,128)} %get-tuple-element.476, f32[768,3072]{1,0:T(8,128)S(1)} %bitcast.455, f32[768,3072]{1,0:T(8,128)} %get-tuple-element.475), kind=kLoop, calls=%fused_computation.1333 | loop fusion | flops 9437184 | bytes 56623104 | tf_op jit(solution)/shard_map/broadcast_in_dim | solution.py:370
  917.6 14.0 conditional.14
  931.9 3.0 copy.594
  947.1 338.5 %all-reduce.8.cloned.1.call-done = (f32[1,768,3072]{2,1,0:T(8,128)}, f32[3072,768]{1,0:T(8,128)}) async-done(((f32[1,768,3072]{2,1,0:T(8,128)}, f32[3072,768]{1,0:T(8,128)}), (f32[1,768,3072]{2,1,0:T(8,128)}, f32[3072,768]{1,0:T(8,128)})) %all-reduce.8.cloned.1.call-update) | async-done | bytes 18874384 | tf_op jit(solution)/shard_map/psum | solution.py:358
  1292.9 27.9 %all-reduce.1 = (f32[1,768]{1,0:T(1,128)}, f32[1,768]{1,0:T(1,128)}, f32[1,768]{1,0:T(1,128)}, f32[3072]{0:T(1024)S(1)}) all-reduce(f32[1,768]{1,0:T(1,128)S(1)} %broadcast_in_dim.307, f32[1,768]{1,0:T(1,128)S(1)} %broadcast_in_dim.308, f32[1,768]{1,0:T(1,128)S(1)} %broadcast_in_dim.319, ...), channel_id=1, replica_groups=mesh['section'=4,'dp'=8] {'dp'}, use_global_device_ids=true, to_apply=%region_156.157 | all-reduce | flops 5376 | bytes 43008 | tf_op jit(solution)/shard_map/psum | solution.py:358
  1322.1 46.5 %all-reduce.6.cloned.1.call-done = bf16[2,512,768]{1,0,2:T(2,128)(2,1)} async-done(((bf16[2,512,768]{1,0,2:T(2,128)(2,1)}), bf16[2,512,768]{1,0,2:T(2,128)(2,1)}) %all-reduce.6.cloned.1.call-update) | async-done | bytes 1572880
  1371.3 32.0 %reduce-scatter.2.cloned.1.call-done = bf16[2,512,192]{1,2,0:T(8,128)(2,1)} async-done(((bf16[2,512,768]{1,2,0:T(8,128)(2,1)}), bf16[2,512,192]{1,2,0:T(8,128)(2,1)}) %reduce-scatter.2.cloned.1.call-update) | async-done | bytes 393232 | tf_op jit(solution)/shard_map/reduce_scatter | solution.py:353
  1405.4 6.5 slice_select_fusion
  1411.8 3.7 copy.932
  (422 shorter events, 193.3 us)
Async XLA Ops:
  7.2 56.4 %collective-permute-start.1 = (bf16[1536,768]{1,0:T(8,128)(2,1)}, bf16[1536,768]{1,0:T(8,128)(2,1)}, u32[]{:S(2)}, u32[]{:S(2)}) collective-permute-start(bf16[1536,768]{1,0:T(8,128)(2,1)} %param.47), channel_id=1, source_target_pairs={{0,8},{8,16},{16,24},{1,9},{9,17},{17,25},{2,10},{10,18},{18,26},{... | collective-permute-start | bytes 7077896 | tf_op jit(solution)/shard_map/ppermute | solution.py:28
  13.4 49.4 %collective-permute-start = (bf16[1536]{0:T(1024)(128)(2,1)}, bf16[1536]{0:T(1024)(128)(2,1)S(1)}, u32[]{:S(2)}, u32[]{:S(2)}) collective-permute-start(bf16[1536]{0:T(1024)(128)(2,1)} %param.48), channel_id=1, source_target_pairs={{0,8},{8,16},{16,24},{1,9},{9,17},{17,25},{2,10},{10,18},{18,26},{... | collective-permute-start | bytes 9224 | tf_op jit(solution)/shard_map/ppermute | solution.py:28
  20.9 267.2 %copy-start.99 = (f32[768]{0:T(1024)}, f32[768]{0:T(1024)S(1)}, u32[]{:S(2)}) copy-start(f32[768]{0:T(1024)S(1)} %get-tuple-element.758) | copy-start | bytes 9220
  21.8 46.5 %copy-start.69 = (pred[256,256]{0,1:T(8,128)(4,1)}, pred[256,256]{0,1:T(8,128)(4,1)S(1)}, u32[]{:S(2)}) copy-start(pred[256,256]{0,1:T(8,128)(4,1)S(1)} %get-tuple-element.746) | copy-start | bytes 196612
  21.8 102.9 %copy-start.71 = (pred[256,256]{0,1:T(8,128)(4,1)}, pred[256,256]{0,1:T(8,128)(4,1)S(1)}, u32[]{:S(2)}) copy-start(pred[256,256]{0,1:T(8,128)(4,1)S(1)} %get-tuple-element.745) | copy-start | bytes 196612
  24.0 42.7 %copy-start.49 = (bf16[1536,768]{1,0:T(8,128)(2,1)S(1)}, bf16[1536,768]{1,0:T(8,128)(2,1)}, u32[]{:S(2)}) copy-start(bf16[1536,768]{1,0:T(8,128)(2,1)} %param.47) | copy-start | bytes 7077892
  68.3 37.6 %copy-start.113 = (s32[2,8]{1,0:T(2,128)S(1)}, s32[2,8]{1,0:T(2,128)}, u32[]{:S(2)}) copy-start(s32[2,8]{1,0:T(2,128)} %param.50) | copy-start | bytes 196
  68.4 37.6 %copy-start.114 = (s32[2,8]{1,0:T(2,128)S(1)}, s32[2,8]{1,0:T(2,128)}, u32[]{:S(2)}) copy-start(s32[2,8]{1,0:T(2,128)} %param.49) | copy-start | bytes 196
  104.6 17.8 %collective-permute-start.2 = (bf16[512,768]{1,0:T(8,128)(2,1)}, bf16[512,768]{1,0:T(8,128)(2,1)S(1)}, u32[]{:S(2)}, u32[]{:S(2)}) collective-permute-start(bf16[512,768]{1,0:T(8,128)(2,1)} %get-tuple-element.456), channel_id=1, source_target_pairs={{0,8},{8,16},{16,24},{1,9},{9,17},{17,25},{2,10},{10,18},{18,26},{... | collective-permute-start | bytes 2359304 | tf_op jit(solution)/shard_map/ppermute | solution.py:28
  106.6 45.1 %copy-start.91 = (s32[8]{0:T(128)}, s32[8]{0:T(128)S(1)}, u32[]{:S(2)}) copy-start(s32[8]{0:T(128)S(1)} %get-tuple-element.750) | copy-start | bytes 100
  106.6 52.6 %copy-start.93 = (s32[8]{0:T(128)}, s32[8]{0:T(128)S(1)}, u32[]{:S(2)}) copy-start(s32[8]{0:T(128)S(1)} %get-tuple-element.756) | copy-start | bytes 100
  150.5 30.4 %copy-start.19 = (bf16[512,768]{1,0:T(8,128)(2,1)}, bf16[512,768]{1,0:T(8,128)(2,1)S(1)}, u32[]{:S(2)}) copy-start(bf16[512,768]{1,0:T(8,128)(2,1)S(1)} %get-tuple-element.887) | copy-start | bytes 2359300
  150.5 56.7 %copy-start.73 = (pred[256,256]{0,1:T(8,128)(4,1)S(1)}, pred[256,256]{0,1:T(8,128)(4,1)}, u32[]{:S(2)}) copy-start(pred[256,256]{0,1:T(8,128)(4,1)} %get-tuple-element.744) | copy-start | bytes 196612
  154.3 25.9 %all-to-all-start = ((bf16[8,64,768]{2,1,0:T(8,128)(2,1)}), bf16[8,64,768]{2,1,0:T(8,128)(2,1)S(1)}, u32[]{:S(2)}, u32[]{:S(2)}) async-start(bf16[8,64,768]{2,1,0:T(8,128)(2,1)} %scatter_fusion), calls=%async_computation | async-start | bytes 1572864 | tf_op jit(solution)/shard_map/all_to_all | solution.py:201
  181.0 26.1 %collective-permute-start.3 = (bf16[512,768]{1,0:T(8,128)(2,1)S(1)}, bf16[512,768]{1,0:T(8,128)(2,1)S(1)}, u32[]{:S(2)}, u32[]{:S(2)}) collective-permute-start(bf16[512,768]{1,0:T(8,128)(2,1)S(1)} %bitcast_select_fusion.12), channel_id=1, source_target_pairs={{0,8},{8,16},{16,24},{1,9},{9,17},{17,25},{2,10},{10,18},{18,26},{... | collective-permute-start | bytes 2359304 | tf_op jit(solution)/shard_map/ppermute | solution.py:28
  217.0 29.0 %copy-start.21 = (bf16[512,768]{1,0:T(8,128)(2,1)}, bf16[512,768]{1,0:T(8,128)(2,1)S(1)}, u32[]{:S(2)}) copy-start(bf16[512,768]{1,0:T(8,128)(2,1)S(1)} %get-tuple-element.888) | copy-start | bytes 2359300
  217.1 71.1 %copy-start.75 = (pred[256,256]{0,1:T(8,128)(4,1)S(1)}, pred[256,256]{0,1:T(8,128)(4,1)}, u32[]{:S(2)}) copy-start(pred[256,256]{0,1:T(8,128)(4,1)} %get-tuple-element.743) | copy-start | bytes 196612
  220.9 24.4 %all-to-all-start.1 = ((bf16[8,64,768]{2,1,0:T(8,128)(2,1)}), bf16[8,64,768]{2,1,0:T(8,128)(2,1)S(1)}, u32[]{:S(2)}, u32[]{:S(2)}) async-start(bf16[8,64,768]{2,1,0:T(8,128)(2,1)} %scatter_fusion.1), calls=%async_computation.1 | async-start | bytes 1572864 | tf_op jit(solution)/shard_map/all_to_all | solution.py:201
  246.2 42.0 %collective-permute-start.4 = (bf16[512,768]{1,0:T(8,128)(2,1)S(1)}, bf16[512,768]{1,0:T(8,128)(2,1)S(1)}, u32[]{:S(2)}, u32[]{:S(2)}) collective-permute-start(bf16[512,768]{1,0:T(8,128)(2,1)S(1)} %bitcast_select_fusion.10), channel_id=1, source_target_pairs={{0,8},{8,16},{16,24},{1,9},{9,17},{17,25},{2,10},{10,18},{18,26},{... | collective-permute-start | bytes 2359304 | tf_op jit(solution)/shard_map/ppermute | solution.py:28
  297.6 20.2 %collective-permute-start.5 = (bf16[512,768]{1,0:T(8,128)(2,1)}, bf16[512,768]{1,0:T(8,128)(2,1)S(1)}, u32[]{:S(2)}, u32[]{:S(2)}) collective-permute-start(bf16[512,768]{1,0:T(8,128)(2,1)} %get-tuple-element.458), channel_id=1, source_target_pairs={{0,8},{8,16},{16,24},{1,9},{9,17},{17,25},{2,10},{10,18},{18,26},{... | collective-permute-start | bytes 2359304 | tf_op jit(solution)/shard_map/ppermute | solution.py:28
  320.4 73.0 %copy-start.76 = (pred[256,256]{0,1:T(8,128)(4,1)S(1)}, pred[256,256]{0,1:T(8,128)(4,1)}, u32[]{:S(2)}) copy-start(pred[256,256]{0,1:T(8,128)(4,1)} %get-tuple-element.743) | copy-start | bytes 196612
  341.7 51.7 %copy-start.5 = (f32[3072,768]{1,0:T(8,128)}, f32[3072,768]{1,0:T(8,128)S(1)}, u32[]{:S(2)}) copy-start(f32[3072,768]{1,0:T(8,128)S(1)} %get-tuple-element.484) | copy-start | bytes 28311556
  341.7 51.7 %copy-start.101 = (f32[768]{0:T(1024)}, f32[768]{0:T(1024)S(1)}, u32[]{:S(2)}) copy-start(f32[768]{0:T(1024)S(1)} %get-tuple-element.464) | copy-start | bytes 9220
  341.7 51.7 %copy-start.103 = (f32[768]{0:T(1024)}, f32[768]{0:T(1024)S(1)}, u32[]{:S(2)}) copy-start(f32[768]{0:T(1024)S(1)} %get-tuple-element.469) | copy-start | bytes 9220
  341.7 51.7 %copy-start.22 = (bf16[512,768]{1,0:T(8,128)(2,1)}, bf16[512,768]{1,0:T(8,128)(2,1)S(1)}, u32[]{:S(2)}) copy-start(bf16[512,768]{1,0:T(8,128)(2,1)S(1)} %get-tuple-element.459) | copy-start | bytes 2359300
  341.7 51.7 %copy-start.77 = (f32[3072]{0:T(1024)}, f32[3072]{0:T(1024)S(1)}, u32[]{:S(2)}) copy-start(f32[3072]{0:T(1024)S(1)} %get-tuple-element.489) | copy-start | bytes 36868
  341.7 51.7 %copy-start.85 = (f32[768]{0:T(1024)}, f32[768]{0:T(1024)S(1)}, u32[]{:S(2)}) copy-start(f32[768]{0:T(1024)S(1)} %get-tuple-element.479) | copy-start | bytes 9220
  341.7 50.4 %collective-permute-start.6 = (bf16[512,768]{1,0:T(8,128)(2,1)S(1)}, bf16[512,768]{1,0:T(8,128)(2,1)S(1)}, u32[]{:S(2)}, u32[]{:S(2)}) collective-permute-start(bf16[512,768]{1,0:T(8,128)(2,1)S(1)} %get-tuple-element.459), channel_id=1, source_target_pairs={{8,0},{16,8},{24,16},{9,1},{17,9},{25,17},{10,2},{18,10},{26,18},{... | collective-permute-start | bytes 2359304 | tf_op jit(solution)/shard_map/ppermute | solution.py:28
  412.9 51.6 %copy-start.13 = (bf16[512,768]{1,0:T(8,128)(2,1)}, bf16[512,768]{1,0:T(8,128)(2,1)S(1)}, u32[]{:S(2)}) copy-start(bf16[512,768]{1,0:T(8,128)(2,1)S(1)} %get-tuple-element.460) | copy-start | bytes 2359300
  412.9 51.6 %copy-start.87 = (f32[768]{0:T(1024)}, f32[768]{0:T(1024)S(1)}, u32[]{:S(2)}) copy-start(f32[768]{0:T(1024)S(1)} %get-tuple-element.480) | copy-start | bytes 9220
  412.9 51.5 %copy-start.2 = (bf16[512,768]{1,0:T(8,128)(2,1)S(1)}, bf16[512,768]{1,0:T(8,128)(2,1)}, u32[]{:S(2)}) copy-start(bf16[512,768]{1,0:T(8,128)(2,1)} %get-tuple-element.737) | copy-start | bytes 2359300
  412.9 51.5 %copy-start.74 = (pred[256,256]{0,1:T(8,128)(4,1)S(1)}, pred[256,256]{0,1:T(8,128)(4,1)}, u32[]{:S(2)}) copy-start(pred[256,256]{0,1:T(8,128)(4,1)} %get-tuple-element.744) | copy-start | bytes 196612
  416.7 24.9 %all-to-all-start.2 = ((bf16[8,64,768]{2,1,0:T(8,128)(2,1)}), bf16[8,64,768]{2,1,0:T(8,128)(2,1)S(1)}, u32[]{:S(2)}, u32[]{:S(2)}) async-start(bf16[8,64,768]{2,1,0:T(8,128)(2,1)} %scatter_fusion.2), calls=%async_computation.2 | async-start | bytes 1572864 | tf_op jit(solution)/shard_map/all_to_all | solution.py:222
  442.5 22.0 %collective-permute-start.7 = (bf16[512,768]{1,0:T(8,128)(2,1)S(1)}, bf16[512,768]{1,0:T(8,128)(2,1)S(1)}, u32[]{:S(2)}, u32[]{:S(2)}) collective-permute-start(bf16[512,768]{1,0:T(8,128)(2,1)S(1)} %bitcast_select_fusion.4), channel_id=1, source_target_pairs={{8,0},{16,8},{24,16},{9,1},{17,9},{25,17},{10,2},{18,10},{26,18},{... | collective-permute-start | bytes 2359304 | tf_op jit(solution)/shard_map/ppermute | solution.py:28
  482.8 29.9 %copy-start.81 = (f32[3072]{0:T(1024)}, f32[3072]{0:T(1024)S(1)}, u32[]{:S(2)}) copy-start(f32[3072]{0:T(1024)S(1)} %get-tuple-element.491) | copy-start | bytes 36868
  482.8 31.1 %copy-start.15 = (bf16[512,768]{1,0:T(8,128)(2,1)}, bf16[512,768]{1,0:T(8,128)(2,1)S(1)}, u32[]{:S(2)}) copy-start(bf16[512,768]{1,0:T(8,128)(2,1)S(1)} %get-tuple-element.461) | copy-start | bytes 2359300
  482.8 184.4 %copy-start.105 = (f32[768]{0:T(1024)}, f32[768]{0:T(1024)S(1)}, u32[]{:S(2)}) copy-start(f32[768]{0:T(1024)S(1)} %get-tuple-element.466) | copy-start | bytes 9220
  482.8 184.4 %copy-start.107 = (f32[768]{0:T(1024)}, f32[768]{0:T(1024)S(1)}, u32[]{:S(2)}) copy-start(f32[768]{0:T(1024)S(1)} %get-tuple-element.471) | copy-start | bytes 9220
  482.8 184.3 %copy-start.1 = (bf16[512,768]{1,0:T(8,128)(2,1)S(1)}, bf16[512,768]{1,0:T(8,128)(2,1)}, u32[]{:S(2)}) copy-start(bf16[512,768]{1,0:T(8,128)(2,1)} %get-tuple-element.736) | copy-start | bytes 2359300
  482.9 184.3 %copy-start.72 = (pred[256,256]{0,1:T(8,128)(4,1)S(1)}, pred[256,256]{0,1:T(8,128)(4,1)}, u32[]{:S(2)}) copy-start(pred[256,256]{0,1:T(8,128)(4,1)} %copy-done.71) | copy-start | bytes 196612
  486.7 24.4 %all-to-all-start.3 = ((bf16[8,64,768]{2,1,0:T(8,128)(2,1)}), bf16[8,64,768]{2,1,0:T(8,128)(2,1)S(1)}, u32[]{:S(2)}, u32[]{:S(2)}) async-start(bf16[8,64,768]{2,1,0:T(8,128)(2,1)} %scatter_fusion.3), calls=%async_computation.3 | async-start | bytes 1572864 | tf_op jit(solution)/shard_map/all_to_all | solution.py:222
  490.3 795.3 %all-reduce.8.cloned.1.call-start = ((), (), s32[]{:S(2)}) async-start(), calls=%async_computation.7 | async-start | bytes 37748736 | tf_op jit(solution)/shard_map/psum | solution.py:358
  514.0 153.1 %collective-permute-start.8 = (bf16[512,768]{1,0:T(8,128)(2,1)S(1)}, bf16[512,768]{1,0:T(8,128)(2,1)S(1)}, u32[]{:S(2)}, u32[]{:S(2)}) collective-permute-start(bf16[512,768]{1,0:T(8,128)(2,1)S(1)} %bitcast_select_fusion.3), channel_id=1, source_target_pairs={{8,0},{16,8},{24,16},{9,1},{17,9},{25,17},{10,2},{18,10},{26,18},{... | collective-permute-start | bytes 2359304 | tf_op jit(solution)/shard_map/ppermute | solution.py:28
  667.2 113.6 %copy-start = (bf16[512,768]{1,0:T(8,128)(2,1)S(1)}, bf16[512,768]{1,0:T(8,128)(2,1)}, u32[]{:S(2)}) copy-start(bf16[512,768]{1,0:T(8,128)(2,1)} %get-tuple-element.735) | copy-start | bytes 2359300
  667.2 113.6 %copy-start.70 = (pred[256,256]{0,1:T(8,128)(4,1)S(1)}, pred[256,256]{0,1:T(8,128)(4,1)}, u32[]{:S(2)}) copy-start(pred[256,256]{0,1:T(8,128)(4,1)} %copy-done.69) | copy-start | bytes 196612
  758.9 22.0 %collective-permute-start.9 = (bf16[512,768]{1,0:T(8,128)(2,1)S(1)}, bf16[512,768]{1,0:T(8,128)(2,1)S(1)}, u32[]{:S(2)}, u32[]{:S(2)}) collective-permute-start(bf16[512,768]{1,0:T(8,128)(2,1)S(1)} %get-tuple-element.462), channel_id=1, source_target_pairs={{8,0},{16,8},{24,16},{9,1},{17,9},{25,17},{10,2},{18,10},{26,18},{... | collective-permute-start | bytes 2359304 | tf_op jit(solution)/shard_map/ppermute | solution.py:28
  914.6 454.0 %all-reduce.6.cloned.1.call-start = ((), (), s32[]{:S(2)}) async-start(), calls=%async_computation.6 | async-start | bytes 3145728
  934.9 468.3 %reduce-scatter.2.cloned.1.call-start = ((), (), s32[]{:S(2)}) async-start(), calls=%async_computation.5 | async-start | bytes 1966080 | tf_op jit(solution)/shard_map/reduce_scatter | solution.py:353
  942.9 346.6 %copy-start.115 = (u32[32]{0:T(128)S(1)}, u32[32]{0:T(128)}, u32[]{:S(2)}) copy-start(u32[32]{0:T(128)} %constant.1138) | copy-start | bytes 388
  942.9 347.8 %copy-start.86 = (f32[768]{0:T(1024)S(1)}, f32[768]{0:T(1024)}, u32[]{:S(2)}) copy-start(f32[768]{0:T(1024)} %copy-done.85) | copy-start | bytes 9220
  942.9 347.8 %copy-start.88 = (f32[768]{0:T(1024)S(1)}, f32[768]{0:T(1024)}, u32[]{:S(2)}) copy-start(f32[768]{0:T(1024)} %copy-done.87) | copy-start | bytes 9220
  942.9 347.8 %copy-start.90 = (f32[768]{0:T(1024)S(1)}, f32[768]{0:T(1024)}, u32[]{:S(2)}) copy-start(f32[768]{0:T(1024)} %copy-done.89) | copy-start | bytes 9220
  942.9 348.5 %copy-start.104 = (f32[768]{0:T(1024)S(1)}, f32[768]{0:T(1024)}, u32[]{:S(2)}) copy-start(f32[768]{0:T(1024)} %copy-done.103) | copy-start | bytes 9220
  942.9 348.5 %copy-start.108 = (f32[768]{0:T(1024)S(1)}, f32[768]{0:T(1024)}, u32[]{:S(2)}) copy-start(f32[768]{0:T(1024)} %copy-done.107) | copy-start | bytes 9220
  942.9 348.5 %copy-start.112 = (f32[768]{0:T(1024)S(1)}, f32[768]{0:T(1024)}, u32[]{:S(2)}) copy-start(f32[768]{0:T(1024)} %copy-done.111) | copy-start | bytes 9220
  942.9 349.2 %copy-start.102 = (f32[768]{0:T(1024)S(1)}, f32[768]{0:T(1024)}, u32[]{:S(2)}) copy-start(f32[768]{0:T(1024)} %copy-done.101) | copy-start | bytes 9220
  943.0 349.2 %copy-start.106 = (f32[768]{0:T(1024)S(1)}, f32[768]{0:T(1024)}, u32[]{:S(2)}) copy-start(f32[768]{0:T(1024)} %copy-done.105) | copy-start | bytes 9220
  943.0 349.2 %copy-start.110 = (f32[768]{0:T(1024)S(1)}, f32[768]{0:T(1024)}, u32[]{:S(2)}) copy-start(f32[768]{0:T(1024)} %copy-done.109) | copy-start | bytes 9220
  943.0 349.9 %copy-start.78 = (f32[3072]{0:T(1024)S(1)}, f32[3072]{0:T(1024)}, u32[]{:S(2)}) copy-start(f32[3072]{0:T(1024)} %copy-done.77) | copy-start | bytes 36868
  943.0 349.9 %copy-start.80 = (f32[3072]{0:T(1024)S(1)}, f32[3072]{0:T(1024)}, u32[]{:S(2)}) copy-start(f32[3072]{0:T(1024)} %copy-done.79) | copy-start | bytes 36868
  943.0 349.9 %copy-start.82 = (f32[3072]{0:T(1024)S(1)}, f32[3072]{0:T(1024)}, u32[]{:S(2)}) copy-start(f32[3072]{0:T(1024)} %copy-done.81) | copy-start | bytes 36868
  943.0 349.9 %copy-start.84 = (f32[3072]{0:T(1024)S(1)}, f32[3072]{0:T(1024)}, u32[]{:S(2)}) copy-start(f32[3072]{0:T(1024)} %copy-done.83) | copy-start | bytes 36868
  1288.2 117.2 %collective-permute-start.10 = (bf16[1536,768]{1,0:T(8,128)(2,1)S(1)}, bf16[1536,768]{1,0:T(8,128)(2,1)}, u32[]{:S(2)}, u32[]{:S(2)}) collective-permute-start(bf16[1536,768]{1,0:T(8,128)(2,1)S(1)} %slice.347), channel_id=1, source_target_pairs={{8,0},{16,8},{24,16},{9,1},{17,9},{25,17},{10,2},{18,10},{26,18},{... | collective-permute-start | bytes 7077896 | tf_op jit(solution)/shard_map/ppermute | solution.py:28
  1320.8 49.8 %collective-permute-start.11 = (bf16[1536]{0:T(1024)(128)(2,1)S(1)}, bf16[1536]{0:T(1024)(128)(2,1)S(1)}, u32[]{:S(2)}, u32[]{:S(2)}) collective-permute-start(bf16[1536]{0:T(1024)(128)(2,1)S(1)} %slice.348), channel_id=1, source_target_pairs={{8,0},{16,8},{24,16},{9,1},{17,9},{25,17},{10,2},{18,10},{26,18},{... | collective-permute-start | bytes 9224 | tf_op jit(solution)/shard_map/ppermute | solution.py:28
  (56 other events, 514.1 us)
Sparse Core Ops, SparseCore 0:
  914.7 370.8 all-reduce.7
  1289.3 79.2 all-reduce.5
  1371.9 31.3 reduce-scatter.1
where the time goes:
time: 1430 us; the launch traced here: 1420 us
  waiting for transfers between devices  845 us (59%)
  local copies, waits for them, and re-layouts  160 us (11%)
  matrix products  121 us (8%)
  other arithmetic  92.3 us (6%)
  loops' own time  84.9 us (6%)
  starting transfers between devices  72.6 us (5%)
  blocking collectives  27.9 us (2%)
  between operations  19.7 us (1%)
    ppermute x12, waiting for transfers between devices, shifted(): lax.ppermute(value, axis, [(source, source + steps) for source in range(l...  344 us
    psum x1, waiting for transfers between devices, on_device(): lax.psum((grad_weight, grad_down, grad_hidden, grad_gain, grad_shift, gra...  339 us
    ppermute x12, starting transfers between devices, shifted(): lax.ppermute(value, axis, [(source, source + steps) for source in range(l...  56.5 us
    unnamed x4, waiting for transfers between devices  46.5 us
    another operation x5, loops' own time, on_device(): lax.switch(selector, [attention_branch, feed_branch, spare_branch], enter...  46.4 us
    all_to_all x2, waiting for transfers between devices, to_tubes(): lax.all_to_all(shortened(outgoing), 'dp', split_axis=0, concat_axis=0, ti...  41.8 us
    all_to_all x2, waiting for transfers between devices, to_frames(): lax.all_to_all(outgoing, 'dp', split_axis=0, concat_axis=0, tiled=True)  41.8 us
    another operation x5, loops' own time, on_device(): lax.switch(selector, [attention_back, feed_back, spare_back], kept_input,...  38.4 us
  transfers between devices with their start and end apart: 19, of which 16 were waited for; matrix products, arithmetic and copies ran while one was open for 2% of the time, Pallas kernels for 0%

commit v1 on v0

v1 whole, which is shorter than its diff:
```python
import functools

import jax
import jax.numpy as jnp
from jax import lax
from jax.experimental import pallas as pl
from jax.experimental.pallas import tpu as pltpu
from jax.sharding import PartitionSpec as P

HEAD_DIM = 64
WINDOW = 256
BLOCK = 16
SECTIONS = 4
EPS = 1e-06
NEGATIVE = -1e30
MESH = pl.DeviceIdType.MESH
F32 = jnp.float32
BF16 = jnp.bfloat16


def mm(left, right):
    return lax.dot_general(left, right, (((1,), (0,)), ((), ())), preferred_element_type=F32)


def mm_nt(left, right):
    return lax.dot_general(left, right, (((1,), (1,)), ((), ())), preferred_element_type=F32)


def mm_tn(left, right):
    return lax.dot_general(left, right, (((0,), (0,)), ((), ())), preferred_element_type=F32)


def remote(src, dst, send_sem, recv_sem, section, dp):
    return pltpu.make_async_remote_copy(
        src_ref=src,
        dst_ref=dst,
        send_sem=send_sem,
        recv_sem=recv_sem,
        device_id=(section, dp),
        device_id_type=MESH,
    )


def normalise(hidden):
    average = jnp.mean(hidden, axis=-1, keepdims=True)
    centred = hidden - average
    inverse = lax.rsqrt(jnp.mean(centred * centred, axis=-1, keepdims=True) + EPS)
    return centred * inverse, inverse


def gelu_and_slope(u):
    size = jnp.abs(u)
    bell = jnp.exp(-0.5 * u * u)
    t = 1.0 / (1.0 + (0.3275911 * 0.7071067811865476) * size)
    poly = t * (
        0.127414796
        + t * (-0.142248368 + t * (0.7107068705 + t * (-0.7265760135 + t * 0.5307027145)))
    )
    tail = poly * bell
    cdf = jnp.where(u >= 0, 1.0 - tail, tail)
    return u * cdf, cdf + u * bell * 0.3989422804014327


def main_kernel(
    cfg,
    tok_hbm,
    cot_hbm,
    gain_ref,
    shift_ref,
    w_hbm,
    bias_ref,
    down_hbm,
    hb_ref,
    ftab,
    ttab,
    kind,
    out_ref,
    gcol_ref,
    grad_hbm,
    small_ref,
    weight,
    down,
    grads,
    keep_a,
    keep_b,
    hin,
    gin,
    leave,
    nrm,
    work,
    xsend,
    xrecv0,
    xrecv1,
    blocks,
    bias_early,
    bias_late,
    mask_add,
    load_sem,
    w_send,
    w_recv,
    h_send,
    h_recv,
    g_send,
    g_recv,
    x_send,
    x_recv,
    o_send,
    o_recv,
):
    n, across, repeat, slots, chunks, width, wide, depth = cfg
    section = lax.axis_index("section")
    me = lax.axis_index("dp")
    core = lax.rem(me, 2)
    sibling = me + 1 - 2 * core
    is_attn = lax.rem(section, 2) == 0
    xrecv = (xrecv0, xrecv1)
    half = wide // 2
    part = half // 2
    quarter = width // SECTIONS

    load_w = pltpu.make_async_copy(w_hbm, weight, load_sem.at[0])
    load_d = pltpu.make_async_copy(down_hbm, down.at[pl.ds(half, half)], load_sem.at[1])
    load_t = pltpu.make_async_copy(tok_hbm, hin, load_sem.at[2])
    load_c = pltpu.make_async_copy(cot_hbm, gin, load_sem.at[3])

    @pl.when(section == 0)
    def _():
        load_t.start()

    load_w.start()

    @pl.when(section == 3)
    def _():
        load_c.start()

    @pl.when(jnp.logical_not(is_attn))
    def _():
        load_d.start()

    barrier = pltpu.get_barrier_semaphore()

    def greet(s, d):
        pl.semaphore_signal(barrier, inc=1, device_id=(s, d), device_id_type=MESH)

    @pl.when(section == 0)
    def _():
        greet(1, me)
        greet(3, me)
        pl.semaphore_wait(barrier, 2)

    @pl.when(section == 1)
    def _():
        greet(0, me)
        greet(1, sibling)
        greet(3, me)

        @pl.loop(0, n)
        def _(d):
            greet(2, d)

        pl.semaphore_wait(barrier, 3 + n)

    @pl.when(section == 2)
    def _():
        greet(3, me)

        @pl.loop(0, n)
        def _(d):
            greet(1, d)

        pl.semaphore_wait(barrier, 1 + n)

    @pl.when(section == 3)
    def _():
        greet(0, me)
        greet(1, me)
        greet(2, me)
        greet(3, sibling)
        pl.semaphore_wait(barrier, 4)

    bias_late[...] = hb_ref[...].astype(F32)
    own_part = pl.ds(core * part, part)
    other_part = pl.ds((1 - core) * part, part)
    send_down = remote(
        down_hbm.at[own_part], down.at[own_part], w_send.at[0], w_recv.at[0], section + 1, me
    )
    send_bias = remote(
        bias_late, bias_early, w_send.at[1], w_recv.at[1], section + 1, me
    )
    pass_down = remote(
        down.at[own_part], down.at[own_part], w_send.at[0], w_recv.at[2], section, sibling
    )

    gain = gain_ref[...].astype(F32)
    shift = shift_ref[...].astype(F32)
    bias = bias_ref[...].astype(F32)
    small_ref[...] = jnp.zeros_like(small_ref)

    def clear_grads(count):
        @pl.loop(0, count)
        def _(j):
            grads[j] = jnp.zeros((width, width), F32)

    def role_of(table, micro, device):
        def step(r, found):
            return found + jnp.where(table[micro, r] == device, r, 0)

        return lax.fori_loop(0, n, step, 0)

    def send_blocks(c, rows, table, to_section, forward):
        blocks[...] = rows.reshape(blocks.shape)
        micro = lax.div(c, slots)
        slot = lax.rem(c, depth)

        @pl.when(c >= depth)
        def _():
            remote(
                xsend.at[slot], xsend.at[slot], x_send.at[c - depth], x_recv.at[0], to_section, me
            ).wait_send()

        @pl.loop(0, n)
        def _(d):
            spot = lax.rem(role_of(table, micro, d), across)
            for g in range(repeat):
                block = g * across + spot if forward else spot * repeat + g
                xsend[slot, d, g] = blocks[block]

        for m in range(2):

            @pl.when(micro == m)
            def _():
                @pl.loop(0, n)
                def _(d):
                    remote(
                        xsend.at[slot, d],
                        xrecv[m].at[lax.rem(c, slots), me],
                        x_send.at[c],
                        x_recv.at[m],
                        to_section,
                        d,
                    ).start()

    def gather_blocks(c, own_table, their_table, target, from_section, forward):
        for m in range(2):

            @pl.when(c == m * slots)
            def _():
                remote(xrecv[m], xrecv[m], x_send.at[0], x_recv.at[m], from_section, me).wait_recv()
                family = lax.rem(lax.div(role_of(own_table, m, me), across), n // across)

                @pl.loop(0, slots)
                def _(s):
                    group, inner = lax.div(s, repeat), lax.rem(s, repeat)

                    @pl.loop(0, across)
                    def _(r):
                        source = their_table[m, family * across + r]
                        for f in range(repeat):
                            block = r * repeat + f if forward else f * across + r
                            rows = pl.ds(pl.multiple_of(block * BLOCK, BLOCK), BLOCK)
                            target[m * slots + s, rows] = xrecv[m][
                                group * repeat + f, source, inner
                            ]

    def norm_back(c, dn, gb):
        nh, inverse = normalise(hin[c].astype(F32))
        weighted = dn * gain
        first = jnp.mean(weighted, axis=-1, keepdims=True)
        second = jnp.mean(weighted * nh, axis=-1, keepdims=True)
        grad = gb.astype(F32) + inverse * (weighted - first - nh * second)
        small_ref[0:1] += jnp.sum(dn * nh, axis=0, keepdims=True)
        small_ref[1:2] += jnp.sum(dn, axis=0, keepdims=True)
        small_ref[2:3] += jnp.sum(gb.astype(F32), axis=0, keepdims=True)
        return grad

    @pl.when(is_attn)
    def _():
        send_down.start()
        send_bias.start()
        load_w.wait()

        @pl.when(section == 0)
        def _():
            load_t.wait()

        lane = lax.broadcasted_iota(jnp.int32, (1, 2 * HEAD_DIM), 1)
        first_head = jnp.where(lane < HEAD_DIM, 1.0, 0.0)
        pick = [first_head.astype(BF16), (1.0 - first_head).astype(BF16)]
        scale = HEAD_DIM ** (-0.5)
        pick_scaled = [
            (first_head * scale).astype(BF16),
            ((1.0 - first_head) * scale).astype(BF16),
        ]
        key_window = lax.broadcasted_iota(jnp.int32, (WINDOW, WINDOW), 0) % 16 // 4
        query_window = lax.broadcasted_iota(jnp.int32, (WINDOW, WINDOW), 1) % 16 // 4
        barred = jnp.where(key_window == query_window, 0.0, NEGATIVE)
        for m in range(2):
            mask_add[m] = barred * kind[m].astype(F32)

        def forward(c):
            @pl.when(section == 2)
            def _():
                gather_blocks(c, ttab, ftab, hin, 1, True)

            micro = lax.div(c, slots)
            hidden = hin[c].astype(F32)
            nh, _ = normalise(hidden)
            normed = (nh * gain + shift).astype(BF16)
            nrm[c] = normed
            for j in range(3):
                columns = pl.ds(j * width, width)
                keep_b[c, :, columns] = mm(normed, weight[:, columns]).astype(BF16)

            @pl.loop(0, width // (2 * HEAD_DIM))
            def _(pair):
                offset = pl.multiple_of(pair * 2 * HEAD_DIM, 2 * HEAD_DIM)
                q = keep_b[c, :, pl.ds(offset, 2 * HEAD_DIM)]
                k = keep_b[c, :, pl.ds(width + offset, 2 * HEAD_DIM)]
                v = keep_b[c, :, pl.ds(2 * width + offset, 2 * HEAD_DIM)]
                o = None
                for one in range(2):
                    z = mm_nt(k, q * pick_scaled[one]) + mask_add[micro]
                    top = jnp.max(z, axis=0, keepdims=True)
                    e = jnp.exp(z - top)
                    p = e * (1.0 / jnp.sum(e, axis=0, keepdims=True))
                    pb = p.astype(BF16)
                    spot = pl.multiple_of((2 * pair + one) * WINDOW, WINDOW)
                    keep_a[c, :, pl.ds(spot, WINDOW)] = pb
                    term = mm_tn(pb, v * pick[one])
                    o = term if o is None else o + term
                keep_b[c, :, pl.ds(3 * width + offset, 2 * HEAD_DIM)] = o.astype(BF16)

            branch = mm(keep_b[c, :, pl.ds(3 * width, width)], weight[:, pl.ds(3 * width, width)])
            leave[c] = (hin[c].astype(F32) + branch + bias).astype(BF16)
            remote(
                leave.at[c], hin.at[c], h_send.at[c], h_recv.at[c], section + 1, me
            ).start()

        def backward(c):
            @pl.when(c == 0)
            def _():
                clear_grads(4)

            remote(gin.at[c], gin.at[c], g_send.at[c], g_recv.at[c], section + 1, me).wait_recv()
            remote(
                leave.at[c], hin.at[c], h_send.at[c], h_recv.at[c], section + 1, me
            ).wait_send()
            gb = gin[c]
            work[...] = mm_nt(gb, weight[:, pl.ds(3 * width, width)]).astype(BF16)

            @pl.loop(0, width // (2 * HEAD_DIM))
            def _(pair):
                offset = pl.multiple_of(pair * 2 * HEAD_DIM, 2 * HEAD_DIM)
                q_at = pl.ds(offset, 2 * HEAD_DIM)
                k_at = pl.ds(width + offset, 2 * HEAD_DIM)
                v_at = pl.ds(2 * width + offset, 2 * HEAD_DIM)
                q, k, v = keep_b[c, :, q_at], keep_b[c, :, k_at], keep_b[c, :, v_at]
                go = work[:, q_at]
                dq = dk = dv = None
                for one in range(2):
                    spot = pl.multiple_of((2 * pair + one) * WINDOW, WINDOW)
                    pb = keep_a[c, :, pl.ds(spot, WINDOW)]
                    p = pb.astype(F32)
                    dp = mm_nt(v, go * pick[one])
                    pdp = p * dp
                    ds = (pdp - p * jnp.sum(pdp, axis=0, keepdims=True)).astype(BF16)
                    tv = mm(pb, go * pick[one])
                    tk = mm(ds, q * pick_scaled[one])
                    tq = mm_tn(ds, k * pick_scaled[one])
                    dv = tv if dv is None else dv + tv
                    dk = tk if dk is None else dk + tk
                    dq = tq if dq is None else dq + tq
                keep_b[c, :, q_at] = dq.astype(BF16)
                keep_b[c, :, k_at] = dk.astype(BF16)
                keep_b[c, :, v_at] = dv.astype(BF16)

            dn = mm_nt(keep_b[c, :, pl.ds(0, 3 * width)], weight[:, pl.ds(0, 3 * width)])
            leaving = norm_back(c, dn, gb).astype(BF16)

            @pl.when(section == 2)
            def _():
                send_blocks(c, leaving, ftab, 1, False)

            @pl.when(section == 0)
            def _():
                for s in range(SECTIONS):
                    gcol_ref[s, c] = leaving[:, s * quarter : (s + 1) * quarter]

            normed = nrm[c]
            for j in range(3):
                grads[j] += mm_tn(normed, keep_b[c, :, pl.ds(j * width, width)])
            grads[3] += mm_tn(keep_b[c, :, pl.ds(3 * width, width)], gin[c])

        @pl.loop(0, 2 * chunks)
        def _(step):
            c = lax.rem(step, chunks)

            @pl.when(step < chunks)
            def _():
                forward(c)

            @pl.when(step >= chunks)
            def _():
                backward(c)

    @pl.when(jnp.logical_not(is_attn))
    def _():
        early = remote(
            down_hbm.at[own_part], down.at[own_part], w_send.at[0], w_recv.at[0], section - 1, me
        )
        early_bias = remote(
            bias_late, bias_early, w_send.at[1], w_recv.at[1], section - 1, me
        )
        other = remote(
            down.at[other_part], down.at[other_part], w_send.at[0], w_recv.at[2], section, sibling
        )
        load_w.wait()
        early_bias.wait_recv()

        @pl.when(section == 3)
        def _():
            load_c.wait()
            clear_grads(8)

        def forward(c):
            remote(hin.at[c], hin.at[c], h_send.at[c], h_recv.at[c], section - 1, me).wait_recv()
            hidden = hin[c].astype(F32)
            nh, _ = normalise(hidden)
            normed = (nh * gain + shift).astype(BF16)
            nrm[c] = normed
            for j in range(4):
                columns = pl.ds(j * width, width)
                u = mm(normed, weight[:, columns])
                u = u + (bias_early, bias_late)[j // 2][:, pl.ds((j % 2) * width, width)]
                active, slope = gelu_and_slope(u)
                keep_a[c, :, columns] = active.astype(BF16)
                keep_b[c, :, columns] = slope.astype(BF16)

            @pl.when(c == 0)
            def _():
                early.wait_recv()
                pass_down.start()
                load_d.wait()
                other.wait_recv()

            branch = mm(keep_a[c], down[...])
            leaving = (hin[c].astype(F32) + branch + bias).astype(BF16)

            @pl.when(section == 1)
            def _():
                send_blocks(c, leaving, ttab, 2, True)

            @pl.when(section == 3)
            def _():
                for s in range(SECTIONS - 1):
                    gcol_ref[s, c] = leaving[:, s * quarter : (s + 1) * quarter]
                out_ref[c] = leaving[:, (SECTIONS - 1) * quarter :]
                for s in range(SECTIONS - 1):
                    remote(
                        gcol_ref.at[s, c], out_ref.at[c], o_send.at[s, c], o_recv.at[0], s, me
                    ).start()

        def backward(c):
            @pl.when(section == 1)
            def _():
                @pl.when(c == 0)
                def _():
                    clear_grads(8)

                gather_blocks(c, ftab, ttab, gin, 2, False)

            gb = gin[c]
            for j in range(4):
                columns = pl.ds(j * width, width)
                da = mm_nt(gb, down[columns])
                du = da * keep_b[c, :, columns].astype(F32)
                keep_b[c, :, columns] = du.astype(BF16)
                small_ref[3 + j : 4 + j] += jnp.sum(du, axis=0, keepdims=True)
            dn = mm_nt(keep_b[c], weight[...])
            leave[c] = norm_back(c, dn, gb).astype(BF16)
            remote(
                leave.at[c], gin.at[c], g_send.at[c], g_recv.at[c], section - 1, me
            ).start()
            normed = nrm[c]
            for j in range(4):
                columns = pl.ds(j * width, width)
                grads[j] += mm_tn(normed, keep_b[c, :, columns])
                grads[4 + j] += mm_tn(keep_a[c, :, columns], gin[c])

        @pl.loop(0, 2 * chunks)
        def _(step):
            last = lax.div(section, 2)
            c = last * lax.div(step, 2) + (1 - last) * lax.rem(step, chunks)
            back = last * lax.rem(step, 2) + (1 - last) * lax.div(step, chunks)

            @pl.when(back == 0)
            def _():
                forward(c)

            @pl.when(back == 1)
            def _():
                backward(c)

    @pl.when(is_attn)
    def _():
        send_down.wait_send()
        send_bias.wait_send()

    @pl.when(jnp.logical_not(is_attn))
    def _():
        pass_down.wait_send()

    stores = []
    for j in range(4):
        weight[:, pl.ds(j * width, width)] = grads[j].astype(BF16)
    for j in range(4):
        columns = pl.ds(j * width, width)
        store = pltpu.make_async_copy(
            weight.at[:, columns], grad_hbm.at[columns], load_sem.at[j]
        )
        store.start()
        stores.append(store)

    @pl.when(jnp.logical_not(is_attn))
    def _():
        more = []
        for j in range(4):
            rows = pl.ds(j * width, width)
            down[rows] = grads[4 + j].astype(BF16)
            store = pltpu.make_async_copy(
                down.at[rows], grad_hbm.at[pl.ds((4 + j) * width, width)], load_sem.at[4 + j]
            )
            store.start()
            more.append(store)
        for store in more:
            store.wait()

        @pl.loop(0, chunks)
        def _(c):
            remote(
                leave.at[c], gin.at[c], g_send.at[c], g_recv.at[c], section - 1, me
            ).wait_send()

    for store in stores:
        store.wait()

    @pl.when((section == 1) | (section == 2))
    def _():
        @pl.loop(chunks - depth, chunks)
        def _(c):
            slot = lax.rem(c, depth)
            remote(
                xsend.at[slot], xsend.at[slot], x_send.at[c], x_recv.at[0], 3 - section, me
            ).wait_send()

    @pl.when(section == 3)
    def _():
        @pl.loop(0, chunks)
        def _(c):
            for s in range(SECTIONS - 1):
                remote(
                    gcol_ref.at[s, c], out_ref.at[c], o_send.at[s, c], o_recv.at[0], s, me
                ).wait_send()

    @pl.when(section != 3)
    def _():
        remote(out_ref, out_ref, o_send.at[0, 0], o_recv.at[0], 3, me).wait_recv()


def pipeline(tokens, cotangent, gain, shift, weight, bias, down, hidden_bias, ftab, ttab, kind):
    micro, rows, width = tokens.shape
    wide = weight.shape[1]
    n = lax.axis_size("dp")
    across = min(n, 16)
    repeat = 16 // across
    slots = rows // WINDOW
    chunks = micro * slots
    quarter = width // SECTIONS
    depth = chunks if n <= 8 else slots
    cfg = (n, across, repeat, slots, chunks, width, wide, depth)
    vmem = pl.BlockSpec(memory_space=pltpu.VMEM)
    smem = pl.BlockSpec(memory_space=pltpu.SMEM)
    anywhere = pl.BlockSpec(memory_space=pl.ANY)
    dma = pltpu.SemaphoreType.DMA
    chunked = (chunks, WINDOW, width)
    return pl.pallas_call(
        functools.partial(main_kernel, cfg),
        out_shape=(
            jax.ShapeDtypeStruct((chunks, WINDOW, quarter), BF16),
            jax.ShapeDtypeStruct((SECTIONS, chunks, WINDOW, quarter), BF16),
            jax.ShapeDtypeStruct((8 * width, width), BF16),
            jax.ShapeDtypeStruct((8, width), F32),
        ),
        in_specs=[anywhere, anywhere, vmem, vmem, anywhere, vmem, anywhere, vmem, smem, smem, smem],
        out_specs=(vmem, vmem, anywhere, vmem),
        scratch_shapes=[
            pltpu.VMEM((width, wide), BF16),
            pltpu.VMEM((wide, width), BF16),
            pltpu.VMEM((8, width, width), F32),
            pltpu.VMEM((chunks, WINDOW, wide), BF16),
            pltpu.VMEM((chunks, WINDOW, wide), BF16),
            pltpu.VMEM(chunked, BF16),
            pltpu.VMEM(chunked, BF16),
            pltpu.VMEM(chunked, BF16),
            pltpu.VMEM(chunked, BF16),
            pltpu.VMEM((WINDOW, width), BF16),
            pltpu.VMEM((depth, n, repeat, BLOCK, width), BF16),
            pltpu.VMEM((slots, n, repeat, BLOCK, width), BF16),
            pltpu.VMEM((slots, n, repeat, BLOCK, width), BF16),
            pltpu.VMEM((WINDOW // BLOCK, BLOCK, width), BF16),
            pltpu.VMEM((1, wide // 2), F32),
            pltpu.VMEM((1, wide // 2), F32),
            pltpu.VMEM((2, WINDOW, WINDOW), F32),
            dma((8,)),
            dma((2,)),
            dma((3,)),
            dma((chunks,)),
            dma((chunks,)),
            dma((chunks,)),
            dma((chunks,)),
            dma((chunks,)),
            dma((micro,)),
            dma((SECTIONS - 1, chunks)),
            dma((1,)),
        ],
        compiler_params=pltpu.CompilerParams(
            collective_id=0, has_side_effects=True, vmem_limit_bytes=62 * 1024 * 1024
        ),
        name="pipeline",
    )(
        tokens.reshape(chunked),
        cotangent.reshape(chunked),
        gain,
        shift,
        weight,
        bias,
        down,
        hidden_bias.reshape(1, -1),
        ftab,
        ttab,
        kind,
    )


def reduce_kernel(
    cfg,
    grad_hbm,
    small_in,
    gcol_hbm,
    total_hbm,
    small_out,
    ig_ref,
    mine,
    theirs,
    from_low,
    from_high,
    acc,
    small_all,
    small_pair,
    load_sem,
    sib_send,
    sib_recv,
    up_send,
    low_recv,
    down_send,
    high_recv,
    left_send,
    right_send,
    total_recv,
    pair_send,
    pair_recv,
    local_sem,
    x_send,
    x_recv,
    small_send,
    small_recv,
    spair_send,
    spair_recv,
    ig_send,
    ig_recv,
    x_ready,
):
    n, chunk, w_chunks, d_chunks, lag, begin = cfg
    section = lax.axis_index("section")
    me = lax.axis_index("dp")
    core = lax.rem(me, 2)
    place = lax.div(me, 2)
    places = n // 2
    sibling = me + 1 - 2 * core
    is_attn = lax.rem(section, 2) == 0
    not_attn = jnp.logical_not(is_attn)
    partner = section + 1 - 2 * lax.rem(section, 2)
    lines = w_chunks + d_chunks
    half_w = w_chunks * chunk
    half_d = d_chunks * chunk

    def pieces(of_core):
        return (
            grad_hbm.at[pl.ds(of_core * half_w, half_w)],
            grad_hbm.at[pl.ds(2 * half_w + 2 * half_d + of_core * half_d, half_d)],
            grad_hbm.at[pl.ds(2 * half_w + of_core * half_d, half_d)],
        )

    spans = ((0, w_chunks), (w_chunks, d_chunks), (lines, d_chunks))
    loads = [
        pltpu.make_async_copy(
            piece, mine.at[pl.ds(first * chunk, count * chunk)], load_sem.at[at]
        )
        for at, (piece, (first, count)) in enumerate(zip(pieces(core), spans))
    ]

    loads[0].start()

    @pl.when(not_attn)
    def _():
        loads[1].start()
        loads[2].start()

    barrier = pltpu.get_barrier_semaphore()

    def greet(s, d):
        pl.semaphore_signal(barrier, inc=1, device_id=(s, d), device_id_type=MESH)

    @pl.loop(0, n)
    def _(d):
        @pl.when(d != me)
        def _():
            greet(section, d)

    @pl.when(section != 0)
    def _():
        greet(0, me)

    @pl.when(section == 3)
    def _():
        greet(2, me)

    pl.semaphore_wait(
        barrier, n - 1 + jnp.where(section == 0, 3, jnp.where(section == 2, 1, 0))
    )

    @pl.when(is_attn)
    def _():
        pl.semaphore_signal(x_ready, inc=1, device_id=(partner, me), device_id_type=MESH)

    def rows(i):
        return pl.ds(pl.multiple_of(i * chunk, chunk), chunk)

    def sib_copy(i, source_row):
        return remote(
            grad_hbm.at[pl.ds(pl.multiple_of(source_row, chunk), chunk)],
            theirs.at[rows(i)],
            sib_send.at[i],
            sib_recv.at[i],
            section,
            sibling,
        )

    def sib_row(i):
        from_w = (1 - core) * half_w + i * chunk
        late = 2 * half_w + 2 * half_d + (1 - core) * half_d + (i - w_chunks) * chunk
        early = 2 * half_w + (1 - core) * half_d + (i - lines) * chunk
        return jnp.where(i < w_chunks, from_w, jnp.where(i < lines, late, early))

    sib_count = jnp.where(is_attn, w_chunks, lines + d_chunks)

    @pl.loop(0, lines + d_chunks)
    def _(i):
        @pl.when(i < sib_count)
        def _():
            sib_copy(i, sib_row(i)).start()

    small_all[me] = small_in[...]

    def small_copy(d):
        return remote(
            small_in, small_all.at[me], small_send.at[d], small_recv.at[0], section, d
        )

    @pl.loop(0, n)
    def _(d):
        @pl.when(d != me)
        def _():
            small_copy(d).start()

    def ig_copy(s):
        return remote(gcol_hbm.at[s], ig_ref, ig_send.at[s], ig_recv.at[0], s, me)

    ig_own = pltpu.make_async_copy(gcol_hbm.at[0], ig_ref, ig_send.at[0])

    @pl.when(section == 0)
    def _():
        ig_own.start()
        for s in range(1, SECTIONS):
            ig_copy(s).start()

    def root_of(i):
        return places // 2 - 1 + lax.rem(i, 2)

    def total_rows(i):
        return total_hbm.at[core, rows(i)]

    def up_copy(i):
        return remote(
            mine.at[rows(i)], from_low.at[rows(i)], up_send.at[i], low_recv.at[i], section, me + 2
        )

    def down_copy(i):
        return remote(
            mine.at[rows(i)],
            from_high.at[rows(i)],
            down_send.at[i],
            high_recv.at[i],
            section,
            me - 2,
        )

    def left_copy(i, source):
        return remote(
            source, total_rows(i), left_send.at[i], total_recv.at[i], section, me - 2
        )

    def right_copy(i, source):
        return remote(
            source, total_rows(i), right_send.at[i], total_recv.at[i], section, me + 2
        )

    def pair_copy(i, source):
        return remote(
            source, total_rows(i), pair_send.at[i], pair_recv.at[0], section, sibling
        )

    def own_copy(i):
        return pltpu.make_async_copy(mine.at[rows(i)], total_rows(i), local_sem.at[i])

    def x_copy(e):
        return remote(
            mine.at[rows(lines + e)],
            mine.at[rows(w_chunks + e)],
            x_send.at[e],
            x_recv.at[e],
            partner,
            me,
        )

    def reduce_stage(i):
        root = root_of(i)
        summed = is_attn & (i >= w_chunks)

        @pl.when(i == 0)
        def _():
            loads[0].wait()

        @pl.when((i == w_chunks) & not_attn)
        def _():
            loads[1].wait()

        @pl.when(summed)
        def _():
            x_copy(i - w_chunks).wait_recv()
            acc[...] = mine[rows(i)].astype(F32)

        @pl.when(jnp.logical_not(summed))
        def _():
            sib_copy(i, 0).wait_recv()
            acc[...] = mine[rows(i)].astype(F32) + theirs[rows(i)].astype(F32)

        @pl.when((place <= root) & (place > 0))
        def _():
            up_copy(i).wait_recv()
            acc[...] += from_low[rows(i)].astype(F32)

        @pl.when((place >= root) & (place < places - 1))
        def _():
            down_copy(i).wait_recv()
            acc[...] += from_high[rows(i)].astype(F32)

        mine[rows(i)] = acc[...].astype(BF16)

        @pl.when(place < root)
        def _():
            up_copy(i).start()

        @pl.when(place > root)
        def _():
            down_copy(i).start()

        @pl.when(place == root)
        def _():
            source = mine.at[rows(i)]

            @pl.when(place > 0)
            def _():
                left_copy(i, source).start()

            @pl.when(place < places - 1)
            def _():
                right_copy(i, source).start()

            pair_copy(i, source).start()
            own_copy(i).start()

    def early_stage(e):
        @pl.when(e == 0)
        def _():
            loads[2].wait()
            pl.semaphore_wait(x_ready, 1)

        sib_copy(lines + e, 0).wait_recv()
        here = rows(lines + e)
        mine[here] = (mine[here].astype(F32) + theirs[here].astype(F32)).astype(BF16)
        x_copy(e).start()

    def spread_stage(i):
        root = root_of(i)

        @pl.when(place != root)
        def _():
            left_copy(i, total_rows(i)).wait_recv()

            @pl.when((place < root) & (place > 0))
            def _():
                left_copy(i, total_rows(i)).start()

            @pl.when((place > root) & (place < places - 1))
            def _():
                right_copy(i, total_rows(i)).start()

            pair_copy(i, total_rows(i)).start()

    @pl.loop(0, lines + lag)
    def _(i):
        @pl.when(i < lines)
        def _():
            reduce_stage(i)

        @pl.when(not_attn & (i >= begin) & (i < begin + d_chunks))
        def _():
            early_stage(i - begin)

        @pl.when(i >= lag)
        def _():
            spread_stage(i - lag)

    remote(
        small_all.at[pl.ds(0, n - 1)],
        small_all.at[pl.ds(0, n - 1)],
        small_send.at[0],
        small_recv.at[0],
        section,
        sibling,
    ).wait_recv()

    def add(d, so_far):
        return so_far + small_all[d]

    small_out[...] = lax.fori_loop(1, n, add, small_all[0])
    to_pair = remote(
        small_out, small_pair, spair_send.at[0], spair_recv.at[0], partner, me
    )

    @pl.when(not_attn)
    def _():
        to_pair.start()
        to_pair.wait_send()

    @pl.when(is_attn)
    def _():
        to_pair.wait_recv()
        small_out[5:7] = small_pair[3:5]

    @pl.loop(0, lines)
    def _(i):
        root = root_of(i)

        @pl.when(place < root)
        def _():
            up_copy(i).wait_send()

        @pl.when(place > root)
        def _():
            down_copy(i).wait_send()

        @pl.when((place <= root) & (place > 0))
        def _():
            left_copy(i, total_rows(i)).wait_send()

        @pl.when((place >= root) & (place < places - 1))
        def _():
            right_copy(i, total_rows(i)).wait_send()

        pair_copy(i, total_rows(i)).wait_send()

        @pl.when(place == root)
        def _():
            own_copy(i).wait()

    @pl.loop(0, lines + d_chunks)
    def _(i):
        @pl.when(i < sib_count)
        def _():
            sib_copy(i, 0).wait_send()

    @pl.when(not_attn)
    def _():
        @pl.loop(0, d_chunks)
        def _(e):
            x_copy(e).wait_send()

    @pl.loop(0, n)
    def _(d):
        @pl.when(d != me)
        def _():
            small_copy(d).wait_send()

    @pl.when(section == 0)
    def _():
        ig_own.wait()
        for s in range(1, SECTIONS):
            ig_copy(s).wait_send()

    @pl.when(section != 0)
    def _():
        ig_copy(0).wait_recv()

    remote(
        total_hbm.at[1 - core],
        total_hbm.at[1 - core],
        pair_send.at[0],
        pair_recv.at[0],
        section,
        sibling,
    ).wait_recv()


def reduction(grads, small, gcol, chunk=96):
    width = grads.shape[1]
    half_w = 2 * width
    half_d = width
    n = lax.axis_size("dp")
    w_chunks, d_chunks = half_w // chunk, half_d // chunk
    lines = w_chunks + d_chunks
    cfg = (n, chunk, w_chunks, d_chunks, min(6, lines), d_chunks)
    vmem = pl.BlockSpec(memory_space=pltpu.VMEM)
    anywhere = pl.BlockSpec(memory_space=pl.ANY)
    dma = pltpu.SemaphoreType.DMA
    every = lines + d_chunks
    return pl.pallas_call(
        functools.partial(reduce_kernel, cfg),
        out_shape=(
            jax.ShapeDtypeStruct((2, half_w + half_d, width), BF16),
            jax.ShapeDtypeStruct((8, width), F32),
            jax.ShapeDtypeStruct(gcol.shape[1:], BF16),
        ),
        in_specs=[anywhere, vmem, anywhere],
        out_specs=(anywhere, vmem, vmem),
        scratch_shapes=[
            pltpu.VMEM((every * chunk, width), BF16),
            pltpu.VMEM((every * chunk, width), BF16),
            pltpu.VMEM((lines * chunk, width), BF16),
            pltpu.VMEM((lines * chunk, width), BF16),
            pltpu.VMEM((chunk, width), F32),
            pltpu.VMEM((n, 8, width), F32),
            pltpu.VMEM((8, width), F32),
            dma((3,)),
            dma((every,)),
            dma((every,)),
            dma((lines,)),
            dma((lines,)),
            dma((lines,)),
            dma((lines,)),
            dma((lines,)),
            dma((lines,)),
            dma((lines,)),
            dma((lines,)),
            dma((1,)),
            dma((lines,)),
            dma((d_chunks,)),
            dma((d_chunks,)),
            dma((n,)),
            dma((1,)),
            dma((1,)),
            dma((1,)),
            dma((SECTIONS,)),
            dma((1,)),
            pltpu.SemaphoreType.REGULAR,
        ],
        compiler_params=pltpu.CompilerParams(
            collective_id=1, has_side_effects=True, vmem_limit_bytes=40 * 1024 * 1024
        ),
        name="reduction",
    )(grads, small, gcol)


def on_device(
    tokens,
    cotangent,
    norm_gain,
    norm_shift,
    in_weight,
    out_bias,
    down_weight,
    hidden_bias,
    frame_device,
    tube_device,
    clip_kind,
):
    micro, rows, width = tokens.shape
    output, gcol, grads, small = pipeline(
        tokens,
        cotangent,
        norm_gain,
        norm_shift,
        in_weight[0],
        out_bias,
        down_weight,
        hidden_bias,
        frame_device,
        tube_device,
        clip_kind,
    )
    total, small_total, input_grad = reduction(grads, small, gcol)
    split = total.shape[1] * 2 // 3
    grad_weight = total[:, :split].reshape(SECTIONS, width, width).transpose(1, 0, 2)
    quarter = width // SECTIONS
    return (
        output.reshape(micro, rows, quarter),
        input_grad.astype(F32).reshape(micro, rows, quarter),
        small_total[0:1],
        small_total[1:2],
        grad_weight.reshape(1, width, -1).astype(F32),
        small_total[2:3],
        total[:, split:].reshape(-1, width).astype(F32),
        small_total[5:7].reshape(-1),
    )


def solution(mesh):
    return jax.shard_map(
        on_device,
        mesh=mesh,
        in_specs=(
            P(None, "dp", None),
            P(None, "dp", None),
            P("section", None),
            P("section", None),
            P("section", None, None),
            P("section", None),
            P("section", None),
            P("section"),
            P(),
            P(),
            P(),
        ),
        out_specs=(
            P(None, "dp", "section"),
            P(None, "dp", "section"),
            P("section", None),
            P("section", None),
            P("section", None, None),
            P("section", None),
            P("section", None),
            P("section"),
        ),
        check_vma=False,
    )
```

time: 1430 us -> 430 us (0.30)
  waiting for transfers between devices: 845 us -> 0 us
  Pallas kernels: 0 us -> 381 us
  matrix products: 121 us -> 0 us
  local copies, waits for them, and re-layouts: 160 us -> 41 us
  other arithmetic: 92.3 us -> 7.34 us
  loops' own time: 84.9 us -> 0 us
  starting transfers between devices: 72.6 us -> 0 us
  blocking collectives: 27.9 us -> 0 us
  between operations: 19.7 us -> 0.68 us
    pallas_call x0 -> x2, Pallas kernels: none -> 381 us  [the longest x1 203 us: pipeline(): pl.pallas_call(functools.partial(main_kernel, cfg), out_shape=(jax.ShapeD...]
    ppermute x12 -> x0, waiting for transfers between devices: 344 us -> none  [shifted(): lax.ppermute(value, axis, [(source, source + steps) for source in range(l...]
    psum x1 -> x0, waiting for transfers between devices: 339 us -> none  [on_device(): lax.psum((grad_weight, grad_down, grad_hidden, grad_gain, grad_shift, gra...]
    dot_general x30 -> x0, matrix products: 121 us -> none  [the longest x2 22.8 us: attention_backward(): jnp.einsum('shqk,sqhd->skhd', grad_scores, queries, preferred_element_typ...]
    another operation x10 -> x0, loops' own time: 84.9 us -> none  [the longest x5 46.4 us: on_device(): lax.switch(selector, [attention_branch, feed_branch, spare_branch], enter...]
    all_to_all x4 -> x0, waiting for transfers between devices: 83.6 us -> none  [the longest x2 41.8 us: to_tubes(): lax.all_to_all(shortened(outgoing), 'dp', split_axis=0, concat_axis=0, ti...]
    ppermute x12 -> x0, starting transfers between devices: 56.5 us -> none  [shifted(): lax.ppermute(value, axis, [(source, source + steps) for source in range(l...]
    unnamed x4 -> x0, waiting for transfers between devices: 46.5 us -> none
  transfers between devices with their start and end apart: 19 -> 0, of which waited for: 16 -> 0; matrix products, arithmetic and copies ran while one was open for 2% -> 0% of each run, Pallas kernels for 0% -> 0%
where the time goes in v1:
time: 430 us
  Pallas kernels  381 us (89%)
  local copies, waits for them, and re-layouts  41 us (10%)
  other arithmetic  7.34 us (2%)
    pallas_call x1, Pallas kernels, pipeline(): pl.pallas_call(functools.partial(main_kernel, cfg), out_shape=(jax.ShapeD...  203 us
    pallas_call x1, Pallas kernels, reduction(): pl.pallas_call(functools.partial(reduce_kernel, cfg), out_shape=(jax.Shap...  177 us
    convert_element_type x2, local copies, waits for them, and re-layouts, on_device(): grad_weight.reshape(1, width, -1).astype(F32)  25.6 us

profile of v1, /device:TPU:0, one launch (start us, length us, event | category | flops | bytes accessed | tf_op | source)
XLA Modules:
  0.0 429.7 jit_solution(6334839280744667380)
XLA Ops:
  0.6 1.3 reshape.60.hb_ref
  1.9 203.5 %pipeline.1 = (bf16[4,256,192]{2,1,0:T(8,128)(2,1)}, bf16[4,4,256,192]{3,2,1,0:T(8,128)(2,1)}, bf16[6144,768]{1,0:T(8,128)(2,1)}, f32[8,768]{1,0:T(8,128)}) custom-call(bf16[4,256,768]{2,1,0:T(8,128)(2,1)} %bitcast.18, bf16[4,256,768]{2,1,0:T(8,128)(2,1)} %bitcast.19, bf16[1,768]{1,0:T(2,128)(2,1)} %gain_ref.1, bf16[1,768]{1,0:T(2,128)(2,1)} %shift_ref.1, ...), custom_call_target="tpu_custom_call" | custom-call | tf_op jit(solution)/shard_map/pipeline/pallas_call | solution.py:586
  205.4 2.0 copy.20
  207.4 0.0 copy-start.1
  207.4 1.6 copy-done.1
  209.0 0.0 copy-start.2
  209.0 0.7 copy-done.2
  209.7 177.2 %reduction.1 = (bf16[2,2304,768]{2,1,0:T(8,128)(2,1)S(1)}, f32[8,768]{1,0:T(8,128)S(1)}, bf16[4,256,192]{2,1,0:T(8,128)(2,1)S(1)}) custom-call(bf16[6144,768]{1,0:T(8,128)(2,1)} %get-tuple-element.16.grad_hbm, f32[8,768]{1,0:T(8,128)S(1)} %copy-done.2, bf16[4,4,256,192]{3,2,1,0:T(8,128)(2,1)S(1)} %copy-done.1), custom_call_target="tpu_custom_call" | custom-call | tf_op jit(solution)/shard_map/reduction/pallas_call | solution.py:1048
  386.9 0.0 copy-start
  387.0 3.0 copy-done
  389.9 0.6 fusion
  390.5 0.6 reshape.64
  391.1 0.1 bitcast_convert_fusion.1
  391.2 1.2 copy.21
  392.4 1.8 slice.22
  394.2 2.6 slice.20
  396.9 2.7 bitcast_convert_fusion
  399.6 4.6 %convert_bitcast_fusion = f32[768,4,768]{2,0,1:T(8,128)} fusion(bf16[4,768,768]{2,1,0:T(8,128)(2,1)S(1)} %bitcast.16), kind=kLoop, calls=%fused_computation | loop fusion | flops 2359296 | bytes 14155776 | tf_op jit(solution)/shard_map/convert_element_type | solution.py:1131
  404.1 13.4 %copy.19 = f32[768,4,768]{2,1,0:T(4,128)} copy(f32[768,4,768]{2,0,1:T(8,128)} %convert_bitcast_fusion) | data formatting | bytes 18874368 | tf_op jit(solution)/shard_map/convert_element_type | solution.py:1131
  417.5 12.3 %reshape.67 = f32[1,768,3072]{2,1,0:T(8,128)} reshape(f32[768,4,768]{2,1,0:T(4,128)} %copy.19) | data formatting | bytes 18874368 | tf_op jit(solution)/shard_map/convert_element_type | solution.py:1131
  (1 shorter events, 0.0 us)
Async XLA Ops:
  207.4 1.6 copy-start.1
  209.0 0.7 copy-start.2
  386.9 3.0 copy-start

commit v2 on v1

--- a/solution.py
+++ b/solution.py
@@ -843,17 +843,8 @@
             me,
         )
 
-    def reduce_stage(i):
-        root = root_of(i)
+    def reduce_stage(i, root):
         summed = is_attn & (i >= w_chunks)
-
-        @pl.when(i == 0)
-        def _():
-            loads[0].wait()
-
-        @pl.when((i == w_chunks) & not_attn)
-        def _():
-            loads[1].wait()
 
         @pl.when(summed)
         def _():
@@ -911,9 +902,7 @@
         mine[here] = (mine[here].astype(F32) + theirs[here].astype(F32)).astype(BF16)
         x_copy(e).start()
 
-    def spread_stage(i):
-        root = root_of(i)
-
+    def spread_stage(i, root):
         @pl.when(place != root)
         def _():
             left_copy(i, total_rows(i)).wait_recv()
@@ -928,19 +917,37 @@
 
             pair_copy(i, total_rows(i)).start()
 
-    @pl.loop(0, lines + lag)
-    def _(i):
-        @pl.when(i < lines)
-        def _():
-            reduce_stage(i)
-
-        @pl.when(not_attn & (i >= begin) & (i < begin + d_chunks))
-        def _():
-            early_stage(i - begin)
-
-        @pl.when(i >= lag)
-        def _():
-            spread_stage(i - lag)
+    loads[0].wait()
+
+    @pl.when(not_attn)
+    def _():
+        loads[1].wait()
+
+    height = places // 2
+    pairs = lines // 2
+
+    @pl.loop(0, pairs + 2 * height * lag)
+    def _(step):
+        @pl.when(not_attn & (step >= begin) & (step < begin + d_chunks // 2))
+        def _():
+            for stream in range(2):
+                early_stage(2 * (step - begin) + stream)
+
+        for stream in range(2):
+            root = height - 1 + stream
+            now = step - lag * (height - jnp.abs(place - root))
+
+            @pl.when((now >= 0) & (now < pairs))
+            def _():
+                reduce_stage(2 * now + stream, root)
+
+        for stream in range(2):
+            root = height - 1 + stream
+            past = step - lag * (height + jnp.abs(place - root))
+
+            @pl.when((past >= 0) & (past < pairs))
+            def _():
+                spread_stage(2 * past + stream, root)
 
     remote(
         small_all.at[pl.ds(0, n - 1)],
@@ -1033,14 +1040,14 @@
     ).wait_recv()
 
 
-def reduction(grads, small, gcol, chunk=96):
+def reduction(grads, small, gcol, chunk=96, lag=1):
     width = grads.shape[1]
     half_w = 2 * width
     half_d = width
     n = lax.axis_size("dp")
     w_chunks, d_chunks = half_w // chunk, half_d // chunk
     lines = w_chunks + d_chunks
-    cfg = (n, chunk, w_chunks, d_chunks, min(6, lines), d_chunks)
+    cfg = (n, chunk, w_chunks, d_chunks, lag, d_chunks // 2)
     vmem = pl.BlockSpec(memory_space=pltpu.VMEM)
     anywhere = pl.BlockSpec(memory_space=pl.ANY)
     dma = pltpu.SemaphoreType.DMA
@@ -1092,6 +1099,96 @@
     )(grads, small, gcol)
 
 
+def finish_kernel(
+    total_ref,
+    small_ref,
+    ig_ref,
+    out_ref,
+    output,
+    input_grad,
+    gain,
+    shift,
+    weight,
+    bias,
+    down,
+    hidden,
+):
+    block, row = pl.program_id(0), pl.program_id(1)
+
+    @pl.when((block == 0) & (row == 0))
+    def _():
+        output[...] = out_ref[...]
+        input_grad[...] = ig_ref[...].astype(F32)
+        gain[...] = small_ref[0:1]
+        shift[...] = small_ref[1:2]
+        bias[...] = small_ref[2:3]
+        hidden[...] = small_ref[5:7]
+
+    is_down = block % 3 == 2
+
+    @pl.when(jnp.logical_not(is_down))
+    def _():
+        weight[...] = total_ref[0].astype(F32)
+
+    @pl.when(is_down)
+    def _():
+        down[...] = total_ref[0].astype(F32)
+
+
+def finish(total, small, input_grad, output):
+    width = total.shape[-1]
+    steps = 2
+    span = width // steps
+
+    def whole(array):
+        return pl.BlockSpec(array.shape, lambda b, r, k=array.ndim: (0,) * k)
+
+    def weight_at(b, r):
+        half, inner = b // 3, b % 3
+        return jnp.where(inner == 2, steps - 1, r), 2 * half + jnp.minimum(inner, 1)
+
+    def down_at(b, r):
+        half, inner = b // 3, b % 3
+        earlier = jnp.where(half == 0, 0, steps - 1)
+        return jnp.where(inner == 2, steps * half + r, earlier), 0
+
+    row = jax.ShapeDtypeStruct((1, width), F32)
+    pair = jax.ShapeDtypeStruct((2, width), F32)
+    wide_grad = jax.ShapeDtypeStruct(input_grad.shape, F32)
+    return pl.pallas_call(
+        finish_kernel,
+        grid=(6, steps),
+        out_shape=(
+            output,
+            wide_grad,
+            row,
+            row,
+            jax.ShapeDtypeStruct((width, SECTIONS * width), F32),
+            row,
+            jax.ShapeDtypeStruct((2 * width, width), F32),
+            pair,
+        ),
+        in_specs=[
+            pl.BlockSpec((1, span, width), lambda b, r: (b, r, 0)),
+            whole(small),
+            whole(input_grad),
+            whole(output),
+        ],
+        out_specs=(
+            whole(output),
+            whole(wide_grad),
+            whole(row),
+            whole(row),
+            pl.BlockSpec((span, width), weight_at),
+            whole(row),
+            pl.BlockSpec((span, width), down_at),
+            whole(pair),
+        ),
+        compiler_params=pltpu.CompilerParams(vmem_limit_bytes=32 * 1024 * 1024),
+        name="finish",
+    )(total.reshape(6, width, width), small, input_grad, output)
+
+
 def on_device(
     tokens,
     cotangent,
@@ -1120,18 +1217,19 @@
         clip_kind,
     )
     total, small_total, input_grad = reduction(grads, small, gcol)
-    split = total.shape[1] * 2 // 3
-    grad_weight = total[:, :split].reshape(SECTIONS, width, width).transpose(1, 0, 2)
+    output, input_grad, gain, shift, weight, bias, down, hidden = finish(
+        total, small_total, input_grad, output
+    )
     quarter = width // SECTIONS
     return (
         output.reshape(micro, rows, quarter),
-        input_grad.astype(F32).reshape(micro, rows, quarter),
-        small_total[0:1],
-        small_total[1:2],
-        grad_weight.reshape(1, width, -1).astype(F32),
-        small_total[2:3],
-        total[:, split:].reshape(-1, width).astype(F32),
-        small_total[5:7].reshape(-1),
+        input_grad.reshape(micro, rows, quarter),
+        gain,
+        shift,
+        weight[None],
+        bias,
+        down,
+        hidden.reshape(-1),
     )
 
 

time: 430 us -> 320 us (0.74)
  Pallas kernels: 381 us -> 313 us
  local copies, waits for them, and re-layouts: 41 us -> 6.35 us
  other arithmetic: 7.34 us -> 0 us
    pallas_call x1, Pallas kernels: 177 us -> 102 us  [reduction(): pl.pallas_call(functools.partial(reduce_kernel, cfg), out_shape=(jax.Shap...]
    convert_element_type x2 -> x0, local copies, waits for them, and re-layouts: 25.6 us -> none  [on_device(): grad_weight.reshape(1, width, -1).astype(F32)]
    pallas_call x0 -> x1, Pallas kernels: none -> 7.58 us  [finish(): pl.pallas_call(finish_kernel, grid=(6, steps), out_shape=(output, wide_gr...]
    convert_element_type x2 -> x0, other arithmetic: 7.26 us -> none  [the longest x1 4.56 us: on_device(): grad_weight.reshape(1, width, -1).astype(F32)]
    slice x4 -> x0, local copies, waits for them, and re-layouts: 5.06 us -> none  [the longest x1 2.65 us: on_device(): total[:, :split].reshape(SECTIONS, width, width).transpose(1, 0, 2)]
where the time goes in v2:
time: 320 us
  Pallas kernels  313 us (98%)
  local copies, waits for them, and re-layouts  6.35 us (2%)
    pallas_call x1, Pallas kernels, pipeline(): pl.pallas_call(functools.partial(main_kernel, cfg), out_shape=(jax.ShapeD...  203 us
    pallas_call x1, Pallas kernels, reduction(): pl.pallas_call(functools.partial(reduce_kernel, cfg), out_shape=(jax.Shap...  102 us
    pallas_call x1, Pallas kernels, finish(): pl.pallas_call(finish_kernel, grid=(6, steps), out_shape=(output, wide_gr...  7.58 us

profile of v2, /device:TPU:0, one launch (start us, length us, event | category | flops | bytes accessed | tf_op | source)
XLA Modules:
  0.0 319.6 jit_solution(5149596395649764051)
XLA Ops:
  0.6 1.3 reshape.39.hb_ref
  1.9 203.5 %pipeline.1 = (bf16[4,256,192]{2,1,0:T(8,128)(2,1)}, bf16[4,4,256,192]{3,2,1,0:T(8,128)(2,1)}, bf16[6144,768]{1,0:T(8,128)(2,1)}, f32[8,768]{1,0:T(8,128)}) custom-call(bf16[4,256,768]{2,1,0:T(8,128)(2,1)} %bitcast.11, bf16[4,256,768]{2,1,0:T(8,128)(2,1)} %bitcast.12, bf16[1,768]{1,0:T(2,128)(2,1)} %gain_ref.1, bf16[1,768]{1,0:T(2,128)(2,1)} %shift_ref.1, ...), custom_call_target="tpu_custom_call" | custom-call | tf_op jit(solution)/shard_map/pipeline/pallas_call | solution.py:586
  205.4 0.0 copy-start
  205.4 1.6 copy-done
  207.0 0.0 copy-start.2
  207.0 0.7 copy-done.2
  207.7 0.0 copy-start.1
  207.7 101.6 %reduction.1 = (bf16[2,2304,768]{2,1,0:T(8,128)(2,1)S(1)}, f32[8,768]{1,0:T(8,128)S(1)}, bf16[4,256,192]{2,1,0:T(8,128)(2,1)S(1)}) custom-call(bf16[6144,768]{1,0:T(8,128)(2,1)} %get-tuple-element.23.grad_hbm, f32[8,768]{1,0:T(8,128)S(1)} %copy-done.2, bf16[4,4,256,192]{3,2,1,0:T(8,128)(2,1)S(1)} %copy-done), custom_call_target="tpu_custom_call" | custom-call | tf_op jit(solution)/shard_map/reduction/pallas_call | solution.py:1055
  309.3 0.0 copy-done.1
  309.3 7.6 %finish.1 = (bf16[4,256,192]{2,1,0:T(8,128)(2,1)S(1)}, f32[4,256,192]{2,1,0:T(8,128)S(1)}, f32[1,768]{1,0:T(1,128)}, f32[1,768]{1,0:T(1,128)}, f32[768,3072]{1,0...) custom-call(bf16[6,768,768]{2,1,0:T(8,128)(2,1)S(1)} %bitcast.7, ...), custom_call_target="tpu_custom_call" | custom-call | tf_op jit(solution)/shard_map/finish/pallas_call | solution.py:1158
  316.9 0.9 copy.19
  317.8 1.2 copy.20
  319.0 0.6 reshape.43
Async XLA Ops:
  205.4 1.6 copy-start
  207.0 0.7 copy-start.2
  207.7 101.6 %copy-start.1 = (bf16[4,256,192]{2,1,0:T(8,128)(2,1)S(1)}, bf16[4,256,192]{2,1,0:T(8,128)(2,1)}, u32[]{:S(2)}) copy-start(bf16[4,256,192]{2,1,0:T(8,128)(2,1)} %get-tuple-element.29.out_ref) | copy-start | bytes 1179652

commit v3 on v2

v3 whole, which is shorter than its diff:
```python
import functools

import jax
import jax.numpy as jnp
from jax import lax
from jax.experimental import pallas as pl
from jax.experimental.pallas import tpu as pltpu
from jax.sharding import PartitionSpec as P

HEAD_DIM = 64
WINDOW = 256
BLOCK = 16
SECTIONS = 4
EPS = 1e-06
NEGATIVE = -1e30
MESH = pl.DeviceIdType.MESH
F32 = jnp.float32
BF16 = jnp.bfloat16


def mm(left, right):
    return lax.dot_general(left, right, (((1,), (0,)), ((), ())), preferred_element_type=F32)


def mm_nt(left, right):
    return lax.dot_general(left, right, (((1,), (1,)), ((), ())), preferred_element_type=F32)


def mm_tn(left, right):
    return lax.dot_general(left, right, (((0,), (0,)), ((), ())), preferred_element_type=F32)


def remote(src, dst, send_sem, recv_sem, section, dp):
    return pltpu.make_async_remote_copy(
        src_ref=src,
        dst_ref=dst,
        send_sem=send_sem,
        recv_sem=recv_sem,
        device_id=(section, dp),
        device_id_type=MESH,
    )


def normalise(hidden):
    average = jnp.mean(hidden, axis=-1, keepdims=True)
    centred = hidden - average
    inverse = lax.rsqrt(jnp.mean(centred * centred, axis=-1, keepdims=True) + EPS)
    return centred * inverse, inverse


def gelu_and_slope(u):
    cdf = 0.5 + 0.5 * lax.erf(u * 0.7071067811865476)
    bell = jnp.exp(-0.5 * u * u)
    return u * cdf, cdf + (0.3989422804014327 * u) * bell


def main_kernel(
    cfg,
    tok_hbm,
    cot_hbm,
    gain_ref,
    shift_ref,
    w_hbm,
    bias_ref,
    down_hbm,
    hb_ref,
    ftab,
    ttab,
    kind,
    out_ref,
    ig_ref,
    total_hbm,
    small_out,
    weights,
    keep_a,
    keep_b,
    hin,
    gin,
    leave,
    nrm,
    work,
    gcol,
    xsend,
    xrecv0,
    xrecv1,
    blocks,
    bias_early,
    bias_late,
    mask_add,
    spots,
    sources,
    guest,
    theirs,
    from_low,
    from_high,
    acc,
    small,
    small_all,
    small_pair,
    load_sem,
    w_send,
    w_recv,
    hb_send,
    hb_recv,
    h_send,
    h_recv,
    g_send,
    g_recv,
    x_send,
    x_recv,
    o_send,
    o_recv,
    ig_send,
    ig_recv,
    sib_send,
    sib_recv,
    up_send,
    low_recv,
    down_send,
    high_recv,
    left_send,
    right_send,
    total_recv,
    pair_send,
    pair_recv,
    local_sem,
    early_send,
    early_recv,
    guest_send,
    guest_recv,
    small_send,
    small_recv,
    spair_send,
    spair_recv,
):
    n, across, repeat, slots, chunks, width, wide, depth, chunk, lag, pieces = cfg
    section = lax.axis_index("section")
    me = lax.axis_index("dp")
    core = lax.rem(me, 2)
    place = lax.div(me, 2)
    places = n // 2
    sibling = me + 1 - 2 * core
    odd_place = lax.rem(place, 2)
    across_z = me + 2 - 4 * odd_place
    odd = lax.rem(section, 2)
    is_attn = odd == 0
    not_attn = odd == 1
    partner = section + 1 - 2 * odd
    is_first, is_last = lax.div(3 - section, 3), lax.div(section, 3)
    xrecv = (xrecv0, xrecv1)
    half = wide // 2
    quarter = width // SECTIONS

    def load_columns(j):
        columns = pl.ds(j * width, width)
        return pltpu.make_async_copy(w_hbm.at[:, columns], weights.at[j], load_sem.at[j])

    def load_rows(j):
        rows = pl.ds(j * width, width)
        return pltpu.make_async_copy(down_hbm.at[rows], weights.at[6 + j], load_sem.at[6 + j])

    load_t = pltpu.make_async_copy(tok_hbm, hin, load_sem.at[5])
    load_c = pltpu.make_async_copy(cot_hbm, gin, load_sem.at[5])

    @pl.when(section == 0)
    def _():
        load_t.start()

    for j in range(4):
        load_columns(j).start()

    @pl.when(section == 3)
    def _():
        load_c.start()

    @pl.when(not_attn)
    def _():
        load_rows(0).start()
        load_rows(1).start()

    barrier = pltpu.get_barrier_semaphore()

    def greet(s, d):
        pl.semaphore_signal(barrier, inc=1, device_id=(s, d), device_id_type=MESH)

    @pl.loop(0, n)
    def _(d):
        @pl.when(d != me)
        def _():
            greet(section, d)

        @pl.when((section == 1) | (section == 2))
        def _():
            greet(3 - section, d)

    greet(partner, me)
    greet(3 - partner, me)

    @pl.when((section == 0) | (section == 3))
    def _():
        greet(3 - section, me)

    def meet():
        edge = is_first + is_last
        pl.semaphore_wait(barrier, n + 1 + edge + (1 - edge) * n)

    bias_late[...] = hb_ref[...].astype(F32)
    send_bias = remote(bias_late, bias_early, hb_send.at[0], hb_recv.at[0], partner, me)
    span = half // 4
    step_rows = span // pieces

    def parts(z_side, which_core, k):
        first = which_core * span + k * step_rows
        in_block = pl.ds(pl.multiple_of(first, step_rows), step_rows)
        in_all = pl.ds(pl.multiple_of(z_side * width + first, step_rows), step_rows)
        return down_hbm.at[in_all], weights.at[4 + z_side, in_block]

    def down_first(k):
        source, here = parts(odd_place, core, k)
        return remote(source, here, w_send.at[0, k], w_recv.at[0, k], partner, me)

    def down_along(k):
        here = parts(odd_place, core, k)[1]
        return remote(here, here, w_send.at[1, k], w_recv.at[1, k], section, across_z)

    def down_pair(k):
        here = parts(odd_place, core, k)[1]
        return remote(here, here, w_send.at[2, k], w_recv.at[2, k], section, sibling)

    def down_last(k):
        here = parts(1 - odd_place, core, k)[1]
        return remote(here, here, w_send.at[3, k], w_recv.at[3, k], section, sibling)

    gain = gain_ref[...].astype(F32)
    shift = shift_ref[...].astype(F32)
    bias = bias_ref[...].astype(F32)
    small[...] = jnp.zeros_like(small)

    def role_of(table, micro, device):
        def step(r, found):
            return found + jnp.where(table[micro, r] == device, r, 0)

        return lax.fori_loop(0, n, step, 0)

    def make_tables(send_table, own_table):
        for m in range(2):

            @pl.loop(0, n)
            def _(d):
                spots[m, d] = lax.rem(role_of(send_table, m, d), across)

            family = lax.rem(lax.div(role_of(own_table, m, me), across), n // across)

            @pl.loop(0, across)
            def _(r):
                sources[m, r] = send_table[m, family * across + r]

    def send_blocks(c, rows, to_section, forward):
        blocks[...] = rows.reshape(blocks.shape)
        micro = lax.div(c, slots)
        slot = lax.rem(c, depth)

        @pl.when(c >= depth)
        def _():
            remote(
                xsend.at[slot], xsend.at[slot], x_send.at[c - depth], x_recv.at[0], to_section, me
            ).wait_send()

        @pl.loop(0, n)
        def _(d):
            spot = spots[micro, d]
            for g in range(repeat):
                block = g * across + spot if forward else spot * repeat + g
                xsend[slot, d, g] = blocks[block]

        for m in range(2):

            @pl.when(micro == m)
            def _():
                @pl.loop(0, n)
                def _(d):
                    remote(
                        xsend.at[slot, d],
                        xrecv[m].at[lax.rem(c, slots), me],
                        x_send.at[c],
                        x_recv.at[m],
                        to_section,
                        d,
                    ).start()

    def gather_blocks(c, target, from_section, forward):
        for m in range(2):

            @pl.when(c == m * slots)
            def _():
                remote(xrecv[m], xrecv[m], x_send.at[0], x_recv.at[m], from_section, me).wait_recv()
                @pl.loop(0, slots)
                def _(s):
                    group, inner = lax.div(s, repeat), lax.rem(s, repeat)

                    @pl.loop(0, across)
                    def _(r):
                        source = sources[m, r]
                        for f in range(repeat):
                            block = r * repeat + f if forward else f * across + r
                            rows = pl.ds(pl.multiple_of(block * BLOCK, BLOCK), BLOCK)
                            target[m * slots + s, rows] = xrecv[m][
                                group * repeat + f, source, inner
                            ]

    def norm_back(c, dn, gb):
        nh, inverse = normalise(hin[c].astype(F32))
        weighted = dn * gain
        first = jnp.mean(weighted, axis=-1, keepdims=True)
        second = jnp.mean(weighted * nh, axis=-1, keepdims=True)
        grad = gb.astype(F32) + inverse * (weighted - first - nh * second)
        small[0:1] += jnp.sum(dn * nh, axis=0, keepdims=True)
        small[1:2] += jnp.sum(dn, axis=0, keepdims=True)
        small[2:3] += jnp.sum(gb.astype(F32), axis=0, keepdims=True)
        return grad

    def ig_copy(s, c):
        return remote(gcol.at[s - 1, c], ig_ref.at[c], ig_send.at[s, c], ig_recv.at[0], s, me)

    @pl.when(is_attn)
    def _():
        @pl.when(section == 2)
        def _():
            make_tables(ftab, ttab)

        lane = lax.broadcasted_iota(jnp.int32, (1, 2 * HEAD_DIM), 1)
        first_head = jnp.where(lane < HEAD_DIM, 1.0, 0.0)
        pick = [first_head.astype(BF16), (1.0 - first_head).astype(BF16)]
        scale = HEAD_DIM ** (-0.5)
        pick_scaled = [
            (first_head * scale).astype(BF16),
            ((1.0 - first_head) * scale).astype(BF16),
        ]
        key_window = lax.broadcasted_iota(jnp.int32, (WINDOW, WINDOW), 0) % 16 // 4
        query_window = lax.broadcasted_iota(jnp.int32, (WINDOW, WINDOW), 1) % 16 // 4
        barred = jnp.where(key_window == query_window, 0.0, NEGATIVE)
        for m in range(2):
            mask_add[m] = barred * kind[m].astype(F32)

        def start_down():
            meet()

            @pl.loop(0, pieces)
            def _(k):
                down_first(k).start()

            send_bias.start()

        @pl.when(section == 2)
        def _():
            start_down()

        def forward(c):
            @pl.when(section == 2)
            def _():
                gather_blocks(c, hin, 1, True)

            @pl.when((section == 0) & (c == 0))
            def _():
                load_t.wait()

            micro = lax.div(c, slots)
            hidden = hin[c].astype(F32)
            nh, _ = normalise(hidden)
            normed = (nh * gain + shift).astype(BF16)
            nrm[c] = normed
            for j in range(3):
                columns = pl.ds(j * width, width)

                @pl.when(c == 0)
                def _():
                    load_columns(j).wait()

                keep_b[c, :, columns] = mm(normed, weights[j]).astype(BF16)

            @pl.when(c == 0)
            def _():
                load_columns(3).wait()

                @pl.when(section == 0)
                def _():
                    start_down()


            places_at = [g * 2 * HEAD_DIM for g in range(width // (2 * HEAD_DIM))]
            scores = []
            for offset in places_at:
                q = keep_b[c, :, pl.ds(offset, 2 * HEAD_DIM)]
                k = keep_b[c, :, pl.ds(width + offset, 2 * HEAD_DIM)]
                for one in range(2):
                    scores.append(mm_nt(k, q * pick_scaled[one]))
            probs = []
            for z in scores:
                z = z + mask_add[micro]
                e = jnp.exp(z - jnp.max(z, axis=0, keepdims=True))
                p = e * (1.0 / jnp.sum(e, axis=0, keepdims=True))
                probs.append(p.astype(BF16))
            for g, offset in enumerate(places_at):
                v = keep_b[c, :, pl.ds(2 * width + offset, 2 * HEAD_DIM)]
                o = None
                for one in range(2):
                    pb = probs[2 * g + one]
                    spot = (2 * g + one) * WINDOW
                    keep_a[c, :, pl.ds(spot, WINDOW)] = pb
                    term = mm_tn(pb, v * pick[one])
                    o = term if o is None else o + term
                keep_b[c, :, pl.ds(3 * width + offset, 2 * HEAD_DIM)] = o.astype(BF16)

            branch = mm(keep_b[c, :, pl.ds(3 * width, width)], weights[3])
            leave[c] = (hin[c].astype(F32) + branch + bias).astype(BF16)
            remote(
                leave.at[c], hin.at[c], h_send.at[c], h_recv.at[c], section + 1, me
            ).start()

        def backward(c):
            remote(gin.at[c], gin.at[c], g_send.at[c], g_recv.at[c], section + 1, me).wait_recv()
            remote(
                leave.at[c], hin.at[c], h_send.at[c], h_recv.at[c], section + 1, me
            ).wait_send()
            gb = gin[c]
            work[...] = mm_nt(gb, weights[3]).astype(BF16)

            places_at = [g * 2 * HEAD_DIM for g in range(width // (2 * HEAD_DIM))]
            grads = []
            for offset in places_at:
                v = keep_b[c, :, pl.ds(2 * width + offset, 2 * HEAD_DIM)]
                go = work[:, pl.ds(offset, 2 * HEAD_DIM)]
                for one in range(2):
                    grads.append(mm_nt(v, go * pick[one]))
            for g, offset in enumerate(places_at):
                q_at = pl.ds(offset, 2 * HEAD_DIM)
                k_at = pl.ds(width + offset, 2 * HEAD_DIM)
                v_at = pl.ds(2 * width + offset, 2 * HEAD_DIM)
                q, k, go = keep_b[c, :, q_at], keep_b[c, :, k_at], work[:, q_at]
                dq = dk = dv = None
                for one in range(2):
                    spot = (2 * g + one) * WINDOW
                    pb = keep_a[c, :, pl.ds(spot, WINDOW)]
                    p = pb.astype(F32)
                    pdp = p * grads[2 * g + one]
                    ds = (pdp - p * jnp.sum(pdp, axis=0, keepdims=True)).astype(BF16)
                    tv = mm(pb, go * pick[one])
                    tk = mm(ds, q * pick_scaled[one])
                    tq = mm_tn(ds, k * pick_scaled[one])
                    dv = tv if dv is None else dv + tv
                    dk = tk if dk is None else dk + tk
                    dq = tq if dq is None else dq + tq
                keep_b[c, :, q_at] = dq.astype(BF16)
                keep_b[c, :, k_at] = dk.astype(BF16)
                keep_b[c, :, v_at] = dv.astype(BF16)

            dn = sum(mm_nt(keep_b[c, :, pl.ds(j * width, width)], weights[j]) for j in range(3))
            leaving = norm_back(c, dn, gb).astype(BF16)

            @pl.when(section == 2)
            def _():
                send_blocks(c, leaving, 1, False)

            @pl.when(section == 0)
            def _():
                for s in range(1, SECTIONS):
                    gcol[s - 1, c] = leaving[:, s * quarter : (s + 1) * quarter]
                ig_ref[c] = leaving[:, 0:quarter]
                for s in range(1, SECTIONS):
                    ig_copy(s, c).start()

        @pl.loop(0, 2 * chunks)
        def _(step):
            c = lax.rem(step, chunks)

            @pl.when(step < chunks)
            def _():
                forward(c)

            @pl.when(step >= chunks)
            def _():
                backward(c)

    @pl.when(not_attn)
    def _():
        meet()

        @pl.when(section == 1)
        def _():
            make_tables(ttab, ftab)

        for j in range(4):
            load_columns(j).wait()

        load_rows(0).wait()
        load_rows(1).wait()

        @pl.loop(0, pieces)
        def _(k):
            down_first(k).wait_recv()
            down_along(k).start()
            down_pair(k).start()

        @pl.loop(0, pieces)
        def _(k):
            down_along(k).wait_recv()
            down_last(k).start()

        send_bias.wait_recv()

        @pl.when(section == 3)
        def _():
            load_c.wait()

        def forward(c):
            remote(hin.at[c], hin.at[c], h_send.at[c], h_recv.at[c], section - 1, me).wait_recv()
            hidden = hin[c].astype(F32)
            nh, _ = normalise(hidden)
            normed = (nh * gain + shift).astype(BF16)
            nrm[c] = normed
            for j in range(4):
                columns = pl.ds(j * width, width)
                u = mm(normed, weights[j])
                u = u + (bias_early, bias_late)[j // 2][:, pl.ds((j % 2) * width, width)]
                active, slope = gelu_and_slope(u)
                keep_a[c, :, columns] = active.astype(BF16)
                keep_b[c, :, columns] = slope.astype(BF16)

            @pl.when(c == 0)
            def _():
                @pl.loop(0, pieces)
                def _(k):
                    down_pair(k).wait_recv()
                    down_last(k).wait_recv()

            branch = mm(keep_a[c], weights[pl.ds(4, 4)].reshape(wide, width))
            leaving = (hin[c].astype(F32) + branch + bias).astype(BF16)

            @pl.when(section == 1)
            def _():
                send_blocks(c, leaving, 2, True)

            @pl.when(section == 3)
            def _():
                for s in range(SECTIONS - 1):
                    gcol[s, c] = leaving[:, s * quarter : (s + 1) * quarter]
                out_ref[c] = leaving[:, (SECTIONS - 1) * quarter :]
                for s in range(SECTIONS - 1):
                    remote(
                        gcol.at[s, c], out_ref.at[c], o_send.at[s, c], o_recv.at[0], s, me
                    ).start()

        def backward(c):
            @pl.when(section == 1)
            def _():
                gather_blocks(c, gin, 2, False)

            gb = gin[c]
            for j in range(4):
                columns = pl.ds(j * width, width)
                da = mm_nt(gb, weights[4 + j])
                du = da * keep_b[c, :, columns].astype(F32)
                keep_b[c, :, columns] = du.astype(BF16)
                small[3 + j : 4 + j] += jnp.sum(du, axis=0, keepdims=True)
            dn = sum(mm_nt(keep_b[c, :, pl.ds(j * width, width)], weights[j]) for j in range(4))
            leave[c] = norm_back(c, dn, gb).astype(BF16)
            remote(
                leave.at[c], gin.at[c], g_send.at[c], g_recv.at[c], section - 1, me
            ).start()
        @pl.loop(0, 2 * chunks)
        def _(step):
            last = lax.div(section, 2)
            c = last * lax.div(step, 2) + (1 - last) * lax.rem(step, chunks)
            back = last * lax.rem(step, 2) + (1 - last) * lax.div(step, chunks)

            @pl.when(back == 0)
            def _():
                forward(c)

            @pl.when(back == 1)
            def _():
                backward(c)

    @pl.when(not_attn)
    def _():
        @pl.loop(0, pieces)
        def _(k):
            down_along(k).wait_send()
            down_pair(k).wait_send()
            down_last(k).wait_send()

    side = width // 2
    per_block = side // chunk
    w_chunks, d_chunks = 4 * per_block, 2 * per_block
    rows_all = chunks * WINDOW

    def grad_rows(block, first, count):
        return weights.at[block, pl.ds(pl.multiple_of(first, count), count)]

    def half_rows(block):
        return pl.ds(pl.multiple_of(block * side, side), side)

    def block_of(turn):
        last = turn + 2 * lax.div(turn, 4) - 4 * lax.div(turn, 6)
        first = turn + 3 * lax.div(turn + 7, 8) - 5 * lax.div(turn + 5, 8) + 2 * lax.div(turn, 6)
        second = odd - is_last
        return second * first + (1 - second) * last

    def sib_copy(block, source):
        return remote(
            source, theirs.at[half_rows(block)], sib_send.at[block], sib_recv.at[block], section, sibling
        )

    def outer(left, left_at, right, right_at, block):
        right_value = right[:, :, right_at].reshape(rows_all, width)

        @pl.loop(0, width // WINDOW)
        def _(k):
            columns = pl.ds(pl.multiple_of(left_at + k * WINDOW, WINDOW), WINDOW)
            left_value = left[:, :, columns].reshape(rows_all, WINDOW)
            rows = pl.ds(pl.multiple_of(k * WINDOW, WINDOW), WINDOW)
            weights[block, rows] = mm_tn(left_value, right_value).astype(BF16)

    def grad_block(turn):
        block = block_of(turn)

        @pl.when((block < 4) & (not_attn | (block < 3)))
        def _():
            columns = pl.ds(pl.multiple_of(block * width, width), width)
            outer(nrm, 0, keep_b, columns, block)

        @pl.when((block == 3) & is_attn)
        def _():
            outer(keep_b, 3 * width, gin, pl.ds(0, width), block)

        @pl.when(block >= 4)
        def _():
            outer(keep_a, (block - 4) * width, gin, pl.ds(0, width), block)

        sib_copy(block, grad_rows(block, (1 - core) * side, side)).start()

    def early_copy(block, source):
        send, recv = early_send.at[block - 4], early_recv.at[block - 4]
        return (
            remote(source, grad_rows(block, core * side, side), send, recv, 2, me),
            remote(source, guest.at[half_rows(block - 4)], send, recv, 3, me),
        )

    def pair_sum(turn):
        block = block_of(turn)
        sib_copy(block, theirs.at[half_rows(block)]).wait_recv()

        here = grad_rows(block, core * side, side)
        value = here[...].astype(F32) + theirs[half_rows(block)].astype(F32)
        here[...] = value.astype(BF16)

        @pl.when((block == 4) | (block == 5))
        def _():
            to_two, to_three = early_copy(block, here)

            @pl.when(section == 3)
            def _():
                to_two.start()

            @pl.when(section == 1)
            def _():
                to_three.start()

    small_all[me] = small[...]

    def small_copy(d):
        return remote(small, small_all.at[me], small_send.at[d], small_recv.at[0], section, d)

    @pl.loop(0, n)
    def _(d):
        @pl.when(d != me)
        def _():
            small_copy(d).start()

    own_lines = w_chunks + d_chunks
    lines = own_lines + d_chunks * (is_last - is_first)

    def line_rows(i):
        return pl.ds(pl.multiple_of(i * chunk, chunk), chunk)

    def with_chunk(i, use):
        slot = lax.div(i, per_block)
        first = core * side + lax.rem(i, per_block) * chunk

        @pl.when(i < own_lines)
        def _():
            block = slot + 2 * odd * lax.div(slot, 4)
            use(grad_rows(block, first, chunk))

        @pl.when(i >= own_lines)
        def _():
            use(guest.at[pl.ds(pl.multiple_of((i - own_lines) * chunk, chunk), chunk)])

    def total_rows(i):
        first = core * side + lax.rem(i, per_block) * chunk
        return total_hbm.at[lax.div(i, per_block), pl.ds(pl.multiple_of(first, chunk), chunk)]

    def low_rows(i):
        return from_low.at[line_rows(i)]

    def high_rows(i):
        return from_high.at[line_rows(i)]

    def up_copy(i, source):
        return remote(source, low_rows(i), up_send.at[i], low_recv.at[i], section, me + 2)

    def down_copy(i, source):
        return remote(source, high_rows(i), down_send.at[i], high_recv.at[i], section, me - 2)

    def left_copy(i, source, target):
        return remote(source, target, left_send.at[i], total_recv.at[i], section, me - 2)

    def right_copy(i, source, target):
        return remote(source, target, right_send.at[i], total_recv.at[i], section, me + 2)

    def pair_copy(i, source):
        return remote(source, total_rows(i), pair_send.at[i], pair_recv.at[0], section, sibling)

    def own_copy(i, source):
        return pltpu.make_async_copy(source, total_rows(i), local_sem.at[i])

    def guest_copy(k, source):
        return remote(
            source, total_rows(w_chunks + k), guest_send.at[k], guest_recv.at[k], 0, me
        )

    def reduce_stage(i, root):
        def run(here):
            acc[...] = here[...].astype(F32)

            @pl.when((place <= root) & (place > 0))
            def _():
                up_copy(i, here).wait_recv()
                acc[...] += from_low[line_rows(i)].astype(F32)

            @pl.when((place >= root) & (place < places - 1))
            def _():
                down_copy(i, here).wait_recv()
                acc[...] += from_high[line_rows(i)].astype(F32)

            here[...] = acc[...].astype(BF16)

            @pl.when(place < root)
            def _():
                up_copy(i, here).start()

            @pl.when(place > root)
            def _():
                down_copy(i, here).start()

            @pl.when((place == root) & (i < own_lines))
            def _():
                @pl.when(place > 0)
                def _():
                    left_copy(i, here, total_rows(i)).start()

                @pl.when(place < places - 1)
                def _():
                    right_copy(i, here, total_rows(i)).start()

                pair_copy(i, here).start()
                own_copy(i, here).start()

            @pl.when((place == root) & (i >= own_lines))
            def _():
                @pl.when(place > 0)
                def _():
                    left_copy(i, here, high_rows(i)).start()

                @pl.when(place < places - 1)
                def _():
                    right_copy(i, here, low_rows(i)).start()

                guest_copy(i - own_lines, here).start()

        with_chunk(i, run)

    def pass_on(i, root, left_at, right_at, finish):
        @pl.when(place < root)
        def _():
            left_copy(i, left_at, left_at).wait_recv()

            @pl.when(place > 0)
            def _():
                left_copy(i, left_at, left_at).start()

            finish(left_at)

        @pl.when(place > root)
        def _():
            right_copy(i, right_at, right_at).wait_recv()

            @pl.when(place < places - 1)
            def _():
                right_copy(i, right_at, right_at).start()

            finish(right_at)

    def spread_stage(i, root):
        @pl.when(i < own_lines)
        def _():
            at = total_rows(i)
            pass_on(i, root, at, at, lambda ref: pair_copy(i, ref).start())

        @pl.when(i >= own_lines)
        def _():
            pass_on(
                i,
                root,
                high_rows(i),
                low_rows(i),
                lambda ref: guest_copy(i - own_lines, ref).start(),
            )

    height = places // 2
    pairs = lax.div(lines, 2)
    turns = 4 + 4 * odd

    @pl.loop(0, 1 + pairs + 2 * height * lag)
    def _(step):
        for at in range(2):
            turn = 2 * step - 1 + at

            @pl.when((turn >= 0) & (turn < turns))
            def _():
                grad_block(turn)

        for at in range(2):
            turn = 2 * step - 3 + at

            @pl.when((turn >= 0) & (turn < turns))
            def _():
                pair_sum(turn)

        for at in range(2):
            half_block = half_rows(at)
            arrived = early_copy(4 + at, theirs.at[half_block])[0]

            @pl.when((section == 2) & (step == 1 + (4 + at) * per_block // 2))
            def _():
                arrived.wait_recv()

            @pl.when((section == 3) & (step == 1 + (6 + at) * per_block // 2))
            def _():
                arrived.wait_recv()

        for stream in range(2):
            root = height - 1 + stream
            now = step - 1 - lag * (height - jnp.abs(place - root))

            @pl.when((now >= 0) & (now < pairs))
            def _():
                reduce_stage(2 * now + stream, root)

        for stream in range(2):
            root = height - 1 + stream
            past = step - 1 - lag * (height + jnp.abs(place - root))

            @pl.when((past >= 0) & (past < pairs))
            def _():
                spread_stage(2 * past + stream, root)

    @pl.when(section == 0)
    def _():
        @pl.loop(0, d_chunks)
        def _(k):
            here = total_rows(w_chunks + k)
            guest_copy(k, here).wait_recv()
            pair_copy(w_chunks + k, here).start()

    remote(
        small_all.at[pl.ds(0, n - 1)],
        small_all.at[pl.ds(0, n - 1)],
        small_send.at[0],
        small_recv.at[0],
        section,
        sibling,
    ).wait_recv()

    def add(d, so_far):
        return so_far + small_all[d]

    small_out[...] = lax.fori_loop(1, n, add, small_all[0])
    to_pair = remote(small_out, small_pair, spair_send.at[0], spair_recv.at[0], partner, me)

    @pl.when(not_attn)
    def _():
        to_pair.start()
        to_pair.wait_send()

    @pl.when(is_attn)
    def _():
        to_pair.wait_recv()
        small_out[5:7] = small_pair[3:5]

    @pl.loop(0, lines)
    def _(i):
        some = low_rows(i)

        for stream in range(2):
            root = height - 1 + stream

            @pl.when(lax.rem(i, 2) == stream)
            def _():
                @pl.when(place < root)
                def _():
                    up_copy(i, some).wait_send()

                @pl.when(place > root)
                def _():
                    down_copy(i, some).wait_send()

                @pl.when((place <= root) & (place > 0))
                def _():
                    left_copy(i, some, some).wait_send()

                @pl.when((place >= root) & (place < places - 1))
                def _():
                    right_copy(i, some, some).wait_send()

                @pl.when((place == root) & (i < own_lines))
                def _():
                    own_copy(i, some).wait()

        @pl.when(i < own_lines)
        def _():
            pair_copy(i, some).wait_send()

        @pl.when(i >= own_lines)
        def _():
            guest_copy(i - own_lines, some).wait_send()

    @pl.when(section == 0)
    def _():
        @pl.loop(w_chunks, own_lines)
        def _(i):
            pair_copy(i, low_rows(i)).wait_send()

    @pl.loop(0, turns)
    def _(turn):
        block = block_of(turn)
        sib_copy(block, theirs.at[half_rows(block)]).wait_send()

    @pl.loop(0, n)
    def _(d):
        @pl.when(d != me)
        def _():
            small_copy(d).wait_send()

    @pl.when(is_attn)
    def _():
        @pl.loop(0, pieces)
        def _(k):
            down_first(k).wait_send()

        send_bias.wait_send()

    @pl.when(not_attn)
    def _():
        for at in range(2):
            early_copy(4 + at, theirs.at[half_rows(at)])[0].wait_send()

        @pl.loop(0, chunks)
        def _(c):
            remote(
                leave.at[c], gin.at[c], g_send.at[c], g_recv.at[c], section - 1, me
            ).wait_send()

    @pl.when((section == 1) | (section == 2))
    def _():
        @pl.loop(chunks - depth, chunks)
        def _(c):
            slot = lax.rem(c, depth)
            remote(
                xsend.at[slot], xsend.at[slot], x_send.at[c], x_recv.at[0], 3 - section, me
            ).wait_send()

    @pl.when(section == 3)
    def _():
        @pl.loop(0, chunks)
        def _(c):
            for s in range(SECTIONS - 1):
                remote(
                    gcol.at[s, c], out_ref.at[c], o_send.at[s, c], o_recv.at[0], s, me
                ).wait_send()

    @pl.when(section != 3)
    def _():
        remote(out_ref, out_ref, o_send.at[0, 0], o_recv.at[0], 3, me).wait_recv()

    @pl.when(section == 0)
    def _():
        @pl.loop(0, chunks)
        def _(c):
            for s in range(1, SECTIONS):
                ig_copy(s, c).wait_send()

    @pl.when(section != 0)
    def _():
        remote(ig_ref, ig_ref, ig_send.at[0, 0], ig_recv.at[0], 0, me).wait_recv()

    remote(
        total_hbm.at[pl.ds(0, 3)],
        total_hbm.at[pl.ds(0, 3)],
        pair_send.at[0],
        pair_recv.at[0],
        section,
        sibling,
    ).wait_recv()


def pipeline(
    tokens, cotangent, gain, shift, weight, bias, down, hidden_bias, ftab, ttab, kind, chunk=96, lag=1
):
    micro, rows, width = tokens.shape
    wide = weight.shape[1]
    n = lax.axis_size("dp")
    across = min(n, 16)
    repeat = 16 // across
    slots = rows // WINDOW
    chunks = micro * slots
    quarter = width // SECTIONS
    depth = chunks if n <= 8 else 1
    pieces = 4
    cfg = (n, across, repeat, slots, chunks, width, wide, depth, chunk, lag, pieces)
    vmem = pl.BlockSpec(memory_space=pltpu.VMEM)
    smem = pl.BlockSpec(memory_space=pltpu.SMEM)
    anywhere = pl.BlockSpec(memory_space=pl.ANY)
    dma = pltpu.SemaphoreType.DMA
    chunked = (chunks, WINDOW, width)
    side = width // 2
    lines = 8 * side // chunk
    per_chunk = [dma((lines,)) for _ in range(8)]
    return pl.pallas_call(
        functools.partial(main_kernel, cfg),
        out_shape=(
            jax.ShapeDtypeStruct((chunks, WINDOW, quarter), BF16),
            jax.ShapeDtypeStruct((chunks, WINDOW, quarter), BF16),
            jax.ShapeDtypeStruct((6, width, width), BF16),
            jax.ShapeDtypeStruct((8, width), F32),
        ),
        in_specs=[anywhere, anywhere, vmem, vmem, anywhere, vmem, anywhere, vmem, smem, smem, smem],
        out_specs=(vmem, vmem, anywhere, vmem),
        scratch_shapes=[
            pltpu.VMEM((8, width, width), BF16),
            pltpu.VMEM((chunks, WINDOW, wide), BF16),
            pltpu.VMEM((chunks, WINDOW, wide), BF16),
            pltpu.VMEM(chunked, BF16),
            pltpu.VMEM(chunked, BF16),
            pltpu.VMEM(chunked, BF16),
            pltpu.VMEM(chunked, BF16),
            pltpu.VMEM((WINDOW, width), BF16),
            pltpu.VMEM((SECTIONS - 1, chunks, WINDOW, quarter), BF16),
            pltpu.VMEM((depth, n, repeat, BLOCK, width), BF16),
            pltpu.VMEM((slots, n, repeat, BLOCK, width), BF16),
            pltpu.VMEM((slots, n, repeat, BLOCK, width), BF16),
            pltpu.VMEM((WINDOW // BLOCK, BLOCK, width), BF16),
            pltpu.VMEM((1, wide // 2), F32),
            pltpu.VMEM((1, wide // 2), F32),
            pltpu.VMEM((2, WINDOW, WINDOW), F32),
            pltpu.SMEM((2, n), jnp.int32),
            pltpu.SMEM((2, across), jnp.int32),
            pltpu.VMEM((2 * side, width), BF16),
            pltpu.VMEM((8 * side, width), BF16),
            pltpu.VMEM((lines * chunk, width), BF16),
            pltpu.VMEM((lines * chunk, width), BF16),
            pltpu.VMEM((chunk, width), F32),
            pltpu.VMEM((8, width), F32),
            pltpu.VMEM((n, 8, width), F32),
            pltpu.VMEM((8, width), F32),
            dma((8,)),
            dma((4, pieces)),
            dma((4, pieces)),
            dma((1,)),
            dma((1,)),
            dma((chunks,)),
            dma((chunks,)),
            dma((chunks,)),
            dma((chunks,)),
            dma((chunks,)),
            dma((micro,)),
            dma((SECTIONS - 1, chunks)),
            dma((1,)),
            dma((SECTIONS, chunks)),
            dma((1,)),
            dma((8,)),
            dma((8,)),
            *per_chunk,
            dma((1,)),
            dma((lines,)),
            dma((2,)),
            dma((2,)),
            dma((lines // 4,)),
            dma((lines // 4,)),
            dma((n,)),
            dma((1,)),
            dma((1,)),
            dma((1,)),
        ],
        compiler_params=pltpu.CompilerParams(
            collective_id=0, has_side_effects=True, vmem_limit_bytes=63 * 1024 * 1024
        ),
        name="pipeline",
    )(
        tokens.reshape(chunked),
        cotangent.reshape(chunked),
        gain,
        shift,
        weight,
        bias,
        down,
        hidden_bias.reshape(1, -1),
        ftab,
        ttab,
        kind,
    )


def finish_kernel(
    total_ref,
    small_ref,
    ig_ref,
    out_ref,
    output,
    input_grad,
    gain,
    shift,
    weight,
    bias,
    down,
    hidden,
):
    block, row = pl.program_id(0), pl.program_id(1)

    @pl.when((block == 0) & (row == 0))
    def _():
        output[...] = out_ref[...]
        input_grad[...] = ig_ref[...].astype(F32)
        gain[...] = small_ref[0:1]
        shift[...] = small_ref[1:2]
        bias[...] = small_ref[2:3]
        hidden[...] = small_ref[5:7]

    is_down = block >= 4

    @pl.when(jnp.logical_not(is_down))
    def _():
        weight[...] = total_ref[0].astype(F32)

    @pl.when(is_down)
    def _():
        down[...] = total_ref[0].astype(F32)


def finish(total, small, input_grad, output):
    width = total.shape[-1]
    steps = 2
    span = width // steps

    def whole(array):
        return pl.BlockSpec(array.shape, lambda b, r, k=array.ndim: (0,) * k)

    def weight_at(b, r):
        return jnp.where(b < 4, r, steps - 1), jnp.minimum(b, 3)

    def down_at(b, r):
        return jnp.where(b < 4, 0, (b - 4) * steps + r), 0

    row = jax.ShapeDtypeStruct((1, width), F32)
    pair = jax.ShapeDtypeStruct((2, width), F32)
    wide_grad = jax.ShapeDtypeStruct(input_grad.shape, F32)
    return pl.pallas_call(
        finish_kernel,
        grid=(6, steps),
        out_shape=(
            output,
            wide_grad,
            row,
            row,
            jax.ShapeDtypeStruct((width, SECTIONS * width), F32),
            row,
            jax.ShapeDtypeStruct((2 * width, width), F32),
            pair,
        ),
        in_specs=[
            pl.BlockSpec((1, span, width), lambda b, r: (b, r, 0)),
            whole(small),
            whole(input_grad),
            whole(output),
        ],
        out_specs=(
            whole(output),
            whole(wide_grad),
            whole(row),
            whole(row),
            pl.BlockSpec((span, width), weight_at),
            whole(row),
            pl.BlockSpec((span, width), down_at),
            whole(pair),
        ),
        compiler_params=pltpu.CompilerParams(vmem_limit_bytes=32 * 1024 * 1024),
        name="finish",
    )(total, small, input_grad, output)


def on_device(
    tokens,
    cotangent,
    norm_gain,
    norm_shift,
    in_weight,
    out_bias,
    down_weight,
    hidden_bias,
    frame_device,
    tube_device,
    clip_kind,
):
    micro, rows, width = tokens.shape
    output, input_grad, total, small_total = pipeline(
        tokens,
        cotangent,
        norm_gain,
        norm_shift,
        in_weight[0],
        out_bias,
        down_weight,
        hidden_bias,
        frame_device,
        tube_device,
        clip_kind,
    )
    output, input_grad, gain, shift, weight, bias, down, hidden = finish(
        total, small_total, input_grad, output
    )
    quarter = width // SECTIONS
    return (
        output.reshape(micro, rows, quarter),
        input_grad.reshape(micro, rows, quarter),
        gain,
        shift,
        weight[None],
        bias,
        down,
        hidden.reshape(-1),
    )


def solution(mesh):
    return jax.shard_map(
        on_device,
        mesh=mesh,
        in_specs=(
            P(None, "dp", None),
            P(None, "dp", None),
            P("section", None),
            P("section", None),
            P("section", None, None),
            P("section", None),
            P("section", None),
            P("section"),
            P(),
            P(),
            P(),
        ),
        out_specs=(
            P(None, "dp", "section"),
            P(None, "dp", "section"),
            P("section", None),
            P("section", None),
            P("section", None, None),
            P("section", None),
            P("section", None),
            P("section"),
        ),
        check_vma=False,
    )
```

time: 320 us -> 281 us (0.88)
  Pallas kernels: 313 us -> 270 us
  local copies, waits for them, and re-layouts: 6.35 us -> 9.85 us
    pallas_call x1 -> x0, Pallas kernels: 102 us -> none  [reduction(): pl.pallas_call(functools.partial(reduce_kernel, cfg), out_shape=(jax.Shap...]
    pallas_call x1, Pallas kernels: 203 us -> 262 us  [pipeline(): pl.pallas_call(functools.partial(main_kernel, cfg), out_shape=(jax.ShapeD...]
    unnamed x8 -> x10, local copies, waits for them, and re-layouts: 4.46 us -> 7.96 us
where the time goes in v3:
time: 281 us; the launch traced here: 280 us
  Pallas kernels  270 us (96%)
  local copies, waits for them, and re-layouts  9.85 us (4%)
    pallas_call x1, Pallas kernels, pipeline(): pl.pallas_call(functools.partial(main_kernel, cfg), out_shape=(jax.ShapeD...  262 us
    unnamed x10, local copies, waits for them, and re-layouts  7.96 us
    pallas_call x1, Pallas kernels, finish(): pl.pallas_call(finish_kernel, grid=(6, steps), out_shape=(output, wide_gr...  7.48 us

profile of v3, /device:TPU:0, one launch (start us, length us, event | category | flops | bytes accessed | tf_op | source)
XLA Modules:
  0.0 280.2 jit_solution(16996458595855521285)
XLA Ops:
  0.6 1.3 reshape.36.hb_ref
  1.9 262.2 %pipeline.1 = (bf16[4,256,192]{2,1,0:T(8,128)(2,1)}, bf16[4,256,192]{2,1,0:T(8,128)(2,1)}, bf16[6,768,768]{2,1,0:T(8,128)(2,1)}, f32[8,768]{1,0:T(8,128)}) custom-call(bf16[4,256,768]{2,1,0:T(8,128)(2,1)} %bitcast.9, bf16[4,256,768]{2,1,0:T(8,128)(2,1)} %bitcast.10, bf16[1,768]{1,0:T(2,128)(2,1)} %gain_ref.1, bf16[1,768]{1,0:T(2,128)(2,1)} %shift_ref.1, ...), custom_call_target="tpu_custom_call" | custom-call | tf_op jit(solution)/shard_map/pipeline/pallas_call | solution.py:1039
  264.1 0.0 copy-start
  264.1 3.0 %copy-done = bf16[6,768,768]{2,1,0:T(8,128)(2,1)S(1)} copy-done((bf16[6,768,768]{2,1,0:T(8,128)(2,1)S(1)}, bf16[6,768,768]{2,1,0:T(8,128)(2,1)}, u32[]{:S(2)}) %copy-start) | copy-done | bytes 7077912
  267.1 0.0 copy-start.1
  267.1 1.0 copy-done.1
  268.2 0.0 copy-start.2
  268.2 1.0 copy-done.2
  269.2 0.0 copy-start.3
  269.2 0.7 copy-done.3
  270.0 7.5 %finish.1 = (bf16[4,256,192]{2,1,0:T(8,128)(2,1)S(1)}, f32[4,256,192]{2,1,0:T(8,128)S(1)}, f32[1,768]{1,0:T(1,128)}, f32[1,768]{1,0:T(1,128)}, f32[768,3072]{1,0...) custom-call(bf16[6,768,768]{2,1,0:T(8,128)(2,1)S(1)} %copy-done, f32[8,768]{1,0:T(8,128)S(1)} %copy-done.3, ...), custom_call_target="tpu_custom_call" | custom-call | tf_op jit(solution)/shard_map/finish/pallas_call | solution.py:1177
  277.4 0.9 copy.19
  278.4 1.2 copy.20
  279.6 0.6 reshape.39
Async XLA Ops:
  264.1 3.0 %copy-start = (bf16[6,768,768]{2,1,0:T(8,128)(2,1)S(1)}, bf16[6,768,768]{2,1,0:T(8,128)(2,1)}, u32[]{:S(2)}) copy-start(bf16[6,768,768]{2,1,0:T(8,128)(2,1)} %get-tuple-element.20.total_ref) | copy-start | bytes 21233668
  267.1 1.0 copy-start.1
  268.2 1.0 copy-start.2
  269.2 0.7 copy-start.3

commit v4 on v3

--- a/solution.py
+++ b/solution.py
@@ -83,6 +83,8 @@
     xsend,
     xrecv0,
     xrecv1,
+    xrecv2,
+    xrecv3,
     blocks,
     bias_early,
     bias_late,
@@ -147,7 +149,8 @@
     not_attn = odd == 1
     partner = section + 1 - 2 * odd
     is_first, is_last = lax.div(3 - section, 3), lax.div(section, 3)
-    xrecv = (xrecv0, xrecv1)
+    xrecv = (xrecv0, xrecv1, xrecv2, xrecv3)
+    share = WINDOW // repeat
     half = wide // 2
     quarter = width // SECTIONS
 
@@ -204,7 +207,7 @@
         edge = is_first + is_last
         pl.semaphore_wait(barrier, n + 1 + edge + (1 - edge) * n)
 
-    bias_late[...] = hb_ref[...].astype(F32)
+    bias_late[...] = hb_ref[...].astype(F32).reshape(bias_late.shape)
     send_bias = remote(bias_late, bias_early, hb_send.at[0], hb_recv.at[0], partner, me)
     span = half // 4
     step_rows = span // pieces
@@ -254,6 +257,39 @@
             @pl.loop(0, across)
             def _(r):
                 sources[m, r] = send_table[m, family * across + r]
+
+    def slot_of(unit, f):
+        return lax.div(unit, repeat) * repeat + f
+
+    def share_rows(k):
+        return pl.ds(pl.multiple_of(k * share, share), share)
+
+    def unit_copy(k):
+        unit, f = lax.div(k, repeat), lax.rem(k, repeat)
+        return remote(
+            leave.at[slot_of(unit, f), share_rows(lax.rem(unit, repeat))],
+            hin.at[unit, share_rows(f)],
+            h_send.at[k],
+            h_recv.at[unit],
+            1,
+            me,
+        )
+
+    def unit_back(unit, f):
+        return remote(
+            leave.at[unit, share_rows(f)],
+            gin.at[slot_of(unit, f), share_rows(lax.rem(unit, repeat))],
+            g_send.at[unit, f],
+            g_recv.at[slot_of(unit, f)],
+            0,
+            me,
+        )
+
+    def slot_copy(c):
+        return remote(leave.at[c], hin.at[c], h_send.at[c], h_recv.at[c], 3, me)
+
+    def slot_back(c):
+        return remote(leave.at[c], gin.at[c], g_send.at[c, 0], g_recv.at[c], 2, me)
 
     def send_blocks(c, rows, to_section, forward):
         blocks[...] = rows.reshape(blocks.shape)
@@ -273,40 +309,35 @@
                 block = g * across + spot if forward else spot * repeat + g
                 xsend[slot, d, g] = blocks[block]
 
-        for m in range(2):
-
-            @pl.when(micro == m)
+        for i in range(chunks):
+
+            @pl.when(c == i)
             def _():
                 @pl.loop(0, n)
                 def _(d):
                     remote(
                         xsend.at[slot, d],
-                        xrecv[m].at[lax.rem(c, slots), me],
+                        xrecv[i].at[me],
                         x_send.at[c],
-                        x_recv.at[m],
+                        x_recv.at[i],
                         to_section,
                         d,
                     ).start()
 
     def gather_blocks(c, target, from_section, forward):
-        for m in range(2):
-
-            @pl.when(c == m * slots)
-            def _():
-                remote(xrecv[m], xrecv[m], x_send.at[0], x_recv.at[m], from_section, me).wait_recv()
-                @pl.loop(0, slots)
-                def _(s):
-                    group, inner = lax.div(s, repeat), lax.rem(s, repeat)
-
-                    @pl.loop(0, across)
-                    def _(r):
-                        source = sources[m, r]
-                        for f in range(repeat):
-                            block = r * repeat + f if forward else f * across + r
-                            rows = pl.ds(pl.multiple_of(block * BLOCK, BLOCK), BLOCK)
-                            target[m * slots + s, rows] = xrecv[m][
-                                group * repeat + f, source, inner
-                            ]
+        for i in range(chunks):
+
+            @pl.when(c == i)
+            def _():
+                remote(xrecv[i], xrecv[i], x_send.at[0], x_recv.at[i], from_section, me).wait_recv()
+
+                @pl.loop(0, across)
+                def _(r):
+                    source = sources[i // slots, r]
+                    for f in range(repeat):
+                        block = r * repeat + f if forward else f * across + r
+                        rows = pl.ds(pl.multiple_of(block * BLOCK, BLOCK), BLOCK)
+                        target[i, rows] = xrecv[i][source, f]
 
     def norm_back(c, dn, gb):
         nh, inverse = normalise(hin[c].astype(F32))
@@ -324,10 +355,6 @@
 
     @pl.when(is_attn)
     def _():
-        @pl.when(section == 2)
-        def _():
-            make_tables(ftab, ttab)
-
         lane = lax.broadcasted_iota(jnp.int32, (1, 2 * HEAD_DIM), 1)
         first_head = jnp.where(lane < HEAD_DIM, 1.0, 0.0)
         pick = [first_head.astype(BF16), (1.0 - first_head).astype(BF16)]
@@ -342,18 +369,17 @@
         for m in range(2):
             mask_add[m] = barred * kind[m].astype(F32)
 
-        def start_down():
-            meet()
-
-            @pl.loop(0, pieces)
-            def _(k):
-                down_first(k).start()
-
-            send_bias.start()
+        meet()
+
+        @pl.loop(0, pieces)
+        def _(k):
+            down_first(k).start()
+
+        send_bias.start()
 
         @pl.when(section == 2)
         def _():
-            start_down()
+            make_tables(ftab, ttab)
 
         def forward(c):
             @pl.when(section == 2)
@@ -381,10 +407,6 @@
             @pl.when(c == 0)
             def _():
                 load_columns(3).wait()
-
-                @pl.when(section == 0)
-                def _():
-                    start_down()
 
 
             places_at = [g * 2 * HEAD_DIM for g in range(width // (2 * HEAD_DIM))]
@@ -413,15 +435,24 @@
 
             branch = mm(keep_b[c, :, pl.ds(3 * width, width)], weights[3])
             leave[c] = (hin[c].astype(F32) + branch + bias).astype(BF16)
-            remote(
-                leave.at[c], hin.at[c], h_send.at[c], h_recv.at[c], section + 1, me
-            ).start()
+
+            @pl.when(section == 2)
+            def _():
+                slot_copy(c).start()
+
+            @pl.when(section == 0)
+            def _():
+                unit_copy(c).start()
+
+            @pl.when((section == 0) & (c == chunks - 1))
+            def _():
+                @pl.loop(chunks, chunks * repeat)
+                def _(k):
+                    unit_copy(k - 2).wait_send()
+                    unit_copy(k).start()
 
         def backward(c):
-            remote(gin.at[c], gin.at[c], g_send.at[c], g_recv.at[c], section + 1, me).wait_recv()
-            remote(
-                leave.at[c], hin.at[c], h_send.at[c], h_recv.at[c], section + 1, me
-            ).wait_send()
+            slot_back(c).wait_recv()
             gb = gin[c]
             work[...] = mm_nt(gb, weights[3]).astype(BF16)
 
@@ -513,7 +544,7 @@
             load_c.wait()
 
         def forward(c):
-            remote(hin.at[c], hin.at[c], h_send.at[c], h_recv.at[c], section - 1, me).wait_recv()
+            slot_copy(c).wait_recv()
             hidden = hin[c].astype(F32)
             nh, _ = normalise(hidden)
             normed = (nh * gain + shift).astype(BF16)
@@ -564,9 +595,15 @@
                 small[3 + j : 4 + j] += jnp.sum(du, axis=0, keepdims=True)
             dn = sum(mm_nt(keep_b[c, :, pl.ds(j * width, width)], weights[j]) for j in range(4))
             leave[c] = norm_back(c, dn, gb).astype(BF16)
-            remote(
-                leave.at[c], gin.at[c], g_send.at[c], g_recv.at[c], section - 1, me
-            ).start()
+
+            @pl.when(section == 3)
+            def _():
+                slot_back(c).start()
+
+            @pl.when(section == 1)
+            def _():
+                for f in range(repeat):
+                    unit_back(c, f).start()
         @pl.loop(0, 2 * chunks)
         def _(step):
             last = lax.div(section, 2)
@@ -960,16 +997,39 @@
 
         send_bias.wait_send()
 
+        @pl.when(section == 0)
+        def _():
+            @pl.loop(0, chunks - 2)
+            def _(k):
+                unit_copy(k).wait_send()
+
+            @pl.loop(chunks * repeat - 2, chunks * repeat)
+            def _(k):
+                unit_copy(k).wait_send()
+
+        @pl.when(section == 2)
+        def _():
+            @pl.loop(0, chunks)
+            def _(c):
+                slot_copy(c).wait_send()
+
     @pl.when(not_attn)
     def _():
         for at in range(2):
             early_copy(4 + at, theirs.at[half_rows(at)])[0].wait_send()
 
-        @pl.loop(0, chunks)
-        def _(c):
-            remote(
-                leave.at[c], gin.at[c], g_send.at[c], g_recv.at[c], section - 1, me
-            ).wait_send()
+        @pl.when(section == 3)
+        def _():
+            @pl.loop(0, chunks)
+            def _(c):
+                slot_back(c).wait_send()
+
+        @pl.when(section == 1)
+        def _():
+            @pl.loop(0, chunks)
+            def _(c):
+                for f in range(repeat):
+                    unit_back(c, f).wait_send()
 
     @pl.when((section == 1) | (section == 2))
     def _():
@@ -1057,8 +1117,7 @@
             pltpu.VMEM((WINDOW, width), BF16),
             pltpu.VMEM((SECTIONS - 1, chunks, WINDOW, quarter), BF16),
             pltpu.VMEM((depth, n, repeat, BLOCK, width), BF16),
-            pltpu.VMEM((slots, n, repeat, BLOCK, width), BF16),
-            pltpu.VMEM((slots, n, repeat, BLOCK, width), BF16),
+            *[pltpu.VMEM((n, repeat, BLOCK, width), BF16) for _ in range(4)],
             pltpu.VMEM((WINDOW // BLOCK, BLOCK, width), BF16),
             pltpu.VMEM((1, wide // 2), F32),
             pltpu.VMEM((1, wide // 2), F32),
@@ -1078,12 +1137,12 @@
             dma((4, pieces)),
             dma((1,)),
             dma((1,)),
+            dma((chunks * repeat,)),
+            dma((chunks,)),
+            dma((chunks, repeat)),
             dma((chunks,)),
             dma((chunks,)),
             dma((chunks,)),
-            dma((chunks,)),
-            dma((chunks,)),
-            dma((micro,)),
             dma((SECTIONS - 1, chunks)),
             dma((1,)),
             dma((SECTIONS, chunks)),
@@ -1114,7 +1173,7 @@
         weight,
         bias,
         down,
-        hidden_bias.reshape(1, -1),
+        hidden_bias,
         ftab,
         ttab,
         kind,
@@ -1122,7 +1181,7 @@
 
 
 def finish_kernel(
-    total_ref,
+    total_hbm,
     small_ref,
     ig_ref,
     out_ref,
@@ -1130,80 +1189,79 @@
     input_grad,
     gain,
     shift,
-    weight,
+    weight_hbm,
     bias,
-    down,
+    down_hbm,
     hidden,
+    short,
+    full,
+    in_sem,
+    out_sem,
 ):
-    block, row = pl.program_id(0), pl.program_id(1)
-
-    @pl.when((block == 0) & (row == 0))
-    def _():
-        output[...] = out_ref[...]
-        input_grad[...] = ig_ref[...].astype(F32)
-        gain[...] = small_ref[0:1]
-        shift[...] = small_ref[1:2]
-        bias[...] = small_ref[2:3]
-        hidden[...] = small_ref[5:7]
-
-    is_down = block >= 4
-
-    @pl.when(jnp.logical_not(is_down))
-    def _():
-        weight[...] = total_ref[0].astype(F32)
-
-    @pl.when(is_down)
-    def _():
-        down[...] = total_ref[0].astype(F32)
-
-
-def finish(total, small, input_grad, output):
+    width = total_hbm.shape[2]
+    steps = short.shape[1]
+    span = width // steps
+    order = [(b, r) for b in range(6) for r in range(steps)]
+
+    def read(b, r):
+        rows = pl.ds(r * span, span)
+        return pltpu.make_async_copy(total_hbm.at[b, rows], short.at[b, r], in_sem.at[b, r])
+
+    def write(b, r):
+        if b < 4:
+            target = weight_hbm.at[pl.ds(r * span, span), pl.ds(b * width, width)]
+        else:
+            target = down_hbm.at[pl.ds((b - 4) * width + r * span, span)]
+        return pltpu.make_async_copy(full.at[b, r], target, out_sem.at[b, r])
+
+    for b, r in order:
+        read(b, r).start()
+    for b, r in order:
+        read(b, r).wait()
+        full[b, r] = short[b, r].astype(F32)
+        write(b, r).start()
+    slots = output.shape[2] // WINDOW
+    for c in range(out_ref.shape[0]):
+        at = pl.ds(c % slots * WINDOW, WINDOW)
+        output[c // slots, :, at] = out_ref[c].T
+        input_grad[c // slots, :, at] = ig_ref[c].astype(F32).T
+    gain[...] = small_ref[0:1]
+    shift[...] = small_ref[1:2]
+    bias[...] = small_ref[2:3]
+    for k in range(2):
+        hidden[pl.ds(k * width, width)] = small_ref[5 + k]
+    for b, r in order:
+        write(b, r).wait()
+
+
+def finish(total, small, input_grad, output, micro):
     width = total.shape[-1]
     steps = 2
-    span = width // steps
-
-    def whole(array):
-        return pl.BlockSpec(array.shape, lambda b, r, k=array.ndim: (0,) * k)
-
-    def weight_at(b, r):
-        return jnp.where(b < 4, r, steps - 1), jnp.minimum(b, 3)
-
-    def down_at(b, r):
-        return jnp.where(b < 4, 0, (b - 4) * steps + r), 0
-
+    turned = (micro, output.shape[2], output.size // micro // output.shape[2])
     row = jax.ShapeDtypeStruct((1, width), F32)
-    pair = jax.ShapeDtypeStruct((2, width), F32)
-    wide_grad = jax.ShapeDtypeStruct(input_grad.shape, F32)
+    vmem = pl.BlockSpec(memory_space=pltpu.VMEM)
+    anywhere = pl.BlockSpec(memory_space=pl.ANY)
     return pl.pallas_call(
         finish_kernel,
-        grid=(6, steps),
         out_shape=(
-            output,
-            wide_grad,
+            jax.ShapeDtypeStruct(turned, BF16),
+            jax.ShapeDtypeStruct(turned, F32),
             row,
             row,
             jax.ShapeDtypeStruct((width, SECTIONS * width), F32),
             row,
             jax.ShapeDtypeStruct((2 * width, width), F32),
-            pair,
+            jax.ShapeDtypeStruct((2 * width,), F32),
         ),
-        in_specs=[
-            pl.BlockSpec((1, span, width), lambda b, r: (b, r, 0)),
-            whole(small),
-            whole(input_grad),
-            whole(output),
+        in_specs=[anywhere, vmem, vmem, vmem],
+        out_specs=(vmem, vmem, vmem, vmem, anywhere, vmem, anywhere, vmem),
+        scratch_shapes=[
+            pltpu.VMEM((6, steps, width // steps, width), BF16),
+            pltpu.VMEM((6, steps, width // steps, width), F32),
+            pltpu.SemaphoreType.DMA((6, steps)),
+            pltpu.SemaphoreType.DMA((6, steps)),
         ],
-        out_specs=(
-            whole(output),
-            whole(wide_grad),
-            whole(row),
-            whole(row),
-            pl.BlockSpec((span, width), weight_at),
-            whole(row),
-            pl.BlockSpec((span, width), down_at),
-            whole(pair),
-        ),
-        compiler_params=pltpu.CompilerParams(vmem_limit_bytes=32 * 1024 * 1024),
+        compiler_params=pltpu.CompilerParams(vmem_limit_bytes=60 * 1024 * 1024),
         name="finish",
     )(total, small, input_grad, output)
 
@@ -1236,18 +1294,17 @@
         clip_kind,
     )
     output, input_grad, gain, shift, weight, bias, down, hidden = finish(
-        total, small_total, input_grad, output
+        total, small_total, input_grad, output, micro
     )
-    quarter = width // SECTIONS
     return (
-        output.reshape(micro, rows, quarter),
-        input_grad.reshape(micro, rows, quarter),
+        output.transpose(0, 2, 1),
+        input_grad.transpose(0, 2, 1),
         gain,
         shift,
         weight[None],
         bias,
         down,
-        hidden.reshape(-1),
+        hidden,
     )
 
 

time: 281 us -> 259 us (0.922)
  Pallas kernels: 270 us -> 258 us
  local copies, waits for them, and re-layouts: 9.85 us -> 0 us
    pallas_call x1, Pallas kernels: 262 us -> 249 us  [pipeline(): pl.pallas_call(functools.partial(main_kernel, cfg), out_shape=(jax.ShapeD...]
    unnamed x10 -> x0, local copies, waits for them, and re-layouts: 7.96 us -> none
where the time goes in v4:
time: 259 us
  Pallas kernels  258 us (100%)
    pallas_call x1, Pallas kernels, pipeline(): pl.pallas_call(functools.partial(main_kernel, cfg), out_shape=(jax.ShapeD...  249 us
    pallas_call x1, Pallas kernels, finish(): pl.pallas_call(finish_kernel, out_shape=(jax.ShapeDtypeStruct(turned, BF1...  9.17 us

profile of v4, /device:TPU:0, one launch (start us, length us, event | category | flops | bytes accessed | tf_op | source)
XLA Modules:
  0.0 258.8 jit_solution(11958044262625627203)
XLA Ops:
  0.6 248.8 %pipeline.1 = (bf16[4,256,192]{2,1,0:T(8,128)(2,1)}, bf16[4,256,192]{2,1,0:T(8,128)(2,1)}, bf16[6,768,768]{2,1,0:T(8,128)(2,1)}, f32[8,768]{1,0:T(8,128)}) custom-call(bf16[4,256,768]{2,1,0:T(8,128)(2,1)} %bitcast.7, bf16[4,256,768]{2,1,0:T(8,128)(2,1)} %bitcast.8, bf16[1,768]{1,0:T(2,128)(2,1)} %gain_ref.1, bf16[1,768]{1,0:T(2,128)(2,1)} %shift_ref.1, ...), custom_call_target="tpu_custom_call" | custom-call | tf_op jit(solution)/shard_map/pipeline/pallas_call | solution.py:1099
  249.4 9.2 %finish.1 = (bf16[2,192,512]{2,1,0:T(8,128)(2,1)}, f32[2,192,512]{2,1,0:T(8,128)}, f32[1,768]{1,0:T(1,128)}, f32[1,768]{1,0:T(1,128)}, f32[768,3072]{1,0:T(8,128...) custom-call(bf16[6,768,768]{2,1,0:T(8,128)(2,1)} %get-tuple-element.20.total_hbm, ...), custom_call_target="tpu_custom_call" | custom-call | tf_op jit(solution)/shard_map/finish/pallas_call | solution.py:1244

commit v5 on v4

--- a/solution.py
+++ b/solution.py
@@ -102,6 +102,8 @@
     load_sem,
     w_send,
     w_recv,
+    r_send,
+    r_recv,
     hb_send,
     hb_recv,
     h_send,
@@ -135,7 +137,7 @@
     spair_send,
     spair_recv,
 ):
-    n, across, repeat, slots, chunks, width, wide, depth, chunk, lag, pieces = cfg
+    n, across, repeat, slots, chunks, width, wide, depth, chunk, lag, pieces, direct = cfg
     section = lax.axis_index("section")
     me = lax.axis_index("dp")
     core = lax.rem(me, 2)
@@ -222,6 +224,21 @@
         source, here = parts(odd_place, core, k)
         return remote(source, here, w_send.at[0, k], w_recv.at[0, k], partner, me)
 
+    def guest_rows(k):
+        return guest.at[pl.ds(pl.multiple_of(k * step_rows, step_rows), step_rows)]
+
+    def down_round_0(k):
+        source, here = parts(odd_place, core, k)
+        return remote(source, here, w_send.at[0, k], r_recv.at[k], 2, me)
+
+    def down_round_2(k):
+        here = parts(odd_place, core, k)[1]
+        return remote(here, guest_rows(k), r_send.at[k], r_recv.at[k], 3, me)
+
+    def down_round_3(k):
+        here = parts(odd_place, core, k)[1]
+        return remote(guest_rows(k), here, r_send.at[k], w_recv.at[0, k], 1, me)
+
     def down_along(k):
         here = parts(odd_place, core, k)[1]
         return remote(here, here, w_send.at[1, k], w_recv.at[1, k], section, across_z)
@@ -270,7 +287,7 @@
             leave.at[slot_of(unit, f), share_rows(lax.rem(unit, repeat))],
             hin.at[unit, share_rows(f)],
             h_send.at[k],
-            h_recv.at[unit],
+            h_recv.at[k],
             1,
             me,
         )
@@ -291,23 +308,49 @@
     def slot_back(c):
         return remote(leave.at[c], gin.at[c], g_send.at[c, 0], g_recv.at[c], 2, me)
 
-    def send_blocks(c, rows, to_section, forward):
+    def wait_depth(c, to_section):
+        @pl.when(c >= depth)
+        def _():
+            some = xsend.at[lax.rem(c, depth)]
+            remote(some, some, x_send.at[c - depth], x_recv.at[0], to_section, me).wait_send()
+
+    def send_share(unit, f, rows):
+        micro, slot = lax.div(unit, slots), lax.rem(unit, depth)
+        blocks[pl.ds(0, across)] = rows.reshape(across, BLOCK, width)
+
+        @pl.when(f == 0)
+        def _():
+            wait_depth(unit, 2)
+
+        @pl.loop(0, n)
+        def _(d):
+            xsend[slot, d, f] = blocks[spots[micro, d]]
+
+        for i in range(chunks):
+
+            @pl.when(unit == i)
+            def _():
+                @pl.loop(0, n)
+                def _(d):
+                    remote(
+                        xsend.at[slot, d, f],
+                        xrecv[i].at[me, f],
+                        x_send.at[i],
+                        x_recv.at[i],
+                        2,
+                        d,
+                    ).start()
+
+    def send_slot(c, rows):
+        micro, slot = lax.div(c, slots), lax.rem(c, depth)
         blocks[...] = rows.reshape(blocks.shape)
-        micro = lax.div(c, slots)
-        slot = lax.rem(c, depth)
-
-        @pl.when(c >= depth)
-        def _():
-            remote(
-                xsend.at[slot], xsend.at[slot], x_send.at[c - depth], x_recv.at[0], to_section, me
-            ).wait_send()
+        wait_depth(c, 1)
 
         @pl.loop(0, n)
         def _(d):
             spot = spots[micro, d]
-            for g in range(repeat):
-                block = g * across + spot if forward else spot * repeat + g
-                xsend[slot, d, g] = blocks[block]
+            for f in range(repeat):
+                xsend[slot, d, f] = blocks[spot * repeat + f]
 
         for i in range(chunks):
 
@@ -318,9 +361,9 @@
                     remote(
                         xsend.at[slot, d],
                         xrecv[i].at[me],
-                        x_send.at[c],
+                        x_send.at[i],
                         x_recv.at[i],
-                        to_section,
+                        1,
                         d,
                     ).start()
 
@@ -371,14 +414,33 @@
 
         meet()
 
-        @pl.loop(0, pieces)
-        def _(k):
-            down_first(k).start()
+        @pl.when(section == 0)
+        def _():
+            @pl.loop(direct, pieces)
+            def _(k):
+                down_round_0(k).start()
+
+            @pl.loop(0, direct)
+            def _(k):
+                down_first(k).start()
 
         send_bias.start()
 
         @pl.when(section == 2)
         def _():
+            @pl.loop(direct, pieces)
+            def _(k):
+                down_round_0(k).wait_recv()
+                down_round_2(k).start()
+
+            @pl.loop(direct, pieces)
+            def _(k):
+                down_round_2(k).wait_send()
+
+            @pl.loop(0, pieces)
+            def _(k):
+                down_first(k).start()
+
             make_tables(ftab, ttab)
 
         def forward(c):
@@ -439,6 +501,12 @@
             @pl.when(section == 2)
             def _():
                 slot_copy(c).start()
+
+            @pl.when((section == 0) & (c == 0))
+            def _():
+                @pl.loop(0, direct)
+                def _(k):
+                    down_first(k).wait_send()
 
             @pl.when(section == 0)
             def _():
@@ -490,7 +558,7 @@
 
             @pl.when(section == 2)
             def _():
-                send_blocks(c, leaving, 1, False)
+                send_slot(c, leaving)
 
             @pl.when(section == 0)
             def _():
@@ -526,60 +594,73 @@
         load_rows(0).wait()
         load_rows(1).wait()
 
+        @pl.when(section == 3)
+        def _():
+            @pl.loop(direct, pieces)
+            def _(k):
+                down_round_2(k).wait_recv()
+                down_round_3(k).start()
+
+            @pl.loop(direct, pieces)
+            def _(k):
+                down_round_3(k).wait_send()
+
         @pl.loop(0, pieces)
         def _(k):
             down_first(k).wait_recv()
             down_along(k).start()
             down_pair(k).start()
 
-        @pl.loop(0, pieces)
-        def _(k):
-            down_along(k).wait_recv()
-            down_last(k).start()
-
         send_bias.wait_recv()
 
         @pl.when(section == 3)
         def _():
             load_c.wait()
 
-        def forward(c):
-            slot_copy(c).wait_recv()
-            hidden = hin[c].astype(F32)
+        def forward(c, at, first):
+            hidden = hin[c, at].astype(F32)
             nh, _ = normalise(hidden)
             normed = (nh * gain + shift).astype(BF16)
-            nrm[c] = normed
+            nrm[c, at] = normed
             for j in range(4):
                 columns = pl.ds(j * width, width)
                 u = mm(normed, weights[j])
                 u = u + (bias_early, bias_late)[j // 2][:, pl.ds((j % 2) * width, width)]
                 active, slope = gelu_and_slope(u)
-                keep_a[c, :, columns] = active.astype(BF16)
-                keep_b[c, :, columns] = slope.astype(BF16)
-
-            @pl.when(c == 0)
-            def _():
+                keep_a[c, at, columns] = active.astype(BF16)
+                keep_b[c, at, columns] = slope.astype(BF16)
+
+            @pl.when(first)
+            def _():
+                @pl.loop(0, pieces)
+                def _(k):
+                    down_along(k).wait_recv()
+                    down_last(k).start()
+
                 @pl.loop(0, pieces)
                 def _(k):
                     down_pair(k).wait_recv()
                     down_last(k).wait_recv()
 
-            branch = mm(keep_a[c], weights[pl.ds(4, 4)].reshape(wide, width))
-            leaving = (hin[c].astype(F32) + branch + bias).astype(BF16)
-
-            @pl.when(section == 1)
-            def _():
-                send_blocks(c, leaving, 2, True)
-
-            @pl.when(section == 3)
-            def _():
-                for s in range(SECTIONS - 1):
-                    gcol[s, c] = leaving[:, s * quarter : (s + 1) * quarter]
-                out_ref[c] = leaving[:, (SECTIONS - 1) * quarter :]
-                for s in range(SECTIONS - 1):
-                    remote(
-                        gcol.at[s, c], out_ref.at[c], o_send.at[s, c], o_recv.at[0], s, me
-                    ).start()
+            branch = mm(keep_a[c, at], weights[pl.ds(4, 4)].reshape(wide, width))
+            return (hin[c, at].astype(F32) + branch + bias).astype(BF16)
+
+        def forward_share(k):
+            unit, f = lax.div(k, repeat), lax.rem(k, repeat)
+            unit_copy(k).wait_recv()
+            leaving = forward(unit, share_rows(f), k == 0)
+            send_share(unit, f, leaving)
+
+        def forward_slot(c):
+            slot_copy(c).wait_recv()
+            leaving = forward(c, pl.ds(0, WINDOW), c == 0)
+            for s in range(SECTIONS - 1):
+                gcol[s, c] = leaving[:, s * quarter : (s + 1) * quarter]
+            out_ref[c] = leaving[:, (SECTIONS - 1) * quarter :]
+            for s in range(SECTIONS - 1):
+                remote(
+                    gcol.at[s, c], out_ref.at[c], o_send.at[s, c], o_recv.at[0], s, me
+                ).start()
 
         def backward(c):
             @pl.when(section == 1)
@@ -602,21 +683,23 @@
 
             @pl.when(section == 1)
             def _():
-                for f in range(repeat):
+                unit_back(c, 0).start()
+
+            @pl.when((section == 1) & (c < chunks - 1))
+            def _():
+                for f in range(1, repeat):
                     unit_back(c, f).start()
-        @pl.loop(0, 2 * chunks)
-        def _(step):
-            last = lax.div(section, 2)
-            c = last * lax.div(step, 2) + (1 - last) * lax.rem(step, chunks)
-            back = last * lax.rem(step, 2) + (1 - last) * lax.div(step, chunks)
-
-            @pl.when(back == 0)
-            def _():
-                forward(c)
-
-            @pl.when(back == 1)
-            def _():
-                backward(c)
+        @pl.when(section == 1)
+        def _():
+            pl.loop(0, chunks * repeat)(forward_share)
+
+        @pl.loop(0, chunks)
+        def _(c):
+            @pl.when(section == 3)
+            def _():
+                forward_slot(c)
+
+            backward(c)
 
     @pl.when(not_attn)
     def _():
@@ -676,11 +759,17 @@
 
         sib_copy(block, grad_rows(block, (1 - core) * side, side)).start()
 
-    def early_copy(block, source):
-        send, recv = early_send.at[block - 4], early_recv.at[block - 4]
+    def early_copy(at, source):
         return (
-            remote(source, grad_rows(block, core * side, side), send, recv, 2, me),
-            remote(source, guest.at[half_rows(block - 4)], send, recv, 3, me),
+            remote(
+                source,
+                grad_rows(4 + at, core * side, side),
+                early_send.at[at],
+                early_recv.at[at],
+                2,
+                me,
+            ),
+            remote(source, guest.at[half_rows(at)], early_send.at[at], early_recv.at[at], 3, me),
         )
 
     def pair_sum(turn):
@@ -691,17 +780,17 @@
         value = here[...].astype(F32) + theirs[half_rows(block)].astype(F32)
         here[...] = value.astype(BF16)
 
-        @pl.when((block == 4) | (block == 5))
-        def _():
-            to_two, to_three = early_copy(block, here)
-
-            @pl.when(section == 3)
-            def _():
-                to_two.start()
-
-            @pl.when(section == 1)
-            def _():
-                to_three.start()
+        @pl.when((section == 3) & ((block == 4) | (block == 5)))
+        def _():
+            early_copy(block - 4, here)[0].start()
+
+        @pl.when((section == 1) & ((block == 4) | (block == 5)))
+        def _():
+            early_copy(block - 4, here)[1].start()
+
+        @pl.when((section == 1) & (block == 7))
+        def _():
+            early_copy(2, here)[1].start()
 
     small_all[me] = small[...]
 
@@ -715,7 +804,8 @@
             small_copy(d).start()
 
     own_lines = w_chunks + d_chunks
-    lines = own_lines + d_chunks * (is_last - is_first)
+    is_second = odd - is_last
+    lines = own_lines + d_chunks * (is_last - is_first) + per_block * (is_last - is_second)
 
     def line_rows(i):
         return pl.ds(pl.multiple_of(i * chunk, chunk), chunk)
@@ -762,9 +852,9 @@
         return pltpu.make_async_copy(source, total_rows(i), local_sem.at[i])
 
     def guest_copy(k, source):
-        return remote(
-            source, total_rows(w_chunks + k), guest_send.at[k], guest_recv.at[k], 0, me
-        )
+        owner = lax.div(k, d_chunks)
+        home = total_rows(w_chunks + k - per_block * owner)
+        return remote(source, home, guest_send.at[k], guest_recv.at[k], owner, me)
 
     def reduce_stage(i, root):
         def run(here):
@@ -854,6 +944,27 @@
                 lambda ref: guest_copy(i - own_lines, ref).start(),
             )
 
+    to_pair = remote(small_out, small_pair, spair_send.at[0], spair_recv.at[0], partner, me)
+
+    def sum_small():
+        remote(
+            small_all.at[pl.ds(0, n - 1)],
+            small_all.at[pl.ds(0, n - 1)],
+            small_send.at[0],
+            small_recv.at[0],
+            section,
+            sibling,
+        ).wait_recv()
+
+        def add(d, so_far):
+            return so_far + small_all[d]
+
+        small_out[...] = lax.fori_loop(1, n, add, small_all[0])
+
+        @pl.when(not_attn)
+        def _():
+            to_pair.start()
+
     height = places // 2
     pairs = lax.div(lines, 2)
     turns = 4 + 4 * odd
@@ -867,6 +978,18 @@
             def _():
                 grad_block(turn)
 
+        if repeat > 1:
+
+            @pl.when((section == 1) & (step == 0))
+            def _():
+                unit_back(chunks - 1, 0).wait_send()
+                for f in range(1, repeat):
+                    unit_back(chunks - 1, f).start()
+
+        @pl.when(step == 6)
+        def _():
+            sum_small()
+
         for at in range(2):
             turn = 2 * step - 3 + at
 
@@ -874,13 +997,15 @@
             def _():
                 pair_sum(turn)
 
-        for at in range(2):
-            half_block = half_rows(at)
-            arrived = early_copy(4 + at, theirs.at[half_block])[0]
-
-            @pl.when((section == 2) & (step == 1 + (4 + at) * per_block // 2))
-            def _():
-                arrived.wait_recv()
+        for at in range(3):
+            arrived = early_copy(min(at, 1), theirs.at[half_rows(at)])[0]
+            if at == 2:
+                arrived = early_copy(at, theirs.at[half_rows(at)])[1]
+            else:
+
+                @pl.when((section == 2) & (step == 1 + (4 + at) * per_block // 2))
+                def _():
+                    arrived.wait_recv()
 
             @pl.when((section == 3) & (step == 1 + (6 + at) * per_block // 2))
             def _():
@@ -902,32 +1027,16 @@
             def _():
                 spread_stage(2 * past + stream, root)
 
-    @pl.when(section == 0)
-    def _():
-        @pl.loop(0, d_chunks)
-        def _(k):
-            here = total_rows(w_chunks + k)
-            guest_copy(k, here).wait_recv()
-            pair_copy(w_chunks + k, here).start()
-
-    remote(
-        small_all.at[pl.ds(0, n - 1)],
-        small_all.at[pl.ds(0, n - 1)],
-        small_send.at[0],
-        small_recv.at[0],
-        section,
-        sibling,
-    ).wait_recv()
-
-    def add(d, so_far):
-        return so_far + small_all[d]
-
-    small_out[...] = lax.fori_loop(1, n, add, small_all[0])
-    to_pair = remote(small_out, small_pair, spair_send.at[0], spair_recv.at[0], partner, me)
+    @pl.when(section < 2)
+    def _():
+        @pl.loop(lines, own_lines)
+        def _(i):
+            here = total_rows(i)
+            guest_copy(i - w_chunks + per_block * odd, here).wait_recv()
+            pair_copy(i, here).start()
 
     @pl.when(not_attn)
     def _():
-        to_pair.start()
         to_pair.wait_send()
 
     @pl.when(is_attn)
@@ -972,9 +1081,9 @@
         def _():
             guest_copy(i - own_lines, some).wait_send()
 
-    @pl.when(section == 0)
-    def _():
-        @pl.loop(w_chunks, own_lines)
+    @pl.when(section < 2)
+    def _():
+        @pl.loop(lines, own_lines)
         def _(i):
             pair_copy(i, low_rows(i)).wait_send()
 
@@ -991,7 +1100,7 @@
 
     @pl.when(is_attn)
     def _():
-        @pl.loop(0, pieces)
+        @pl.loop(direct * is_first, pieces)
         def _(k):
             down_first(k).wait_send()
 
@@ -1016,7 +1125,11 @@
     @pl.when(not_attn)
     def _():
         for at in range(2):
-            early_copy(4 + at, theirs.at[half_rows(at)])[0].wait_send()
+            early_copy(at, theirs.at[half_rows(at)])[0].wait_send()
+
+        @pl.when(section == 1)
+        def _():
+            early_copy(2, theirs.at[half_rows(2)])[1].wait_send()
 
         @pl.when(section == 3)
         def _():
@@ -1026,10 +1139,13 @@
 
         @pl.when(section == 1)
         def _():
-            @pl.loop(0, chunks)
+            @pl.loop(0, chunks - 1)
             def _(c):
                 for f in range(repeat):
                     unit_back(c, f).wait_send()
+
+            for f in range(min(1, repeat - 1), repeat):
+                unit_back(chunks - 1, f).wait_send()
 
     @pl.when((section == 1) | (section == 2))
     def _():
@@ -1086,15 +1202,15 @@
     chunks = micro * slots
     quarter = width // SECTIONS
     depth = chunks if n <= 8 else 1
-    pieces = 4
-    cfg = (n, across, repeat, slots, chunks, width, wide, depth, chunk, lag, pieces)
+    pieces, direct = 8, 6
+    cfg = (n, across, repeat, slots, chunks, width, wide, depth, chunk, lag, pieces, direct)
     vmem = pl.BlockSpec(memory_space=pltpu.VMEM)
     smem = pl.BlockSpec(memory_space=pltpu.SMEM)
     anywhere = pl.BlockSpec(memory_space=pl.ANY)
     dma = pltpu.SemaphoreType.DMA
     chunked = (chunks, WINDOW, width)
     side = width // 2
-    lines = 8 * side // chunk
+    lines = 9 * side // chunk
     per_chunk = [dma((lines,)) for _ in range(8)]
     return pl.pallas_call(
         functools.partial(main_kernel, cfg),
@@ -1124,7 +1240,7 @@
             pltpu.VMEM((2, WINDOW, WINDOW), F32),
             pltpu.SMEM((2, n), jnp.int32),
             pltpu.SMEM((2, across), jnp.int32),
-            pltpu.VMEM((2 * side, width), BF16),
+            pltpu.VMEM((3 * side, width), BF16),
             pltpu.VMEM((8 * side, width), BF16),
             pltpu.VMEM((lines * chunk, width), BF16),
             pltpu.VMEM((lines * chunk, width), BF16),
@@ -1135,10 +1251,12 @@
             dma((8,)),
             dma((4, pieces)),
             dma((4, pieces)),
+            dma((pieces,)),
+            dma((pieces,)),
             dma((1,)),
             dma((1,)),
             dma((chunks * repeat,)),
-            dma((chunks,)),
+            dma((chunks * repeat,)),
             dma((chunks, repeat)),
             dma((chunks,)),
             dma((chunks,)),
@@ -1152,10 +1270,10 @@
             *per_chunk,
             dma((1,)),
             dma((lines,)),
-            dma((2,)),
-            dma((2,)),
-            dma((lines // 4,)),
-            dma((lines // 4,)),
+            dma((3,)),
+            dma((3,)),
+            dma((lines // 3,)),
+            dma((lines // 3,)),
             dma((n,)),
             dma((1,)),
             dma((1,)),

time: 259 us -> 250 us (0.965)
  the two profiles are of different devices: /device:TPU:0 before, /device:TPU:27 now
where the time goes in v5:
time: 250 us; the launch traced here: 249 us
  Pallas kernels  249 us (100%)
    pallas_call x1, Pallas kernels, pipeline(): pl.pallas_call(functools.partial(main_kernel, cfg), out_shape=(jax.ShapeD...  239 us
    pallas_call x1, Pallas kernels, finish(): pl.pallas_call(finish_kernel, out_shape=(jax.ShapeDtypeStruct(turned, BF1...  9.17 us

profile of v5, /device:TPU:27, one launch (start us, length us, event | category | flops | bytes accessed | tf_op | source)
XLA Modules:
  0.0 249.4 jit_solution(12034164510849979374)
XLA Ops:
  0.6 239.4 %pipeline.1 = (bf16[4,256,192]{2,1,0:T(8,128)(2,1)}, bf16[4,256,192]{2,1,0:T(8,128)(2,1)}, bf16[6,768,768]{2,1,0:T(8,128)(2,1)}, f32[8,768]{1,0:T(8,128)}) custom-call(bf16[4,256,768]{2,1,0:T(8,128)(2,1)} %bitcast.7, bf16[4,256,768]{2,1,0:T(8,128)(2,1)} %bitcast.8, bf16[1,768]{1,0:T(2,128)(2,1)} %gain_ref.1, bf16[1,768]{1,0:T(2,128)(2,1)} %shift_ref.1, ...), custom_call_target="tpu_custom_call" | custom-call | tf_op jit(solution)/shard_map/pipeline/pallas_call | solution.py:1215
  240.0 9.2 %finish.1 = (bf16[2,192,512]{2,1,0:T(8,128)(2,1)}, f32[2,192,512]{2,1,0:T(8,128)}, f32[1,768]{1,0:T(1,128)}, f32[1,768]{1,0:T(1,128)}, f32[768,3072]{1,0:T(8,128...) custom-call(bf16[6,768,768]{2,1,0:T(8,128)(2,1)} %get-tuple-element.20.total_hbm, ...), custom_call_target="tpu_custom_call" | custom-call | tf_op jit(solution)/shard_map/finish/pallas_call | solution.py:1362

commit v6 on v5

--- a/solution.py
+++ b/solution.py
@@ -153,8 +153,31 @@
     is_first, is_last = lax.div(3 - section, 3), lax.div(section, 3)
     xrecv = (xrecv0, xrecv1, xrecv2, xrecv3)
     share = WINDOW // repeat
+    few = n <= 8
     half = wide // 2
     quarter = width // SECTIONS
+
+    barrier = pltpu.get_barrier_semaphore()
+
+    def greet(s, d):
+        pl.semaphore_signal(barrier, inc=1, device_id=(s, d), device_id_type=MESH)
+
+    greet(partner, me)
+    greet(3 - partner, me)
+
+    @pl.when((section == 0) | (section == 3))
+    def _():
+        greet(3 - section, me)
+
+    @pl.loop(0, n, unroll=few)
+    def _(d):
+        @pl.when(d != me)
+        def _():
+            greet(section, d)
+
+        @pl.when((section == 1) | (section == 2))
+        def _():
+            greet(3 - section, d)
 
     def load_columns(j):
         columns = pl.ds(j * width, width)
@@ -182,28 +205,6 @@
     def _():
         load_rows(0).start()
         load_rows(1).start()
-
-    barrier = pltpu.get_barrier_semaphore()
-
-    def greet(s, d):
-        pl.semaphore_signal(barrier, inc=1, device_id=(s, d), device_id_type=MESH)
-
-    @pl.loop(0, n)
-    def _(d):
-        @pl.when(d != me)
-        def _():
-            greet(section, d)
-
-        @pl.when((section == 1) | (section == 2))
-        def _():
-            greet(3 - section, d)
-
-    greet(partner, me)
-    greet(3 - partner, me)
-
-    @pl.when((section == 0) | (section == 3))
-    def _():
-        greet(3 - section, me)
 
     def meet():
         edge = is_first + is_last
@@ -322,7 +323,7 @@
         def _():
             wait_depth(unit, 2)
 
-        @pl.loop(0, n)
+        @pl.loop(0, n, unroll=few)
         def _(d):
             xsend[slot, d, f] = blocks[spots[micro, d]]
 
@@ -330,7 +331,7 @@
 
             @pl.when(unit == i)
             def _():
-                @pl.loop(0, n)
+                @pl.loop(0, n, unroll=few)
                 def _(d):
                     remote(
                         xsend.at[slot, d, f],
@@ -346,7 +347,7 @@
         blocks[...] = rows.reshape(blocks.shape)
         wait_depth(c, 1)
 
-        @pl.loop(0, n)
+        @pl.loop(0, n, unroll=few)
         def _(d):
             spot = spots[micro, d]
             for f in range(repeat):
@@ -356,7 +357,7 @@
 
             @pl.when(c == i)
             def _():
-                @pl.loop(0, n)
+                @pl.loop(0, n, unroll=few)
                 def _(d):
                     remote(
                         xsend.at[slot, d],
@@ -374,7 +375,7 @@
             def _():
                 remote(xrecv[i], xrecv[i], x_send.at[0], x_recv.at[i], from_section, me).wait_recv()
 
-                @pl.loop(0, across)
+                @pl.loop(0, across, unroll=few)
                 def _(r):
                     source = sources[i // slots, r]
                     for f in range(repeat):
@@ -657,10 +658,6 @@
             for s in range(SECTIONS - 1):
                 gcol[s, c] = leaving[:, s * quarter : (s + 1) * quarter]
             out_ref[c] = leaving[:, (SECTIONS - 1) * quarter :]
-            for s in range(SECTIONS - 1):
-                remote(
-                    gcol.at[s, c], out_ref.at[c], o_send.at[s, c], o_recv.at[0], s, me
-                ).start()
 
         def backward(c):
             @pl.when(section == 1)
@@ -760,17 +757,18 @@
         sib_copy(block, grad_rows(block, (1 - core) * side, side)).start()
 
     def early_copy(at, source):
-        return (
-            remote(
-                source,
-                grad_rows(4 + at, core * side, side),
-                early_send.at[at],
-                early_recv.at[at],
-                2,
-                me,
-            ),
-            remote(source, guest.at[half_rows(at)], early_send.at[at], early_recv.at[at], 3, me),
+        return remote(
+            source,
+            grad_rows(4 + at, core * side, side),
+            early_send.at[at],
+            early_recv.at[at],
+            2,
+            me,
         )
+
+    def guest_block(at, source):
+        place_of = guest.at[half_rows(at % 2)]
+        return remote(source, place_of, early_send.at[at], early_recv.at[at], 3 - at // 2, me)
 
     def pair_sum(turn):
         block = block_of(turn)
@@ -782,15 +780,13 @@
 
         @pl.when((section == 3) & ((block == 4) | (block == 5)))
         def _():
-            early_copy(block - 4, here)[0].start()
-
-        @pl.when((section == 1) & ((block == 4) | (block == 5)))
-        def _():
-            early_copy(block - 4, here)[1].start()
-
-        @pl.when((section == 1) & (block == 7))
-        def _():
-            early_copy(2, here)[1].start()
+            early_copy(block - 4, here).start()
+
+        for at, which in enumerate((4, 5, 7)):
+
+            @pl.when((section == 1) & (block == which))
+            def _():
+                guest_block(at, here).start()
 
     small_all[me] = small[...]
 
@@ -804,8 +800,14 @@
             small_copy(d).start()
 
     own_lines = w_chunks + d_chunks
-    is_second = odd - is_last
-    lines = own_lines + d_chunks * (is_last - is_first) + per_block * (is_last - is_second)
+    is_second, is_third = odd - is_last, 1 - odd - is_first
+    lines = own_lines + d_chunks * (is_last - is_first) + per_block * (is_third - is_second)
+    guests = d_chunks * is_last + per_block * is_third
+    ahead = own_lines - per_block
+
+    def line_at(turn):
+        late, last = lax.div(turn, ahead), lax.div(turn, ahead + guests)
+        return turn + per_block * late - (per_block + guests) * last
 
     def line_rows(i):
         return pl.ds(pl.multiple_of(i * chunk, chunk), chunk)
@@ -852,8 +854,8 @@
         return pltpu.make_async_copy(source, total_rows(i), local_sem.at[i])
 
     def guest_copy(k, source):
-        owner = lax.div(k, d_chunks)
-        home = total_rows(w_chunks + k - per_block * owner)
+        owner = 1 - is_last
+        home = total_rows(w_chunks + k + per_block * owner)
         return remote(source, home, guest_send.at[k], guest_recv.at[k], owner, me)
 
     def reduce_stage(i, root):
@@ -990,6 +992,15 @@
         def _():
             sum_small()
 
+        @pl.when((section == 3) & (step == 8))
+        def _():
+            @pl.loop(0, chunks)
+            def _(c):
+                for s in range(SECTIONS - 1):
+                    remote(
+                        gcol.at[s, c], out_ref.at[c], o_send.at[s, c], o_recv.at[0], s, me
+                    ).start()
+
         for at in range(2):
             turn = 2 * step - 3 + at
 
@@ -997,19 +1008,19 @@
             def _():
                 pair_sum(turn)
 
-        for at in range(3):
-            arrived = early_copy(min(at, 1), theirs.at[half_rows(at)])[0]
-            if at == 2:
-                arrived = early_copy(at, theirs.at[half_rows(at)])[1]
-            else:
-
-                @pl.when((section == 2) & (step == 1 + (4 + at) * per_block // 2))
-                def _():
-                    arrived.wait_recv()
-
-            @pl.when((section == 3) & (step == 1 + (6 + at) * per_block // 2))
-            def _():
-                arrived.wait_recv()
+        for at in range(2):
+
+            @pl.when((section == 2) & (step == 1 + (4 + 2 * at) * per_block // 2))
+            def _():
+                early_copy(at, theirs.at[half_rows(at)]).wait_recv()
+
+            @pl.when((section == 3) & (step == 1 + (5 + at) * per_block // 2))
+            def _():
+                guest_block(at, theirs.at[half_rows(at)]).wait_recv()
+
+        @pl.when((section == 2) & (step == 1 + 5 * per_block // 2))
+        def _():
+            guest_block(2, theirs.at[half_rows(0)]).wait_recv()
 
         for stream in range(2):
             root = height - 1 + stream
@@ -1017,7 +1028,7 @@
 
             @pl.when((now >= 0) & (now < pairs))
             def _():
-                reduce_stage(2 * now + stream, root)
+                reduce_stage(line_at(2 * now + stream), root)
 
         for stream in range(2):
             root = height - 1 + stream
@@ -1025,14 +1036,15 @@
 
             @pl.when((past >= 0) & (past < pairs))
             def _():
-                spread_stage(2 * past + stream, root)
+                spread_stage(line_at(2 * past + stream), root)
 
     @pl.when(section < 2)
     def _():
         @pl.loop(lines, own_lines)
         def _(i):
             here = total_rows(i)
-            guest_copy(i - w_chunks + per_block * odd, here).wait_recv()
+            k = i - lines
+            remote(here, here, guest_send.at[k], guest_recv.at[k], 3 - section, me).wait_recv()
             pair_copy(i, here).start()
 
     @pl.when(not_attn)
@@ -1125,11 +1137,11 @@
     @pl.when(not_attn)
     def _():
         for at in range(2):
-            early_copy(at, theirs.at[half_rows(at)])[0].wait_send()
+            early_copy(at, theirs.at[half_rows(at)]).wait_send()
 
         @pl.when(section == 1)
         def _():
-            early_copy(2, theirs.at[half_rows(2)])[1].wait_send()
+            guest_block(2, theirs.at[half_rows(0)]).wait_send()
 
         @pl.when(section == 3)
         def _():
@@ -1202,7 +1214,7 @@
     chunks = micro * slots
     quarter = width // SECTIONS
     depth = chunks if n <= 8 else 1
-    pieces, direct = 8, 6
+    pieces, direct = 4, 3
     cfg = (n, across, repeat, slots, chunks, width, wide, depth, chunk, lag, pieces, direct)
     vmem = pl.BlockSpec(memory_space=pltpu.VMEM)
     smem = pl.BlockSpec(memory_space=pltpu.SMEM)
@@ -1210,7 +1222,7 @@
     dma = pltpu.SemaphoreType.DMA
     chunked = (chunks, WINDOW, width)
     side = width // 2
-    lines = 9 * side // chunk
+    lines = 8 * side // chunk
     per_chunk = [dma((lines,)) for _ in range(8)]
     return pl.pallas_call(
         functools.partial(main_kernel, cfg),
@@ -1240,7 +1252,7 @@
             pltpu.VMEM((2, WINDOW, WINDOW), F32),
             pltpu.SMEM((2, n), jnp.int32),
             pltpu.SMEM((2, across), jnp.int32),
-            pltpu.VMEM((3 * side, width), BF16),
+            pltpu.VMEM((2 * side, width), BF16),
             pltpu.VMEM((8 * side, width), BF16),
             pltpu.VMEM((lines * chunk, width), BF16),
             pltpu.VMEM((lines * chunk, width), BF16),
@@ -1272,8 +1284,8 @@
             dma((lines,)),
             dma((3,)),
             dma((3,)),
-            dma((lines // 3,)),
-            dma((lines // 3,)),
+            dma((lines // 4,)),
+            dma((lines // 4,)),
             dma((n,)),
             dma((1,)),
             dma((1,)),

time: 250 us -> 234 us (0.936)
  the two profiles are of different devices: /device:TPU:27 before, /device:TPU:29 now
where the time goes in v6:
time: 234 us
  Pallas kernels  233 us (100%)
    pallas_call x1, Pallas kernels, pipeline(): pl.pallas_call(functools.partial(main_kernel, cfg), out_shape=(jax.ShapeD...  224 us
    pallas_call x1, Pallas kernels, finish(): pl.pallas_call(finish_kernel, out_shape=(jax.ShapeDtypeStruct(turned, BF1...  9.17 us

profile of v6, /device:TPU:29, one launch (start us, length us, event | category | flops | bytes accessed | tf_op | source)
XLA Modules:
  0.0 233.9 jit_solution(6028389107729418992)
XLA Ops:
  0.6 223.9 %pipeline.1 = (bf16[4,256,192]{2,1,0:T(8,128)(2,1)}, bf16[4,256,192]{2,1,0:T(8,128)(2,1)}, bf16[6,768,768]{2,1,0:T(8,128)(2,1)}, f32[8,768]{1,0:T(8,128)}) custom-call(bf16[4,256,768]{2,1,0:T(8,128)(2,1)} %bitcast.7, bf16[4,256,768]{2,1,0:T(8,128)(2,1)} %bitcast.8, bf16[1,768]{1,0:T(2,128)(2,1)} %gain_ref.1, bf16[1,768]{1,0:T(2,128)(2,1)} %shift_ref.1, ...), custom_call_target="tpu_custom_call" | custom-call | tf_op jit(solution)/shard_map/pipeline/pallas_call | solution.py:1227
  224.6 9.2 %finish.1 = (bf16[2,192,512]{2,1,0:T(8,128)(2,1)}, f32[2,192,512]{2,1,0:T(8,128)}, f32[1,768]{1,0:T(1,128)}, f32[1,768]{1,0:T(1,128)}, f32[768,3072]{1,0:T(8,128...) custom-call(bf16[6,768,768]{2,1,0:T(8,128)(2,1)} %get-tuple-element.20.total_hbm, ...), custom_call_target="tpu_custom_call" | custom-call | tf_op jit(solution)/shard_map/finish/pallas_call | solution.py:1374
